TPU v7x, 512 devices: a whole 4x8x8 slice. The times are simulated.
512 devices in a mesh: group: 8 (over x, core), member: 64 (over y, z).
Axes of the slice: x: 4, y: 8, z: 8, core: 2. Of those that a mesh axis runs over, the one named last changes fastest.
Arguments:
- features: bfloat16 [131072, 256], P(('group', 'member')), may hold values from -6 to 6
- neighbours: int32 [131072, 10], P(('group', 'member')), may hold values from 0 to 3327
- send_rows: int32 [32768, 16], P(('group', 'member')), may hold values from 0 to 255
- block_counts: int32 [32768], P(('group', 'member')), may hold values from 1 to 16, as said below
- hub_rows: int32 [512, 4], P(('group', 'member')), may hold values from 0 to 255
- w_self: bfloat16 [256, 256], replicated, may hold values from -0.375 to 0.375
- w_nbr: bfloat16 [256, 256], replicated, may hold values from -0.375 to 0.375
- cotangent: bfloat16 [131072, 256], P(('group', 'member')), may hold values from -6 to 6
Outputs:
- grad_self: float32 [256, 256], replicated
- grad_nbr: float32 [256, 256], replicated
- grad_features: bfloat16 [131072, 256], P(('group', 'member'))
Inputs may be any that keep to these rules, and one draw needn't show every extreme that they name: `block_counts`: entry pair of every fourth pair (pair % 4 == 0) is exactly 16.
All inputs are finite; a program needn't handle non-finite values.
Results may differ from a plain program's by a relative error of at most 0.005.
Values may be sent and summed in bfloat16 or wider, within the bound.
No kernel may reach another device: no remote copies, remote signals or barrier semaphores. Data moves between devices by JAX's collectives and lax.ppermute only.
A program may use at most 64 MiB of HBM per device.

v0:
```python
import math

import jax
import jax.numpy as jnp
from jax import lax
from jax.sharding import PartitionSpec as P


def local(features, neighbours, send_rows, block_counts, hub_rows, w_self, w_nbr, cotangent):
    node_count, width = features.shape
    member_count = lax.axis_size("member")
    group_count = lax.axis_size("group")
    block_size = send_rows.shape[1]
    fan_count = neighbours.shape[1]
    keep_slot = jnp.arange(block_size, dtype=jnp.int32)[None, :] < block_counts[:, None]
    outgoing = jnp.where(keep_slot[:, :, None], features[send_rows], jnp.zeros((), jnp.bfloat16))
    incoming = lax.all_to_all(outgoing, "member", split_axis=0, concat_axis=0, tiled=True)
    owned_hubs = features[hub_rows.reshape(-1)]
    hub_table = lax.all_gather(owned_hubs, ("group", "member"), axis=0, tiled=True)
    table = jnp.concatenate([features, incoming.reshape(-1, width), hub_table], axis=0)
    agg_sum = jnp.zeros((node_count, width), jnp.float32)
    for sample in range(fan_count):
        agg_sum = agg_sum + table[neighbours[:, sample]].astype(jnp.float32)
    agg = (agg_sum / fan_count).astype(jnp.bfloat16)
    pre = jnp.dot(features, w_self, preferred_element_type=jnp.float32) + jnp.dot(
        agg, w_nbr, preferred_element_type=jnp.float32
    )
    sigma = jax.nn.sigmoid(pre)
    dpre = (cotangent.astype(jnp.float32) * sigma * (1.0 + pre * (1.0 - sigma))).astype(
        jnp.bfloat16
    )
    contract = (((0,), (0,)), ((), ()))
    part_self = lax.dot_general(features, dpre, contract, preferred_element_type=jnp.float32)
    part_nbr = lax.dot_general(agg, dpre, contract, preferred_element_type=jnp.float32)
    own_grad = jnp.dot(dpre, w_self.T, preferred_element_type=jnp.float32)
    dagg = jnp.dot(dpre, w_nbr.T, preferred_element_type=jnp.float32) / fan_count
    spread = jnp.zeros((table.shape[0], width), jnp.float32)
    for sample in range(fan_count):
        spread = spread.at[neighbours[:, sample]].add(dagg)
    border_stop = node_count + member_count * block_size
    border_grad = spread[node_count:border_stop].reshape(member_count, block_size, width)
    returned = lax.all_to_all(
        border_grad.astype(jnp.bfloat16), "member", split_axis=0, concat_axis=0, tiled=True
    ).astype(border_grad.dtype)
    returned = jnp.where(keep_slot[:, :, None], returned, 0.0)
    hub_grad = spread[border_stop:]
    hub_mine = lax.psum_scatter(hub_grad, ("group", "member"), scatter_dimension=0, tiled=True)
    total_grad = own_grad + spread[:node_count]
    total_grad = total_grad.at[send_rows.reshape(-1)].add(returned.reshape(-1, width))
    total_grad = total_grad.at[hub_rows.reshape(-1)].add(hub_mine)
    summed_self, summed_nbr = lax.psum((part_self, part_nbr), ("group", "member"))
    scale = 1.0 / math.sqrt(node_count * group_count * member_count)
    return (summed_self * scale, summed_nbr * scale, total_grad.astype(jnp.bfloat16))


def solution(mesh):
    in_specs = (
        P(("group", "member"), None),
        P(("group", "member"), None),
        P(("group", "member"), None),
        P(("group", "member")),
        P(("group", "member"), None),
        P(),
        P(),
        P(("group", "member"), None),
    )
    out_specs = (P(), P(), P(("group", "member"), None))
    return jax.shard_map(local, mesh=mesh, in_specs=in_specs, out_specs=out_specs, check_vma=False)
```

profile of v0, /device:TPU:16, one launch (start us, length us, event | category | flops | bytes accessed | tf_op | source)
XLA Modules:
  0.0 485.8 jit_solution(18188416479168719938)
XLA Ops:
  7.2 0.7 fusion.4
  7.9 2.1 gather_fusion.1
  10.0 0.7 compare_select_fusion.1
  10.7 0.1 copy.19
  10.8 0.1 reshape.104
  10.9 4.4 gather_fusion
  15.4 0.1 iota_compare_fusion
  15.4 1.0 broadcast_select_fusion
  16.5 16.5 %all-to-all-start = ((bf16[64,16,256]{2,1,0:T(8,128)(2,1)}), bf16[64,16,256]{2,1,0:T(8,128)(2,1)S(1)}, u32[]{:S(2)}, u32[]{:S(2)}) async-start(bf16[64,16,256]{2,1,0:T(8,128)(2,1)} %broadcast_select_fusion), calls=%async_computation | async-start | bytes 1048576 | tf_op jit(solution)/shard_map/all_to_all | solution.py:17
  33.1 0.6 pad_clamp_fusion.1
  33.7 0.6 pad_clamp_fusion
  34.3 0.6 pad_clamp_fusion.9
  34.9 0.6 pad_clamp_fusion.8
  35.5 0.6 pad_clamp_fusion.7
  36.1 0.6 pad_clamp_fusion.6
  36.7 0.6 pad_clamp_fusion.5
  37.3 0.6 pad_clamp_fusion.4
  37.9 0.6 pad_clamp_fusion.3
  38.5 0.6 pad_clamp_fusion.2
  39.1 0.9 fusion.5
  40.0 88.5 %all-gather.4.cloned.1.call-done = bf16[512,4,256]{2,1,0:T(4,128)(2,1)} async-done(((bf16[1,4,256]{2,1,0:T(4,128)(2,1)}), bf16[512,4,256]{2,1,0:T(4,128)(2,1)}) %all-gather.4.cloned.1.call-update) | async-done | bytes 1048592 | tf_op jit(solution)/shard_map/all_gather | solution.py:19
  128.5 1.3 reshape.298
  129.9 0.1 pad_maximum_fusion
  130.0 1.3 gather_fusion.10
  131.3 1.3 gather_fusion.11
  132.6 1.3 gather_fusion.2
  133.9 1.3 gather_fusion.3
  135.2 1.3 gather_fusion.4
  136.5 1.4 gather_fusion.5
  137.9 1.3 gather_fusion.6
  139.2 1.3 gather_fusion.7
  140.5 1.3 gather_fusion.8
  141.8 1.3 gather_fusion.9
  143.0 0.2 multiply_convert_fusion.1
  143.2 1.2 multiply_convert_fusion
  144.4 0.9 convolution_multiply_fusion
  145.4 0.9 fusion.6
  146.3 0.9 convolution_bitcast_fusion
  147.2 3.2 scatter_custom_fusion
  150.4 3.8 scatter_fusion
  154.2 3.6 scatter_fusion.1
  157.8 3.6 scatter_fusion.2
  161.4 3.6 scatter_fusion.3
  165.1 3.6 scatter_fusion.4
  168.7 3.6 scatter_fusion.5
  172.3 3.6 scatter_fusion.6
  175.9 3.6 scatter_fusion.7
  179.5 3.6 scatter_fusion.8
  183.1 1.6 slice.89
  184.8 0.7 copy-done.1
  185.5 0.8 slice.102
  186.3 10.8 %all-to-all-start.1 = ((bf16[64,16,256]{2,1,0:T(8,128)(2,1)}), bf16[64,16,256]{2,1,0:T(8,128)(2,1)S(1)}, u32[]{:S(2)}, u32[]{:S(2)}) async-start(bf16[64,16,256]{2,1,0:T(8,128)(2,1)} %bitcast.36), calls=%async_computation.1 | async-start | bytes 1048576 | tf_op jit(solution)/shard_map/all_to_all | solution.py:42
  197.2 0.1 copy.21
  197.3 0.1 reshape.100
  197.4 1.3 convolution_add_fusion
  198.7 19.3 %all-to-all-done.1 = bf16[64,16,256]{2,1,0:T(8,128)(2,1)S(1)} async-done(((bf16[64,16,256]{2,1,0:T(8,128)(2,1)}), bf16[64,16,256]{2,1,0:T(8,128)(2,1)S(1)}, u32[]{:S(2)}, u32[]{:S(2)}) %all-to-all-start.1) | async-done | bytes 524320 | tf_op jit(solution)/shard_map/all_to_all | solution.py:42
  217.9 0.2 convert_select_fusion
  218.2 6.2 %scatter_fusion.9 = f32[256,256]{1,0:T(8,128)S(1)} fusion(f32[256,256]{1,0:T(8,128)S(1)} %convolution_add_fusion, s32[1024]{0:T(1024)S(1)} %bitcast.38, f32[1024,256]{1,0:T(8,128)S(1)} %bitcast.34), kind=kCustom, calls=%fused_computation.22 | custom fusion | flops 262144 | bytes 3149824 | tf_op jit(solution)/shard_map/scatter-add | solution.py:49
  224.3 250.3 %all-reduce.4.cloned.1.call-done = (f32[256,256]{0,1:T(8,128)}, f32[256,256]{0,1:T(8,128)}, f32[2048,256]{1,0:T(8,128)}) async-done(((f32[256,256]{0,1:T(8,128)}, f32[256,256]{0,1:T(8,128)}, f32[2048,256]{1,0:T(8,128)}), (f32[256,256]{0,1:T(8,128)}, f32[256,256]{0,1:T(8,128)}, f32[2048,256]{1,0:T(8,128)})) %all-reduce.4.cloned.1.call-update) | async-done | bytes 2621456 | tf_op jit(solution)/shard_map/psum | solution.py:51
  474.6 0.9 scatter_custom_fusion.11
  475.5 0.7 convert_element_type.64
  476.2 1.1 broadcast_multiply_fusion
  477.3 0.8 copy.22
  478.1 0.8 copy.23
  (44 shorter events, 0.2 us)
Async XLA Ops:
  7.2 136.1 %copy-start = (bf16[256,256]{1,0:T(8,128)(2,1)S(1)}, bf16[256,256]{1,0:T(8,128)(2,1)}, u32[]{:S(2)}) copy-start(bf16[256,256]{1,0:T(8,128)(2,1)} %param.14) | copy-start | bytes 393220
  7.2 8.2 %copy-start.16 = (s32[64]{0:T(128)S(1)}, s32[64]{0:T(128)}, u32[]{:S(2)}) copy-start(s32[64]{0:T(128)} %param.11) | copy-start | bytes 772
  7.2 121.3 %all-gather.4.cloned.1.call-start = ((), (), s32[]{:S(2)}) async-start(), calls=%async_computation.2 | async-start | bytes 1050624 | tf_op jit(solution)/shard_map/all_gather | solution.py:19
  7.9 2.1 copy-start.17
  10.9 22.1 %copy-start.14 = (s32[256,10]{0,1:T(8,128)S(1)}, s32[256,10]{0,1:T(8,128)}, u32[]{:S(2)}) copy-start(s32[256,10]{0,1:T(8,128)} %param.9) | copy-start | bytes 30724
  10.9 28.2 %copy-start.2 = (bf16[256,256]{1,0:T(8,128)(2,1)S(1)}, bf16[256,256]{1,0:T(8,128)(2,1)}, u32[]{:S(2)}) copy-start(bf16[256,256]{1,0:T(8,128)(2,1)} %param.8) | copy-start | bytes 393220
  10.9 28.2 %copy-start.4 = (bf16[256,256]{1,0:T(8,128)(2,1)S(1)}, bf16[256,256]{1,0:T(8,128)(2,1)}, u32[]{:S(2)}) copy-start(bf16[256,256]{1,0:T(8,128)(2,1)} %param.13) | copy-start | bytes 393220
  16.5 113.3 %all-to-all-start = ((bf16[64,16,256]{2,1,0:T(8,128)(2,1)}), bf16[64,16,256]{2,1,0:T(8,128)(2,1)S(1)}, u32[]{:S(2)}, u32[]{:S(2)}) async-start(bf16[64,16,256]{2,1,0:T(8,128)(2,1)} %broadcast_select_fusion), calls=%async_computation | async-start | bytes 1048576 | tf_op jit(solution)/shard_map/all_to_all | solution.py:17
  32.9 441.7 %all-reduce.4.cloned.1.call-start = ((), (), s32[]{:S(2)}) async-start(), calls=%async_computation.3 | async-start | bytes 5242880 | tf_op jit(solution)/shard_map/psum | solution.py:51
  33.0 96.8 %copy-start.7 = (s32[256,1]{0,1:T(1,128)}, s32[256,1]{0,1:T(1,128)S(1)}, u32[]{:S(2)}) copy-start(s32[256,1]{0,1:T(1,128)S(1)} %get-tuple-element.16) | copy-start | bytes 3076
  33.0 96.8 %copy-start.8 = (s32[256,1]{0,1:T(1,128)}, s32[256,1]{0,1:T(1,128)S(1)}, u32[]{:S(2)}) copy-start(s32[256,1]{0,1:T(1,128)S(1)} %get-tuple-element.17) | copy-start | bytes 3076
  33.1 96.8 %copy-start.9 = (s32[256,1]{0,1:T(1,128)}, s32[256,1]{0,1:T(1,128)S(1)}, u32[]{:S(2)}) copy-start(s32[256,1]{0,1:T(1,128)S(1)} %get-tuple-element.18) | copy-start | bytes 3076
  33.1 96.8 %copy-start.10 = (s32[256,1]{0,1:T(1,128)}, s32[256,1]{0,1:T(1,128)S(1)}, u32[]{:S(2)}) copy-start(s32[256,1]{0,1:T(1,128)S(1)} %get-tuple-element.19) | copy-start | bytes 3076
  33.1 96.8 %copy-start.11 = (s32[256,1]{0,1:T(1,128)}, s32[256,1]{0,1:T(1,128)S(1)}, u32[]{:S(2)}) copy-start(s32[256,1]{0,1:T(1,128)S(1)} %get-tuple-element.20) | copy-start | bytes 3076
  33.1 96.8 %copy-start.12 = (s32[256,1]{0,1:T(1,128)}, s32[256,1]{0,1:T(1,128)S(1)}, u32[]{:S(2)}) copy-start(s32[256,1]{0,1:T(1,128)S(1)} %get-tuple-element.21) | copy-start | bytes 3076
  33.1 96.8 %copy-start.13 = (s32[256,1]{0,1:T(1,128)}, s32[256,1]{0,1:T(1,128)S(1)}, u32[]{:S(2)}) copy-start(s32[256,1]{0,1:T(1,128)S(1)} %get-tuple-element.22) | copy-start | bytes 3076
  33.1 96.8 %copy-start.15 = (s32[256,1]{0,1:T(1,128)}, s32[256,1]{0,1:T(1,128)S(1)}, u32[]{:S(2)}) copy-start(s32[256,1]{0,1:T(1,128)S(1)} %get-tuple-element.15) | copy-start | bytes 3076
  136.5 6.8 %copy-start.5 = (f32[256,256]{1,0:T(8,128)S(1)}, f32[256,256]{1,0:T(8,128)}, u32[]{:S(2)}) copy-start(f32[256,256]{1,0:T(8,128)} %fusion.5) | copy-start | bytes 786436
  144.4 1.9 copy-start.3
  183.1 2.3 copy-start.1
  184.7 12.4 %copy-start.6 = (s32[64,16]{0,1:T(8,128)S(1)}, s32[64,16]{0,1:T(8,128)}, u32[]{:S(2)}) copy-start(s32[64,16]{0,1:T(8,128)} %param.10) | copy-start | bytes 12292
  186.3 31.6 %all-to-all-start.1 = ((bf16[64,16,256]{2,1,0:T(8,128)(2,1)}), bf16[64,16,256]{2,1,0:T(8,128)(2,1)S(1)}, u32[]{:S(2)}, u32[]{:S(2)}) async-start(bf16[64,16,256]{2,1,0:T(8,128)(2,1)} %bitcast.36), calls=%async_computation.1 | async-start | bytes 1048576 | tf_op jit(solution)/shard_map/all_to_all | solution.py:42
Sparse Core Ops, SparseCore 0:
  12.2 116.1 all-gather.3
  184.9 289.6 all-reduce.3
where the time goes:
time: 489 us; the launch traced here: 486 us
  waiting for transfers between devices  358 us (73%)
  other arithmetic  53.6 us (11%)
  starting transfers between devices  27.4 us (6%)
  local copies, waits for them, and re-layouts  26.1 us (5%)
  between operations  14.5 us (3%)
  matrix products  6.16 us (1%)
    psum x1, waiting for transfers between devices, local(): lax.psum((part_self, part_nbr), ('group', 'member'))  250 us
    all_gather x1, waiting for transfers between devices, local(): lax.all_gather(owned_hubs, ('group', 'member'), axis=0, tiled=True)  88.5 us
    scatter-add x10, other arithmetic, local(): spread = spread.at[neighbours[:, sample]].add(dagg)  35.8 us
    all_to_all x1, waiting for transfers between devices, local(): lax.all_to_all(border_grad.astype(jnp.bfloat16), 'member', split_axis=0,...  19.3 us
    all_to_all x1, starting transfers between devices, local(): lax.all_to_all(outgoing, 'member', split_axis=0, concat_axis=0, tiled=True)  16.5 us
    gather x10, local copies, waits for them, and re-layouts, local(): agg_sum = agg_sum + table[neighbours[:, sample]].astype(jnp.float32)  13 us
    all_to_all x1, starting transfers between devices, local(): lax.all_to_all(border_grad.astype(jnp.bfloat16), 'member', split_axis=0,...  10.8 us
  transfers between devices with their start and end apart: 4, of which 3 were waited for; matrix products, arithmetic and copies ran while one was open for 5% of the time, Pallas kernels for 0%

commit v1 on v0

v1 whole, which is shorter than its diff:
```python
import math

import jax
import jax.numpy as jnp
from jax import lax
from jax.sharding import Mesh, PartitionSpec as P

BF = jnp.bfloat16
F32 = jnp.float32
GROUP = ("x", "core")
MEMBER = ("y", "z")
ALL = ("x", "core", "y", "z")


def swap_blocks(array, axes):
    return lax.all_to_all(array, axes, split_axis=0, concat_axis=0, tiled=True)


def local(features, neighbours, send_rows, block_counts, hub_rows, w_self, w_nbr, cotangent):
    nodes, width = features.shape
    members, slots = send_rows.shape
    fan = neighbours.shape[1]
    hubs = hub_rows.shape[1]
    groups = lax.axis_size(GROUP)
    xs = lax.axis_size("x")
    wide = 24
    scale = 1.0 / math.sqrt(nodes * groups * members)

    keep = jnp.arange(slots, dtype=jnp.int32)[None, :] < block_counts[:, None]
    sent = jnp.where(keep, send_rows, -1)
    row_ids = jnp.concatenate(
        [
            sent,
            jnp.broadcast_to(hub_rows, (members, hubs)),
            jnp.full((members, wide - slots - hubs), -1, jnp.int32),
        ],
        axis=1,
    ).reshape(members * wide, 1)
    node_iota = jnp.arange(nodes, dtype=jnp.int32)
    pick = (row_ids == node_iota[None, :]).astype(BF)
    outgoing = jnp.dot(pick, features, preferred_element_type=F32).astype(BF)
    incoming = swap_blocks(outgoing, MEMBER)
    my_hubs = incoming.reshape(members, wide, width)[:, slots : slots + hubs].reshape(members * hubs, width)
    hub_table = lax.all_gather(my_hubs, GROUP, axis=0, tiled=True)

    border = neighbours - nodes
    border_stop = members * slots
    column = jnp.where(
        border < 0,
        neighbours,
        jnp.where(
            border < border_stop,
            nodes + (border // slots) * wide + border % slots,
            border - border_stop + nodes + members * wide,
        ),
    )
    total = nodes + members * wide + groups * members * hubs
    ids = jnp.arange(total, dtype=jnp.int32)
    counts = jnp.zeros((nodes, total), BF)
    for f in range(fan):
        counts = counts + (column[:, f : f + 1] == ids[None, :]).astype(BF)
    first, second = nodes, nodes + members * wide
    agg_sum = (
        jnp.dot(counts[:, :first], features, preferred_element_type=F32)
        + jnp.dot(counts[:, first:second], incoming, preferred_element_type=F32)
        + jnp.dot(counts[:, second:], hub_table, preferred_element_type=F32)
    )
    agg = (agg_sum / fan).astype(BF)
    pre = jnp.dot(features, w_self, preferred_element_type=F32) + jnp.dot(agg, w_nbr, preferred_element_type=F32)
    sigma = jax.nn.sigmoid(pre)
    dpre = (cotangent.astype(F32) * sigma * (1.0 + pre * (1.0 - sigma))).astype(BF)

    over_rows = (((0,), (0,)), ((), ()))
    own_grad = jnp.dot(dpre, w_self.T, preferred_element_type=F32)
    dagg = (jnp.dot(dpre, w_nbr.T, preferred_element_type=F32) / fan).astype(BF)
    spread = lax.dot_general(counts, dagg, over_rows, preferred_element_type=F32)
    part = lax.dot_general(jnp.concatenate([features, agg], axis=1), dpre, over_rows, preferred_element_type=F32)

    border_grad = spread[first:second].astype(BF).reshape(members, wide, width)
    weight_rows = 2 * width // members
    outward = jnp.concatenate(
        [border_grad[:, :slots], part.astype(BF).reshape(members, weight_rows, width)], axis=1
    ).reshape(members * wide, width)
    returned = swap_blocks(outward, MEMBER).reshape(members, wide, width)
    weight_sum = jnp.sum(returned[:, slots:].astype(F32), axis=0).astype(BF)
    weight_all = swap_blocks(jnp.broadcast_to(weight_sum, (groups, weight_rows, width)).reshape(-1, width), GROUP)
    weight_done = jnp.sum(weight_all.reshape(groups, weight_rows, width).astype(F32), axis=0)

    hub_grad = spread[second:].astype(BF).reshape(xs, 2, members * hubs, width)
    core = lax.axis_index("core")
    mine = lax.dynamic_index_in_dim(hub_grad, core, 1, keepdims=False)
    other = lax.dynamic_index_in_dim(hub_grad, 1 - core, 1, keepdims=False)
    met = lax.ppermute(other, "core", [(0, 1), (1, 0)])
    paired = (mine.astype(F32) + met.astype(F32)).astype(BF)
    along = swap_blocks(paired.reshape(xs * members * hubs, width), "x")
    hub_part = jnp.sum(along.reshape(xs, members, hubs, width).astype(F32), axis=0).astype(BF)
    last = 16
    final = jnp.concatenate(
        [
            jnp.broadcast_to((weight_done * scale).astype(BF), (members, weight_rows, width)),
            hub_part,
            jnp.zeros((members, last - weight_rows - hubs, width), BF),
        ],
        axis=1,
    ).reshape(members * last, width)
    final = swap_blocks(final, MEMBER).reshape(members, last, width)
    weights = final[:, :weight_rows].reshape(2 * width, width).astype(F32)
    hub_mine = jnp.sum(final[:, weight_rows : weight_rows + hubs].astype(F32), axis=0)

    back = jnp.concatenate([returned[:, :slots].reshape(members * slots, width), hub_mine.astype(BF)], axis=0)
    home = jnp.concatenate([sent.reshape(1, -1), hub_rows], axis=1)
    place = (node_iota[:, None] == home).astype(BF)
    grad = own_grad + spread[:first] + jnp.dot(place, back, preferred_element_type=F32)
    return weights[:width], weights[width:], grad.astype(BF)


def solution(mesh):
    split = Mesh(mesh.devices.reshape(4, 2, 8, 8), ALL)
    rows = P(ALL, None)
    in_specs = (rows, rows, rows, P(ALL), rows, P(), P(), rows)
    out_specs = (P(), P(), rows)
    return jax.shard_map(local, mesh=split, in_specs=in_specs, out_specs=out_specs, check_vma=False)
```

time: 489 us -> 185 us (0.38)
  waiting for transfers between devices: 358 us -> 89.3 us
  other arithmetic: 53.6 us -> 10.8 us
  local copies, waits for them, and re-layouts: 26.1 us -> 6.07 us
  starting transfers between devices: 27.4 us -> 45.4 us
  matrix products: 6.16 us -> 18.1 us
    psum x1 -> x0, waiting for transfers between devices: 250 us -> none  [local(): lax.psum((part_self, part_nbr), ('group', 'member'))]
    all_gather x1, waiting for transfers between devices: 88.5 us -> 13.4 us  [local(): hub_table = lax.all_gather(my_hubs, GROUP, axis=0, tiled=True)]
    all_to_all x2 -> x5, waiting for transfers between devices: 19.3 us -> 74.1 us  [swap_blocks(): return lax.all_to_all(array, axes, split_axis=0, concat_axis=0, tiled=True)]
    scatter-add x12 -> x0, other arithmetic: 42.9 us -> none  [the longest x10 35.8 us: local(): spread = spread.at[neighbours[:, sample]].add(dagg)]
    gather x12 -> x0, local copies, waits for them, and re-layouts: 19.5 us -> none  [the longest x10 13 us: local(): agg_sum = agg_sum + table[neighbours[:, sample]].astype(jnp.float32)]
    all_to_all x2 -> x5, starting transfers between devices: 27.3 us -> 43.5 us  [swap_blocks(): return lax.all_to_all(array, axes, split_axis=0, concat_axis=0, tiled=True)]
    dot_general x6 -> x10, matrix products: 6.16 us -> 18.1 us  [the longest x1 7.93 us: local(): lax.dot_general(counts, dagg, over_rows, preferred_element_type=F32)]
    gather x12 -> x0, other arithmetic: 5.96 us -> none  [the longest x10 5.95 us: local(): agg_sum = agg_sum + table[neighbours[:, sample]].astype(jnp.float32)]
  transfers between devices with their start and end apart: 4 -> 7, of which waited for: 3 -> 7; matrix products, arithmetic and copies ran while one was open for 5% -> 7% of each run, Pallas kernels for 0% -> 0%
where the time goes in v1:
time: 185 us; the launch traced here: 184 us
  waiting for transfers between devices  89.3 us (48%)
  starting transfers between devices  45.4 us (25%)
  matrix products  18.1 us (10%)
  between operations  14.4 us (8%)
  other arithmetic  10.8 us (6%)
  local copies, waits for them, and re-layouts  6.07 us (3%)
    all_to_all x5, waiting for transfers between devices, swap_blocks(): return lax.all_to_all(array, axes, split_axis=0, concat_axis=0, tiled=True)  74.1 us
    all_to_all x5, starting transfers between devices, swap_blocks(): return lax.all_to_all(array, axes, split_axis=0, concat_axis=0, tiled=True)  43.5 us
    all_gather x1, waiting for transfers between devices, local(): hub_table = lax.all_gather(my_hubs, GROUP, axis=0, tiled=True)  13.4 us
    dot_general x1, matrix products, local(): lax.dot_general(counts, dagg, over_rows, preferred_element_type=F32)  7.93 us
    add x1, other arithmetic, local(): counts = counts + (column[:, f:f + 1] == ids[None, :]).astype(BF)  5.86 us
  transfers between devices with their start and end apart: 7, of which 7 were waited for; matrix products, arithmetic and copies ran while one was open for 7% of the time, Pallas kernels for 0%

profile of v1, /device:TPU:16, one launch (start us, length us, event | category | flops | bytes accessed | tf_op | source)
XLA Modules:
  0.0 184.2 jit_solution(1674754660080060285)
XLA Ops:
  7.2 0.0 copy-start
  7.2 0.0 copy-start.2
  7.2 0.8 pad.12.clone
  8.0 0.1 pad.13.clone
  8.1 0.7 fusion.52
  8.8 0.1 add_add_fusion
  8.8 0.1 copy.15
  8.9 0.1 eq.222
  9.0 2.2 %convolution_convert_fusion = bf16[1536,256]{1,0:T(8,128)(2,1)} fusion(bf16[256,256]{1,0:T(8,128)(2,1)} %param.8, s32[1536]{0:T(1024)S(1)} %eq.222), kind=kOutput, calls=%fused_computation.20 | convolution fusion | flops 202113024 | bytes 923648 | tf_op jit(solution)/shard_map/dot_general | solution.py:41
  11.3 16.5 %all-to-all-start = ((bf16[64,24,256]{2,1,0:T(8,128)(2,1)}), bf16[64,24,256]{2,1,0:T(8,128)(2,1)S(1)}, u32[]{:S(2)}, u32[]{:S(2)}) async-start(bf16[64,24,256]{2,1,0:T(8,128)(2,1)} %bitcast.11), calls=%async_computation | async-start | bytes 1572864 | tf_op jit(solution)/shard_map/all_to_all | solution.py:16
  27.7 0.0 all-gather.2.cloned.1.call-start
  27.8 1.0 copy.17
  28.8 23.8 %all-to-all-done = bf16[64,24,256]{2,1,0:T(8,128)(2,1)S(1)} async-done(((bf16[64,24,256]{2,1,0:T(8,128)(2,1)}), bf16[64,24,256]{2,1,0:T(8,128)(2,1)S(1)}, u32[]{:S(2)}, u32[]{:S(2)}) %all-to-all-start) | async-done | bytes 786464 | tf_op jit(solution)/shard_map/all_to_all | solution.py:16
  52.6 0.7 reshape.62
  53.3 0.0 all-gather.2.cloned.1.call-update
  53.4 0.7 fusion.47
  54.1 0.0 copy-start.5
  54.1 0.0 copy-start.6
  54.1 0.0 copy-start.7
  54.2 0.0 copy-start.8
  54.2 0.0 copy-start.9
  54.2 0.0 copy-start.10
  54.2 0.0 copy-start.11
  54.2 0.0 copy-start.12
  54.2 1.9 %fusion.59 = f32[256,256]{1,0:T(8,128)} fusion(bf16[256,256]{1,0:T(8,128)(2,1)} %param.8, bf16[256,256]{1,0:T(8,128)(2,1)} %param.13), kind=kOutput, calls=%fused_computation.98 | convolution fusion | flops 33554432 | bytes 524288 | tf_op jit(solution)/shard_map/dot_general | solution.py:69
  56.1 0.0 copy-done.5
  56.1 5.9 %fusion.10 = bf16[256,3840]{1,0:T(8,128)(2,1)S(1)} fusion(s32[256]{0:T(256)S(1)} %bitcast.47, s32[256]{0:T(256)S(1)} %bitcast.49, s32[256]{0:T(256)S(1)} %bitcast.51, s32[256]{0:T(256)S(1)} %bitcast.53, s32[256]{0:T(256)S(1)} %bitcast.55, s32[256]{0:T(256)S(1)} %bitcast.57, s32[256]{0:T(256)S(1)} %bitcast.59, s32[256]{0:T(256)S(1)} %bitcast.61, ...), kind=kLoop, calls=%fused_computation.21 | loop fusion | flops 39321600 | bytes 1976320 | tf_op jit(solution)/shard_map/add | solution.py:61
  61.9 0.0 copy-done.6
  62.0 0.0 copy-done.7
  62.0 0.2 fusion.40
  62.3 13.4 %all-gather.2.cloned.1.call-done = bf16[2048,256]{1,0:T(8,128)(2,1)} async-done(((bf16[256,256]{1,0:T(8,128)(2,1)}), bf16[2048,256]{1,0:T(8,128)(2,1)}) %all-gather.2.cloned.1.call-update) | async-done | bytes 1048592 | tf_op jit(solution)/shard_map/all_gather | solution.py:44
  75.6 1.8 fusion.28
  77.4 0.4 fusion.24
  77.9 1.2 multiply_convert_fusion
  79.1 7.9 %fusion.58 = (bf16[3840,256]{1,0:T(8,128)(2,1)S(1)}, f32[3840,256]{1,0:T(8,128)}) fusion(bf16[256,256]{1,0:T(8,128)(2,1)S(1)} %multiply_convert_fusion, bf16[256,256]{1,0:T(8,128)(2,1)S(1)} %copy-done, s32[256]{0:T(256)S(1)} %bitcast.48, s32[256]{0:T(256)} %bitcast.50, s32[256]{0:T(256)} %bitcast.52, s32[256]{0:T(256)} %bitcast.54, s32[256]{0:T(256)} %bitcast.56, ...), kind=kOutput, calls=%fused_computation.97 | convolution fusion | flops 577306624 | bytes 6170624 | tf_op jit(solution)/shard_map/dot_general | solution.py:76
  87.0 0.2 fusion.21
  87.3 0.1 slice.120
  87.4 1.2 pad_maximum_fusion
  88.6 13.4 %all-to-all-start.1 = ((bf16[64,24,256]{2,1,0:T(8,128)(2,1)}), bf16[64,24,256]{2,1,0:T(8,128)(2,1)S(1)}, u32[]{:S(2)}, u32[]{:S(2)}) async-start(bf16[64,24,256]{2,1,0:T(8,128)(2,1)} %pad_maximum_fusion), calls=%async_computation.1 | async-start | bytes 1572864 | tf_op jit(solution)/shard_map/all_to_all | solution.py:16
  102.0 1.3 slice.123
  103.3 0.0 copy-start.13
  103.3 0.0 copy-start.3
  103.4 1.9 %collective-permute-start = (bf16[4,256,256]{2,1,0:T(8,128)(2,1)S(1)}, bf16[4,256,256]{2,1,0:T(8,128)(2,1)S(1)}, u32[]{:S(2)}, u32[]{:S(2)}) collective-permute-start(bf16[4,256,256]{2,1,0:T(8,128)(2,1)S(1)} %dynamic-slice_bitcast_fusion), channel_id=1, source_target_pairs={{0,64},{64,0},{1,65},{65,1},{2,66},{66,2},{3,67},{67,3},{4,68},{68... | collective-permute-start | bytes 1572872 | tf_op jit(solution)/shard_map/ppermute | solution.py:93
  105.3 1.9 %collective-permute-done = bf16[4,256,256]{2,1,0:T(8,128)(2,1)S(1)} collective-permute-done((bf16[4,256,256]{2,1,0:T(8,128)(2,1)S(1)}, bf16[4,256,256]{2,1,0:T(8,128)(2,1)S(1)}, u32[]{:S(2)}, u32[]{:S(2)}) %collective-permute-start) | collective-permute-done | bytes 524320 | tf_op jit(solution)/shard_map/ppermute | solution.py:93
  107.2 0.9 fusion.30
  108.1 19.2 %all-to-all-done.1 = bf16[64,24,256]{2,1,0:T(8,128)(2,1)S(1)} async-done(((bf16[64,24,256]{2,1,0:T(8,128)(2,1)}), bf16[64,24,256]{2,1,0:T(8,128)(2,1)S(1)}, u32[]{:S(2)}, u32[]{:S(2)}) %all-to-all-start.1) | async-done | bytes 786464 | tf_op jit(solution)/shard_map/all_to_all | solution.py:16
  127.3 3.5 %all-to-all-start.3 = ((bf16[4,256,256]{2,1,0:T(8,128)(2,1)}), bf16[4,256,256]{2,1,0:T(8,128)(2,1)S(1)}, u32[]{:S(2)}, u32[]{:S(2)}) async-start(bf16[4,256,256]{2,1,0:T(8,128)(2,1)} %fusion.30), calls=%async_computation.3 | async-start | bytes 1048576 | tf_op jit(solution)/shard_map/all_to_all | solution.py:16
  130.8 0.1 slice_reduce_fusion
  130.9 8.0 %all-to-all-done.3 = bf16[4,256,256]{2,1,0:T(8,128)(2,1)S(1)} async-done(((bf16[4,256,256]{2,1,0:T(8,128)(2,1)}), bf16[4,256,256]{2,1,0:T(8,128)(2,1)S(1)}, u32[]{:S(2)}, u32[]{:S(2)}) %all-to-all-start.3) | async-done | bytes 524320 | tf_op jit(solution)/shard_map/all_to_all | solution.py:16
  138.9 0.6 broadcast_in_dim.20
  139.5 3.3 %all-to-all-start.2 = ((bf16[8,8,256]{2,1,0:T(8,128)(2,1)}), bf16[8,8,256]{2,1,0:T(8,128)(2,1)S(1)}, u32[]{:S(2)}, u32[]{:S(2)}) async-start(bf16[8,8,256]{2,1,0:T(8,128)(2,1)} %broadcast_in_dim.20), calls=%async_computation.2 | async-start | bytes 65536 | tf_op jit(solution)/shard_map/all_to_all | solution.py:16
  142.8 0.1 pad.6.clone
  142.9 0.1 reduce_sum.49
  143.0 5.2 %all-to-all-done.2 = bf16[8,8,256]{2,1,0:T(8,128)(2,1)S(1)} async-done(((bf16[8,8,256]{2,1,0:T(8,128)(2,1)}), bf16[8,8,256]{2,1,0:T(8,128)(2,1)S(1)}, u32[]{:S(2)}, u32[]{:S(2)}) %all-to-all-start.2) | async-done | bytes 32800 | tf_op jit(solution)/shard_map/all_to_all | solution.py:16
  148.2 0.9 maximum_maximum_fusion
  149.2 6.8 %all-to-all-start.4 = ((bf16[64,16,256]{2,1,0:T(8,128)(2,1)}), bf16[64,16,256]{2,1,0:T(8,128)(2,1)S(1)}, u32[]{:S(2)}, u32[]{:S(2)}) async-start(bf16[64,16,256]{2,1,0:T(8,128)(2,1)} %maximum_maximum_fusion), calls=%async_computation.4 | async-start | bytes 1048576 | tf_op jit(solution)/shard_map/all_to_all | solution.py:16
  156.0 0.1 copy.18
  156.1 0.1 reshape.66
  156.2 0.0 copy-done.3
  156.2 1.2 convolution_add_fusion
  157.5 17.9 %all-to-all-done.4 = bf16[64,16,256]{2,1,0:T(8,128)(2,1)S(1)} async-done(((bf16[64,16,256]{2,1,0:T(8,128)(2,1)}), bf16[64,16,256]{2,1,0:T(8,128)(2,1)S(1)}, u32[]{:S(2)}, u32[]{:S(2)}) %all-to-all-start.4) | async-done | bytes 524320 | tf_op jit(solution)/shard_map/all_to_all | solution.py:16
  175.4 0.8 slice_bitcast_fusion
  176.2 0.1 slice_reduce_fusion.1
  176.3 1.0 fusion.26
  (25 shorter events, 0.3 us)
Async XLA Ops:
  7.2 70.7 %copy-start = (bf16[256,256]{1,0:T(8,128)(2,1)S(1)}, bf16[256,256]{1,0:T(8,128)(2,1)}, u32[]{:S(2)}) copy-start(bf16[256,256]{1,0:T(8,128)(2,1)} %param.14) | copy-start | bytes 393220
  7.2 54.8 %copy-start.2 = (bf16[256,256]{1,0:T(8,128)(2,1)S(1)}, bf16[256,256]{1,0:T(8,128)(2,1)}, u32[]{:S(2)}) copy-start(bf16[256,256]{1,0:T(8,128)(2,1)} %param.8) | copy-start | bytes 393220
  11.3 41.3 %all-to-all-start = ((bf16[64,24,256]{2,1,0:T(8,128)(2,1)}), bf16[64,24,256]{2,1,0:T(8,128)(2,1)S(1)}, u32[]{:S(2)}, u32[]{:S(2)}) async-start(bf16[64,24,256]{2,1,0:T(8,128)(2,1)} %bitcast.11), calls=%async_computation | async-start | bytes 1572864 | tf_op jit(solution)/shard_map/all_to_all | solution.py:16
  27.7 47.9 %all-gather.2.cloned.1.call-start = ((), (), s32[]{:S(2)}) async-start(), calls=%async_computation.5 | async-start | bytes 1179648 | tf_op jit(solution)/shard_map/all_gather | solution.py:44
  54.1 1.9 %copy-start.5 = (s32[256,1]{0,1:T(1,128)}, s32[256,1]{0,1:T(1,128)S(1)}, u32[]{:S(2)}) copy-start(s32[256,1]{0,1:T(1,128)S(1)} %get-tuple-element.7) | copy-start | bytes 3076
  54.1 7.8 %copy-start.6 = (s32[256,1]{0,1:T(1,128)}, s32[256,1]{0,1:T(1,128)S(1)}, u32[]{:S(2)}) copy-start(s32[256,1]{0,1:T(1,128)S(1)} %get-tuple-element.8) | copy-start | bytes 3076
  54.1 7.8 %copy-start.7 = (s32[256,1]{0,1:T(1,128)}, s32[256,1]{0,1:T(1,128)S(1)}, u32[]{:S(2)}) copy-start(s32[256,1]{0,1:T(1,128)S(1)} %get-tuple-element.9) | copy-start | bytes 3076
  54.2 7.8 %copy-start.8 = (s32[256,1]{0,1:T(1,128)}, s32[256,1]{0,1:T(1,128)S(1)}, u32[]{:S(2)}) copy-start(s32[256,1]{0,1:T(1,128)S(1)} %get-tuple-element.10) | copy-start | bytes 3076
  54.2 7.8 %copy-start.9 = (s32[256,1]{0,1:T(1,128)}, s32[256,1]{0,1:T(1,128)S(1)}, u32[]{:S(2)}) copy-start(s32[256,1]{0,1:T(1,128)S(1)} %get-tuple-element.11) | copy-start | bytes 3076
  54.2 7.8 %copy-start.10 = (s32[256,1]{0,1:T(1,128)}, s32[256,1]{0,1:T(1,128)S(1)}, u32[]{:S(2)}) copy-start(s32[256,1]{0,1:T(1,128)S(1)} %get-tuple-element.12) | copy-start | bytes 3076
  54.2 7.8 %copy-start.11 = (s32[256,1]{0,1:T(1,128)}, s32[256,1]{0,1:T(1,128)S(1)}, u32[]{:S(2)}) copy-start(s32[256,1]{0,1:T(1,128)S(1)} %get-tuple-element.13) | copy-start | bytes 3076
  54.2 7.8 %copy-start.12 = (s32[256,1]{0,1:T(1,128)}, s32[256,1]{0,1:T(1,128)S(1)}, u32[]{:S(2)}) copy-start(s32[256,1]{0,1:T(1,128)S(1)} %get-tuple-element.14) | copy-start | bytes 3076
  75.6 2.3 %copy-start.4 = (f32[256,256]{1,0:T(8,128)S(1)}, f32[256,256]{1,0:T(8,128)}, u32[]{:S(2)}) copy-start(f32[256,256]{1,0:T(8,128)} %fusion.59) | copy-start | bytes 786436
  87.0 1.6 copy-start.1
  88.6 38.7 %all-to-all-start.1 = ((bf16[64,24,256]{2,1,0:T(8,128)(2,1)}), bf16[64,24,256]{2,1,0:T(8,128)(2,1)S(1)}, u32[]{:S(2)}, u32[]{:S(2)}) async-start(bf16[64,24,256]{2,1,0:T(8,128)(2,1)} %pad_maximum_fusion), calls=%async_computation.1 | async-start | bytes 1572864 | tf_op jit(solution)/shard_map/all_to_all | solution.py:16
  103.3 52.9 %copy-start.13 = (s32[1,4]{1,0:T(1,128)S(1)}, s32[1,4]{1,0:T(1,128)}, u32[]{:S(2)}) copy-start(s32[1,4]{1,0:T(1,128)} %param.12) | copy-start | bytes 52
  103.3 52.9 %copy-start.3 = (bf16[256,256]{1,0:T(8,128)(2,1)S(1)}, bf16[256,256]{1,0:T(8,128)(2,1)}, u32[]{:S(2)}) copy-start(bf16[256,256]{1,0:T(8,128)(2,1)} %param.13) | copy-start | bytes 393220
  103.4 3.8 %collective-permute-start = (bf16[4,256,256]{2,1,0:T(8,128)(2,1)S(1)}, bf16[4,256,256]{2,1,0:T(8,128)(2,1)S(1)}, u32[]{:S(2)}, u32[]{:S(2)}) collective-permute-start(bf16[4,256,256]{2,1,0:T(8,128)(2,1)S(1)} %dynamic-slice_bitcast_fusion), channel_id=1, source_target_pairs={{0,64},{64,0},{1,65},{65,1},{2,66},{66,2},{3,67},{67,3},{4,68},{68... | collective-permute-start | bytes 1572872 | tf_op jit(solution)/shard_map/ppermute | solution.py:93
  127.3 11.5 %all-to-all-start.3 = ((bf16[4,256,256]{2,1,0:T(8,128)(2,1)}), bf16[4,256,256]{2,1,0:T(8,128)(2,1)S(1)}, u32[]{:S(2)}, u32[]{:S(2)}) async-start(bf16[4,256,256]{2,1,0:T(8,128)(2,1)} %fusion.30), calls=%async_computation.3 | async-start | bytes 1048576 | tf_op jit(solution)/shard_map/all_to_all | solution.py:16
  139.5 8.7 %all-to-all-start.2 = ((bf16[8,8,256]{2,1,0:T(8,128)(2,1)}), bf16[8,8,256]{2,1,0:T(8,128)(2,1)S(1)}, u32[]{:S(2)}, u32[]{:S(2)}) async-start(bf16[8,8,256]{2,1,0:T(8,128)(2,1)} %broadcast_in_dim.20), calls=%async_computation.2 | async-start | bytes 65536 | tf_op jit(solution)/shard_map/all_to_all | solution.py:16
  149.2 26.2 %all-to-all-start.4 = ((bf16[64,16,256]{2,1,0:T(8,128)(2,1)}), bf16[64,16,256]{2,1,0:T(8,128)(2,1)S(1)}, u32[]{:S(2)}, u32[]{:S(2)}) async-start(bf16[64,16,256]{2,1,0:T(8,128)(2,1)} %maximum_maximum_fusion), calls=%async_computation.4 | async-start | bytes 1048576 | tf_op jit(solution)/shard_map/all_to_all | solution.py:16
Sparse Core Ops, SparseCore 0:
  53.5 22.0 all-gather.1

commit v2 on v0

v2 whole, which is shorter than its diff:
```python
import functools
import math

import jax
import jax.numpy as jnp
from jax import lax
from jax.experimental import pallas as pl
from jax.experimental.pallas import tpu as pltpu
from jax.sharding import Mesh, PartitionSpec as P

BF = jnp.bfloat16
F32 = jnp.float32
I32 = jnp.int32
GROUP = ("x", "core")
MEMBER = ("y", "z")
ALL = ("x", "core", "y", "z")

D = 256
NODES = 256
FAN = 10
MEMBERS = 64
SLOTS = 16
HUBS = 4
GROUPS = 8
XS = 4
HALF = MEMBERS * 8
BORDER = NODES + 2 * HALF
SIDE = XS * MEMBERS * HUBS
TABLE = BORDER + 2 * SIDE
SCALE = 1.0 / math.sqrt(NODES * GROUPS * MEMBERS)
OVER_ROWS = (((0,), (0,)), ((), ()))
OVER_COLS = (((1,), (1,)), ((), ()))

VMEM = pl.BlockSpec(memory_space=pltpu.VMEM)
SMEM = pl.BlockSpec(memory_space=pltpu.SMEM)


def iota(shape, dim):
    return lax.broadcasted_iota(I32, shape, dim)


def dot(a, b):
    return jnp.dot(a, b, preferred_element_type=F32)


def call(body, name, outs, smem, flops, moved, *args):
    return pl.pallas_call(
        body,
        name=name,
        out_shape=[jax.ShapeDtypeStruct(s, t) for s, t in outs],
        in_specs=[SMEM] * smem + [VMEM] * (len(args) - smem),
        out_specs=[VMEM] * len(outs),
        compiler_params=pltpu.CompilerParams(vmem_limit_bytes=40 * 1024 * 1024),
        cost_estimate=pl.CostEstimate(flops=flops, bytes_accessed=moved, transcendentals=0),
    )(*args)


def split_rows(rows):
    left = rows[:, :128].reshape(-1, 8, 128)
    right = rows[:, 128:].reshape(-1, 8, 128)
    low = iota(left.shape, 1) < 4
    even = jnp.where(low, left, pltpu.roll(right, 4, 1))
    odd = jnp.where(low, pltpu.roll(left, 4, 1), right)
    return jnp.stack([even, odd], axis=1).reshape(-1, 8, 128)


def join_rows(tiles):
    pairs = tiles.reshape(-1, 2, 8, 128)
    even, odd = pairs[:, 0], pairs[:, 1]
    low = iota(even.shape, 1) < 4
    left = jnp.where(low, even, pltpu.roll(odd, 4, 1)).reshape(-1, 128)
    right = jnp.where(low, pltpu.roll(even, 4, 1), odd).reshape(-1, 128)
    return left, right


def outgoing_rows(hub, send, count, features, out, pick):
    member = iota((HALF, MEMBERS), 0) >> 3
    own = member == iota((HALF, MEMBERS), 1)
    spread = lax.dot_general(
        own.astype(F32).astype(BF), send[...].astype(F32).astype(BF), OVER_COLS, preferred_element_type=F32
    )
    live = jnp.sum(jnp.where(own, count[...].astype(F32), 0.0), axis=1, keepdims=True)
    lane = iota((HALF, SLOTS), 1)
    slot = iota((HALF, SLOTS), 0) & 7
    place = (iota((HALF, 1), 0) & 7).astype(F32)
    nodes = iota((HALF, NODES), 1).astype(F32)
    f = features[...]
    for a in range(2):
        row = jnp.sum(jnp.where(lane == slot + 8 * a, spread, 0.0), axis=1, keepdims=True)
        row = jnp.where(place + 8.0 * a < live, row, -1.0)
        hot = (nodes == row).astype(F32).astype(BF)
        pick[a * HALF : (a + 1) * HALF, :] = hot
        out[:, a * D : (a + 1) * D] = dot(hot, f).astype(BF)
    which = iota((16, NODES), 0) & 3
    ids = jnp.full((16, NODES), hub[0, 0], I32)
    for h in range(1, HUBS):
        ids = jnp.where(which == h, hub[0, h], ids)
    rows = dot((ids == iota((16, NODES), 1)).astype(F32).astype(BF), f)
    tile = jnp.where(iota((8, 128), 0) < 4, rows[:8, :128], rows[:8, 128:])
    out[:, 2 * D :] = jnp.broadcast_to(tile[None], (MEMBERS, 8, 128)).reshape(HALF, 128).astype(BF)


def table_row(n, core):
    b = n - NODES
    h = b - MEMBERS * SLOTS
    border = NODES + ((b >> 3) & 1) * HALF + (b >> 4) * 8 + (b & 7)
    side = ((h >> 8) & 1) ^ core
    hub = BORDER + side * SIDE + (h >> 9) * 256 + (h & 255)
    return jnp.where(b < 0, n, jnp.where(h < 0, border, hub))


def count_rows(core, near_t, pick, features, w_self, counts, counts_t, home, pre_self):
    row_t = table_row(near_t[...], core[0])
    step = 32

    @pl.loop(0, TABLE // step)
    def _(i):
        base = pl.multiple_of(i * step, step)
        ids = iota((step, NODES), 0) + base
        total = jnp.zeros((step, NODES), F32)
        for f in range(FAN):
            total = total + jnp.where(ids == row_t[f : f + 1, :], 1.0, 0.0)
        counts_t[pl.ds(base, step), :] = total.astype(BF)

    eye = (iota((NODES, NODES), 0) == iota((NODES, NODES), 1)).astype(F32).astype(BF)
    for t in range(TABLE // 256):
        block = lax.dot_general(eye, counts_t[t * 256 : (t + 1) * 256, :], OVER_COLS, preferred_element_type=F32)
        counts[:, t * 256 : (t + 1) * 256] = block.astype(BF)
    home[...] = lax.dot_general(eye, pick[...], OVER_COLS, preferred_element_type=F32).astype(BF)
    pre_self[...] = dot(features[...], w_self[...])


def own_hubs(incoming, out):
    left, right = join_rows(incoming[:, 2 * D :].astype(F32).reshape(MEMBERS, 8, 128))
    left, right = left.astype(BF), right.astype(BF)
    for x in range(XS):
        out[x * 256 : (x + 1) * 256, :128] = left
        out[x * 256 : (x + 1) * 256, 128:] = right


def forward(counts, counts_t, features, incoming, mine, other, pre_self, w_nbr, cotangent, outward, dagg_out, dpre_out):
    f = features[...]
    total = dot(counts[:, :NODES], f)
    total += dot(counts[:, NODES : NODES + HALF], incoming[:, :D])
    total += dot(counts[:, NODES + HALF : BORDER], incoming[:, D : 2 * D])
    total += dot(counts[:, BORDER : BORDER + SIDE], mine[...])
    total += dot(counts[:, BORDER + SIDE :], other[...])
    agg = (total / FAN).astype(BF)
    pre = pre_self[...] + dot(agg, w_nbr[...])
    sigma = 1.0 / (1.0 + jnp.exp(-pre))
    dpre = (cotangent[...].astype(F32) * sigma * (1.0 + pre * (1.0 - sigma))).astype(BF)
    dagg = (lax.dot_general(dpre, w_nbr[...], OVER_COLS, preferred_element_type=F32) / FAN).astype(BF)
    dpre_out[...] = dpre
    dagg_out[...] = dagg
    outward[:, :D] = dot(counts_t[NODES : NODES + HALF, :], dagg).astype(BF)
    outward[:, D : 2 * D] = dot(counts_t[NODES + HALF : BORDER, :], dagg).astype(BF)
    outward[:D, 2 * D :] = lax.dot_general(f, dpre, OVER_ROWS, preferred_element_type=F32).astype(BF)
    outward[D:, 2 * D :] = lax.dot_general(agg, dpre, OVER_ROWS, preferred_element_type=F32).astype(BF)


def other_hubs(counts_t, dagg, out):
    out[...] = dot(counts_t[BORDER + SIDE :, :], dagg[...]).astype(BF)


def mine_and_own(counts_t, dagg, dpre, w_self, hubs, own):
    hubs[...] = dot(counts_t[BORDER : BORDER + SIDE, :], dagg[...]).astype(BF)
    own[...] = dot(counts_t[:NODES, :], dagg[...]) + lax.dot_general(
        dpre[...], w_self[...], OVER_COLS, preferred_element_type=F32
    )


def pair_hubs(x, hubs, met, kept, *to):
    for k, out in enumerate((kept,) + to):
        place = lax.rem(x[0] + k, XS)
        rows = pl.ds(pl.multiple_of(place * 256, 256), 256)
        out[...] = (hubs[rows, :].astype(F32) + met[rows, :].astype(F32)).astype(BF)


def sum_hubs(kept, a, b, c, out):
    total = kept[...].astype(F32) + a[...].astype(F32) + b[...].astype(F32) + c[...].astype(F32)
    out[...] = split_rows(total).reshape(HALF, 128).astype(BF)


def sum_weights(returned, out):
    total = jnp.sum(returned[:, 2 * D :].astype(F32).reshape(MEMBERS, 8, D), axis=0)
    out[...] = jnp.broadcast_to(total[None], (GROUPS, 8, D)).reshape(GROUPS * 8, D).astype(BF)


def add_returned(returned, home, own, out):
    total = own[...] + dot(home[:, :HALF], returned[:, :D])
    out[...] = total + dot(home[:, HALF:], returned[:, D : 2 * D])


def last_message(weights, hubs, out):
    total = jnp.sum(weights[...].astype(F32).reshape(GROUPS, 8, D), axis=0) * SCALE
    out[:, :D] = jnp.broadcast_to(total[None], (MEMBERS, 8, D)).reshape(HALF, D).astype(BF)
    out[:, D:] = hubs[...]


def finish(hub, last, partial, grad_self, grad_nbr, grad):
    grad_self[...] = last[:D, :D].astype(F32)
    grad_nbr[...] = last[D:, :D].astype(F32)
    tile = jnp.sum(last[:, D:].astype(F32).reshape(MEMBERS, 8, 128), axis=0)
    total = partial[...]
    node = iota((NODES, D), 0)
    for h in range(HUBS):
        row = jnp.concatenate([tile[h : h + 1], tile[h + 4 : h + 5]], axis=1)
        total = total + jnp.where(node == hub[0, h], row, 0.0)
    grad[...] = total.astype(BF)


def exchange(array, axes, parts):
    block = array.reshape(parts, -1, array.shape[1])
    return lax.all_to_all(block, axes, split_axis=0, concat_axis=0, tiled=True).reshape(array.shape)


def local(features, neighbours, send_rows, block_counts, hub_rows, w_self, w_nbr, cotangent):
    core = lax.axis_index("core").reshape(1)
    x = lax.axis_index("x").reshape(1)
    counts_in = block_counts.reshape(1, MEMBERS)
    outgoing, pick = call(
        outgoing_rows, "outgoing_rows", [((HALF, 640), BF), ((2 * HALF, NODES), BF)], 1, 2**27, 2**20,
        hub_rows, send_rows.T, counts_in, features,
    )
    incoming = exchange(outgoing, MEMBER, MEMBERS)
    counts, counts_t, home, pre_self = call(
        count_rows, "count_rows",
        [((NODES, TABLE), BF), ((TABLE, NODES), BF), ((NODES, 2 * HALF), BF), ((NODES, D), F32)],
        1, 2**30, 2**22,
        core, neighbours.T, pick, features, w_self,
    )
    (mine,) = call(own_hubs, "own_hubs", [((SIDE, D), BF)], 0, 2**16, 2**19, incoming)
    mine = exchange(mine, "x", XS)
    swap = [(0, 1), (1, 0)]
    other = lax.ppermute(mine, "core", swap)
    outward, dagg, dpre = call(
        forward, "forward", [((HALF, 768), BF), ((NODES, D), BF), ((NODES, D), BF)], 0, 2**30, 2**23,
        counts, counts_t, features, incoming, mine, other, pre_self, w_nbr, cotangent,
    )
    returned = exchange(outward, MEMBER, MEMBERS)

    (theirs,) = call(other_hubs, "other_hubs", [((SIDE, D), BF)], 0, 2**27, 2**20, counts_t, dagg)
    met = lax.ppermute(theirs, "core", swap)
    hubs, own = call(
        mine_and_own, "mine_and_own", [((SIDE, D), BF), ((NODES, D), F32)], 0, 2**28, 2**21, counts_t, dagg, dpre, w_self
    )
    block = ((NODES, D), BF)
    kept, *to = call(pair_hubs, "pair_hubs", [block] * XS, 1, 2**18, 2**20, x, hubs, met)
    came = [lax.ppermute(to[k - 1], "x", [(i, (i + k) % XS) for i in range(XS)]) for k in range(1, XS)]
    (hub_tiles,) = call(sum_hubs, "sum_hubs", [((HALF, 128), BF)], 0, 2**18, 2**20, kept, *came)

    (weights,) = call(sum_weights, "sum_weights", [((GROUPS * 8, D), BF)], 0, 2**17, 2**18, returned)
    weights = exchange(weights, GROUP, GROUPS)
    (partial,) = call(add_returned, "add_returned", [((NODES, D), F32)], 0, 2**27, 2**20, returned, home, own)
    (message,) = call(last_message, "last_message", [((HALF, 384), BF)], 0, 2**17, 2**18, weights, hub_tiles)
    last = exchange(message, MEMBER, MEMBERS)
    return tuple(
        call(
            finish, "finish", [((D, D), F32), ((D, D), F32), ((NODES, D), BF)], 1, 2**18, 2**20, hub_rows, last, partial
        )
    )


def solution(mesh):
    split = Mesh(mesh.devices.reshape(XS, 2, 8, 8), ALL)
    rows = P(ALL, None)
    in_specs = (rows, rows, rows, P(ALL), rows, P(), P(), rows)
    out_specs = (P(), P(), rows)
    return jax.shard_map(local, mesh=split, in_specs=in_specs, out_specs=out_specs, check_vma=False)
```

time: 489 us -> 137 us (0.28)
  waiting for transfers between devices: 358 us -> 31.5 us
  other arithmetic: 53.6 us -> 0 us
  blocking collectives: 0 us -> 50.8 us
  local copies, waits for them, and re-layouts: 26.1 us -> 9.78 us
  Pallas kernels: 0 us -> 14.7 us
  between operations: 14.5 us -> 0.9 us
  matrix products: 6.16 us -> 0 us
    psum x1 -> x0, waiting for transfers between devices: 250 us -> none  [local(): lax.psum((part_self, part_nbr), ('group', 'member'))]
    all_gather x1 -> x0, waiting for transfers between devices: 88.5 us -> none  [local(): lax.all_gather(owned_hubs, ('group', 'member'), axis=0, tiled=True)]
    all_to_all x0 -> x2, blocking collectives: none -> 50.8 us  [exchange(): lax.all_to_all(block, axes, split_axis=0, concat_axis=0, tiled=True)]
    scatter-add x12 -> x0, other arithmetic: 42.9 us -> none  [the longest x10 35.8 us: local(): spread = spread.at[neighbours[:, sample]].add(dagg)]
    gather x12 -> x0, local copies, waits for them, and re-layouts: 19.5 us -> none  [the longest x10 13 us: local(): agg_sum = agg_sum + table[neighbours[:, sample]].astype(jnp.float32)]
    pallas_call x0 -> x12, Pallas kernels: none -> 14.7 us  [call(): pl.pallas_call(body, name=name, out_shape=[jax.ShapeDtypeStruct(s, t) for...]
    ppermute x0 -> x5, starting transfers between devices: none -> 13 us  [the longest x3 9.18 us: local(): lax.ppermute(to[k - 1], 'x', [(i, (i + k) % XS) for i in range(XS)])]
    all_to_all x2 -> x3, starting transfers between devices: 27.3 us -> 15.3 us  [exchange(): lax.all_to_all(block, axes, split_axis=0, concat_axis=0, tiled=True)]
  transfers between devices with their start and end apart: 4 -> 8, of which waited for: 3 -> 4; matrix products, arithmetic and copies ran while one was open for 5% -> 0% of each run, Pallas kernels for 0% -> 6%
where the time goes in v2:
time: 137 us; the launch traced here: 136 us
  blocking collectives  50.8 us (37%)
  waiting for transfers between devices  31.5 us (23%)
  starting transfers between devices  28.3 us (21%)
  Pallas kernels  14.7 us (11%)
  local copies, waits for them, and re-layouts  9.78 us (7%)
    all_to_all x2, blocking collectives, exchange(): lax.all_to_all(block, axes, split_axis=0, concat_axis=0, tiled=True)  50.8 us
    all_to_all x3, waiting for transfers between devices, exchange(): lax.all_to_all(block, axes, split_axis=0, concat_axis=0, tiled=True)  30.6 us
    all_to_all x3, starting transfers between devices, exchange(): lax.all_to_all(block, axes, split_axis=0, concat_axis=0, tiled=True)  15.3 us
    pallas_call x12, Pallas kernels, call(): pl.pallas_call(body, name=name, out_shape=[jax.ShapeDtypeStruct(s, t) for...  14.7 us
    unnamed x36, local copies, waits for them, and re-layouts  9.78 us
    ppermute x3, starting transfers between devices, local(): lax.ppermute(to[k - 1], 'x', [(i, (i + k) % XS) for i in range(XS)])  9.18 us
  transfers between devices with their start and end apart: 8, of which 4 were waited for; matrix products, arithmetic and copies ran while one was open for 0% of the time, Pallas kernels for 6%

profile of v2, /device:TPU:16, one launch (start us, length us, event | category | flops | bytes accessed | tf_op | source)
XLA Modules:
  0.0 136.0 jit_solution(17239688452220142725)
XLA Ops:
  0.6 0.0 copy-start.3
  0.6 0.9 copy-done.3
  1.5 0.0 copy-start.11
  1.5 0.7 copy-done.11
  2.2 0.0 copy-start.14
  2.2 0.7 copy-done.14
  2.9 0.0 copy-start.15
  2.9 0.7 copy-done.15
  3.5 1.1 outgoing_rows.1
  4.6 0.0 copy-start.16
  4.7 0.0 copy-start.13
  4.7 38.6 %all_to_all.25 = bf16[64,8,640]{2,1,0:T(8,128)(2,1)S(1)} all-to-all(bf16[64,8,640]{2,1,0:T(8,128)(2,1)S(1)} %bitcast.24), channel_id=1, replica_groups=mesh['x'=4,'core'=2,'y'=8,'z'=8] {'y','z'}, dimensions={0} | all-to-all | bytes 1310720 | tf_op jit(solution)/shard_map/all_to_all | solution.py:214
  43.3 0.1 own_hubs.1
  43.4 12.2 %all_to_all.26 = bf16[4,256,256]{2,1,0:T(8,128)(2,1)S(1)} all-to-all(bf16[4,256,256]{2,1,0:T(8,128)(2,1)S(1)} %bitcast.19), channel_id=1, replica_groups=mesh['x'=4,'core'=2,'y'=8,'z'=8] {'x'}, dimensions={0} | all-to-all | bytes 1048576 | tf_op jit(solution)/shard_map/all_to_all | solution.py:214
  55.5 0.0 copy-done.16
  55.5 1.9 %collective-permute-start = (bf16[1024,256]{1,0:T(8,128)(2,1)S(1)}, bf16[1024,256]{1,0:T(8,128)(2,1)}, u32[]{:S(2)}, u32[]{:S(2)}) collective-permute-start(bf16[1024,256]{1,0:T(8,128)(2,1)S(1)} %bitcast.20), channel_id=1, source_target_pairs={{0,64},{64,0},{1,65},{65,1},{2,66},{66,2},{3,67},{67,3},{4,68},{68... | collective-permute-start | bytes 1572872 | tf_op jit(solution)/shard_map/ppermute | solution.py:235
  57.5 0.0 copy-done.13
  57.5 0.0 copy-start.4
  57.5 0.9 copy-done.4
  58.4 0.0 copy-start.7
  58.4 0.9 copy-done.7
  59.3 0.0 copy-start.17
  59.3 1.0 copy-done.17
  60.3 0.0 copy-start.5
  60.3 0.0 copy-start.6
  60.3 4.9 %count_rows.1 = (bf16[256,3328]{1,0:T(8,128)(2,1)S(1)}, bf16[3328,256]{1,0:T(8,128)(2,1)S(1)}, bf16[256,1024]{1,0:T(8,128)(2,1)S(1)}, f32[256,256]{1,0:T(8,128)S(1)}) custom-call(s32[1]{0:T(128)} %bitcast.core, s32[10,256]{1,0:T(8,128)S(1)} %bitcast.26, bf16[1024,256]{1,0:T(8,128)(2,1)S(1)} %copy-done.17, bf16[256,256]{1,0:T(8,128)(2,1)S(1)} %copy-done.4, ...), custom_call_target="tpu_custom_call" | custom-call | flops 1073741824 | bytes 4194304 | tf_op jit(solution)/shard_map/count_rows/pallas_call | solution.py:47
  65.3 0.0 collective-permute-done.other
  65.3 0.0 copy-done.5
  65.3 0.0 copy-done.6
  65.3 2.7 %forward.1 = (bf16[512,768]{1,0:T(8,128)(2,1)S(1)}, bf16[256,256]{1,0:T(8,128)(2,1)S(1)}, bf16[256,256]{1,0:T(8,128)(2,1)S(1)}) custom-call(bf16[256,3328]{1,0:T(8,128)(2,1)S(1)} %get-tuple-element.19.counts, bf16[3328,256]{1,0:T(8,128)(2,1)S(1)} %get-tuple-element.20.counts_t, bf16[256,256]{1,0:T(8,128)(2,1)S(1)} %copy-done.4, ...), custom_call_target="tpu_custom_call" | custom-call | flops 1073741824 | bytes 8388608 | tf_op jit(solution)/shard_map/forward/pallas_call | solution.py:47
  68.0 0.0 copy-start
  68.0 0.9 copy-done
  68.9 0.0 copy-start.1
  68.9 0.7 copy-done.1
  69.6 0.7 copy-done.9
  70.3 6.6 %all-to-all-start.2 = ((bf16[64,8,768]{2,1,0:T(8,128)(2,1)}), bf16[64,8,768]{2,1,0:T(8,128)(2,1)S(1)}, u32[]{:S(2)}, u32[]{:S(2)}) async-start(bf16[64,8,768]{2,1,0:T(8,128)(2,1)} %bitcast.23), calls=%async_computation.2 | async-start | bytes 1572864 | tf_op jit(solution)/shard_map/all_to_all | solution.py:214
  76.9 0.0 copy-start.2
  76.9 0.9 copy-done.2
  77.8 1.1 other_hubs.1
  78.9 1.9 %collective-permute-start.1 = (bf16[1024,256]{1,0:T(8,128)(2,1)}, bf16[1024,256]{1,0:T(8,128)(2,1)}, u32[]{:S(2)}, u32[]{:S(2)}) collective-permute-start(bf16[1024,256]{1,0:T(8,128)(2,1)} %other_hubs.1), channel_id=1, source_target_pairs={{0,64},{64,0},{1,65},{65,1},{2,66},{66,2},{3,67},{67,3},{4,68},{68... | collective-permute-start | bytes 1572872 | tf_op jit(solution)/shard_map/ppermute | solution.py:243
  80.8 0.0 copy-done.8
  80.8 0.0 copy-start.10
  80.8 0.9 copy-done.10
  81.7 0.4 mine_and_own.1
  82.1 0.9 collective-permute-done.1.met
  83.0 1.2 pair_hubs.1
  84.2 2.5 %collective-permute-start.2 = (bf16[256,256]{1,0:T(8,128)(2,1)S(1)}, bf16[256,256]{1,0:T(8,128)(2,1)S(1)}, u32[]{:S(2)}, u32[]{:S(2)}) collective-permute-start(bf16[256,256]{1,0:T(8,128)(2,1)S(1)} %get-tuple-element.28), channel_id=1, source_target_pairs={{0,128},{128,256},{256,384},{384,0},{1,129},{129,257},{257,385},{3... | collective-permute-start | bytes 393224 | tf_op jit(solution)/shard_map/ppermute | solution.py:249
  86.7 4.0 %collective-permute-start.3 = (bf16[256,256]{1,0:T(8,128)(2,1)S(1)}, bf16[256,256]{1,0:T(8,128)(2,1)S(1)}, u32[]{:S(2)}, u32[]{:S(2)}) collective-permute-start(bf16[256,256]{1,0:T(8,128)(2,1)S(1)} %get-tuple-element.29), channel_id=1, source_target_pairs={{0,256},{128,384},{256,0},{384,128},{1,257},{129,385},{257,1},{385... | collective-permute-start | bytes 393224 | tf_op jit(solution)/shard_map/ppermute | solution.py:249
  90.7 2.7 %collective-permute-start.4 = (bf16[256,256]{1,0:T(8,128)(2,1)S(1)}, bf16[256,256]{1,0:T(8,128)(2,1)S(1)}, u32[]{:S(2)}, u32[]{:S(2)}) collective-permute-start(bf16[256,256]{1,0:T(8,128)(2,1)S(1)} %get-tuple-element.30), channel_id=1, source_target_pairs={{0,384},{128,0},{256,128},{384,256},{1,385},{129,1},{257,129},{385... | collective-permute-start | bytes 393224 | tf_op jit(solution)/shard_map/ppermute | solution.py:249
  93.4 9.1 %all-to-all-done.2 = bf16[64,8,768]{2,1,0:T(8,128)(2,1)S(1)} async-done(((bf16[64,8,768]{2,1,0:T(8,128)(2,1)}), bf16[64,8,768]{2,1,0:T(8,128)(2,1)S(1)}, u32[]{:S(2)}, u32[]{:S(2)}) %all-to-all-start.2) | async-done | bytes 786464 | tf_op jit(solution)/shard_map/all_to_all | solution.py:214
  102.5 0.7 sum_weights.1
  103.1 3.3 %all-to-all-start.3 = ((bf16[8,8,256]{2,1,0:T(8,128)(2,1)}), bf16[8,8,256]{2,1,0:T(8,128)(2,1)S(1)}, u32[]{:S(2)}, u32[]{:S(2)}) async-start(bf16[8,8,256]{2,1,0:T(8,128)(2,1)} %bitcast.10), calls=%async_computation.3 | async-start | bytes 65536 | tf_op jit(solution)/shard_map/all_to_all | solution.py:214
  106.5 0.0 collective-permute-done.2.a
  106.5 0.0 collective-permute-done.3.b
  106.5 0.0 collective-permute-done.4.c
  106.5 0.1 sum_hubs.1.hubs
  106.6 0.0 copy-start.12
  106.6 5.2 %all-to-all-done.3 = bf16[8,8,256]{2,1,0:T(8,128)(2,1)S(1)} async-done(((bf16[8,8,256]{2,1,0:T(8,128)(2,1)}), bf16[8,8,256]{2,1,0:T(8,128)(2,1)S(1)}, u32[]{:S(2)}, u32[]{:S(2)}) %all-to-all-start.3) | async-done | bytes 32800 | tf_op jit(solution)/shard_map/all_to_all | solution.py:214
  111.9 0.8 last_message.1
  112.6 5.3 %all-to-all-start.4 = ((bf16[64,8,384]{2,1,0:T(8,128)(2,1)}), bf16[64,8,384]{2,1,0:T(8,128)(2,1)S(1)}, u32[]{:S(2)}, u32[]{:S(2)}) async-start(bf16[64,8,384]{2,1,0:T(8,128)(2,1)} %bitcast.13), calls=%async_computation.4 | async-start | bytes 786432 | tf_op jit(solution)/shard_map/all_to_all | solution.py:214
  118.0 0.3 add_returned.1.partial
  118.3 16.3 %all-to-all-done.4 = bf16[64,8,384]{2,1,0:T(8,128)(2,1)S(1)} async-done(((bf16[64,8,384]{2,1,0:T(8,128)(2,1)}), bf16[64,8,384]{2,1,0:T(8,128)(2,1)S(1)}, u32[]{:S(2)}, u32[]{:S(2)}) %all-to-all-start.4) | async-done | bytes 393248 | tf_op jit(solution)/shard_map/all_to_all | solution.py:214
  134.6 0.0 copy-done.12
  134.6 1.4 %finish.1 = (f32[256,256]{1,0:T(8,128)}, f32[256,256]{1,0:T(8,128)}, bf16[256,256]{1,0:T(8,128)(2,1)}) custom-call(s32[1,4]{1,0:T(1,128)S(1)} %copy-done.12, bf16[512,384]{1,0:T(8,128)(2,1)S(1)} %bitcast.22, f32[256,256]{1,0:T(8,128)S(1)} %add_returned.1.partial), custom_call_target="tpu_custom_call" | custom-call | flops 262144 | bytes 1048576 | tf_op jit(solution)/shard_map/finish/pallas_call | solution.py:47
  (2 shorter events, 0.0 us)
Async XLA Ops:
  0.6 0.9 copy-start.3
  1.5 0.7 copy-start.11
  2.2 0.7 copy-start.14
  2.9 0.7 copy-start.15
  4.6 50.9 %copy-start.16 = (bf16[1024,256]{1,0:T(8,128)(2,1)}, bf16[1024,256]{1,0:T(8,128)(2,1)S(1)}, u32[]{:S(2)}) copy-start(bf16[1024,256]{1,0:T(8,128)(2,1)S(1)} %get-tuple-element.18.pick) | copy-start | bytes 1572868
  4.7 52.8 %copy-start.13 = (s32[256,10]{0,1:T(8,128)S(1)}, s32[256,10]{0,1:T(8,128)}, u32[]{:S(2)}) copy-start(s32[256,10]{0,1:T(8,128)} %param.9) | copy-start | bytes 30724
  55.5 9.7 %collective-permute-start = (bf16[1024,256]{1,0:T(8,128)(2,1)S(1)}, bf16[1024,256]{1,0:T(8,128)(2,1)}, u32[]{:S(2)}, u32[]{:S(2)}) collective-permute-start(bf16[1024,256]{1,0:T(8,128)(2,1)S(1)} %bitcast.20), channel_id=1, source_target_pairs={{0,64},{64,0},{1,65},{65,1},{2,66},{66,2},{3,67},{67,3},{4,68},{68... | collective-permute-start | bytes 1572872 | tf_op jit(solution)/shard_map/ppermute | solution.py:235
  57.5 0.9 copy-start.4
  58.4 0.9 copy-start.7
  59.3 1.0 copy-start.17
  60.3 4.9 %copy-start.5 = (bf16[256,256]{1,0:T(8,128)(2,1)S(1)}, bf16[256,256]{1,0:T(8,128)(2,1)}, u32[]{:S(2)}) copy-start(bf16[256,256]{1,0:T(8,128)(2,1)} %w_nbr.1) | copy-start | bytes 393220
  60.3 5.0 %copy-start.6 = (bf16[256,256]{1,0:T(8,128)(2,1)S(1)}, bf16[256,256]{1,0:T(8,128)(2,1)}, u32[]{:S(2)}) copy-start(bf16[256,256]{1,0:T(8,128)(2,1)} %cotangent.1) | copy-start | bytes 393220
  68.0 0.9 copy-start
  68.9 0.7 copy-start.1
  69.6 0.7 copy-start.9
  70.2 10.6 %copy-start.8 = (bf16[256,256]{1,0:T(8,128)(2,1)S(1)}, bf16[256,256]{1,0:T(8,128)(2,1)}, u32[]{:S(2)}) copy-start(bf16[256,256]{1,0:T(8,128)(2,1)} %w_self.3) | copy-start | bytes 393220
  70.3 32.2 %all-to-all-start.2 = ((bf16[64,8,768]{2,1,0:T(8,128)(2,1)}), bf16[64,8,768]{2,1,0:T(8,128)(2,1)S(1)}, u32[]{:S(2)}, u32[]{:S(2)}) async-start(bf16[64,8,768]{2,1,0:T(8,128)(2,1)} %bitcast.23), calls=%async_computation.2 | async-start | bytes 1572864 | tf_op jit(solution)/shard_map/all_to_all | solution.py:214
  76.9 0.9 copy-start.2
  78.9 4.1 %collective-permute-start.1 = (bf16[1024,256]{1,0:T(8,128)(2,1)}, bf16[1024,256]{1,0:T(8,128)(2,1)}, u32[]{:S(2)}, u32[]{:S(2)}) collective-permute-start(bf16[1024,256]{1,0:T(8,128)(2,1)} %other_hubs.1), channel_id=1, source_target_pairs={{0,64},{64,0},{1,65},{65,1},{2,66},{66,2},{3,67},{67,3},{4,68},{68... | collective-permute-start | bytes 1572872 | tf_op jit(solution)/shard_map/ppermute | solution.py:243
  80.8 0.9 copy-start.10
  84.2 22.3 %collective-permute-start.2 = (bf16[256,256]{1,0:T(8,128)(2,1)S(1)}, bf16[256,256]{1,0:T(8,128)(2,1)S(1)}, u32[]{:S(2)}, u32[]{:S(2)}) collective-permute-start(bf16[256,256]{1,0:T(8,128)(2,1)S(1)} %get-tuple-element.28), channel_id=1, source_target_pairs={{0,128},{128,256},{256,384},{384,0},{1,129},{129,257},{257,385},{3... | collective-permute-start | bytes 393224 | tf_op jit(solution)/shard_map/ppermute | solution.py:249
  86.7 19.8 %collective-permute-start.3 = (bf16[256,256]{1,0:T(8,128)(2,1)S(1)}, bf16[256,256]{1,0:T(8,128)(2,1)S(1)}, u32[]{:S(2)}, u32[]{:S(2)}) collective-permute-start(bf16[256,256]{1,0:T(8,128)(2,1)S(1)} %get-tuple-element.29), channel_id=1, source_target_pairs={{0,256},{128,384},{256,0},{384,128},{1,257},{129,385},{257,1},{385... | collective-permute-start | bytes 393224 | tf_op jit(solution)/shard_map/ppermute | solution.py:249
  90.7 15.9 %collective-permute-start.4 = (bf16[256,256]{1,0:T(8,128)(2,1)S(1)}, bf16[256,256]{1,0:T(8,128)(2,1)S(1)}, u32[]{:S(2)}, u32[]{:S(2)}) collective-permute-start(bf16[256,256]{1,0:T(8,128)(2,1)S(1)} %get-tuple-element.30), channel_id=1, source_target_pairs={{0,384},{128,0},{256,128},{384,256},{1,385},{129,1},{257,129},{385... | collective-permute-start | bytes 393224 | tf_op jit(solution)/shard_map/ppermute | solution.py:249
  103.1 8.7 %all-to-all-start.3 = ((bf16[8,8,256]{2,1,0:T(8,128)(2,1)}), bf16[8,8,256]{2,1,0:T(8,128)(2,1)S(1)}, u32[]{:S(2)}, u32[]{:S(2)}) async-start(bf16[8,8,256]{2,1,0:T(8,128)(2,1)} %bitcast.10), calls=%async_computation.3 | async-start | bytes 65536 | tf_op jit(solution)/shard_map/all_to_all | solution.py:214
  106.6 28.0 %copy-start.12 = (s32[1,4]{1,0:T(1,128)S(1)}, s32[1,4]{1,0:T(1,128)}, u32[]{:S(2)}) copy-start(s32[1,4]{1,0:T(1,128)} %hub.3) | copy-start | bytes 52
  112.6 21.9 %all-to-all-start.4 = ((bf16[64,8,384]{2,1,0:T(8,128)(2,1)}), bf16[64,8,384]{2,1,0:T(8,128)(2,1)S(1)}, u32[]{:S(2)}, u32[]{:S(2)}) async-start(bf16[64,8,384]{2,1,0:T(8,128)(2,1)} %bitcast.13), calls=%async_computation.4 | async-start | bytes 786432 | tf_op jit(solution)/shard_map/all_to_all | solution.py:214

commit v3 on v2

v3 whole, which is shorter than its diff:
```python
import math

import jax
import jax.numpy as jnp
from jax import lax
from jax.experimental import pallas as pl
from jax.experimental.pallas import tpu as pltpu
from jax.sharding import Mesh, PartitionSpec as P

BF = jnp.bfloat16
F32 = jnp.float32
I32 = jnp.int32
GROUP = ("x", "core")
MEMBER = ("y", "z")
ALL = ("x", "core", "y", "z")

D = 256
NODES = 256
FAN = 10
MEMBERS = 64
SLOTS = 16
HUBS = 4
GROUPS = 8
XS = 4
HALF = MEMBERS * 8
BORDER = NODES + 2 * HALF
SIDE = XS * MEMBERS * HUBS
TABLE = BORDER + 2 * SIDE
SCALE = 1.0 / math.sqrt(NODES * GROUPS * MEMBERS)
OVER_ROWS = (((0,), (0,)), ((), ()))
OVER_COLS = (((1,), (1,)), ((), ()))

VMEM = pl.BlockSpec(memory_space=pltpu.VMEM)
SMEM = pl.BlockSpec(memory_space=pltpu.SMEM)
HBM = pl.BlockSpec(memory_space=pltpu.HBM)
ANY = pl.BlockSpec(memory_space=pl.ANY)


def iota(shape, dim):
    return lax.broadcasted_iota(I32, shape, dim)


def dot(a, b):
    return jnp.dot(a, b, preferred_element_type=F32)


def call(body, name, outs, flops, moved, *args, kept=(), smem=(), unread=(), to_hbm=(), scratch=()):
    places = [HBM if i in kept else SMEM if i in smem else ANY if i in unread else VMEM for i in range(len(args))]
    return pl.pallas_call(
        body,
        name=name,
        out_shape=[(pltpu.HBM if i in to_hbm else jax.ShapeDtypeStruct)(s, t) for i, (s, t) in enumerate(outs)],
        in_specs=places,
        out_specs=[HBM if i in to_hbm else VMEM for i in range(len(outs))],
        scratch_shapes=list(scratch),
        compiler_params=pltpu.CompilerParams(vmem_limit_bytes=40 * 1024 * 1024),
        cost_estimate=pl.CostEstimate(flops=flops, bytes_accessed=moved, transcendentals=0),
    )(*[pltpu.with_memory_space_constraint(a, pltpu.HBM) if i in kept else a for i, a in enumerate(args)])


def send(sources, targets, sems, first=0):
    copies = [pltpu.make_async_copy(a, b, sems.at[first + i]) for i, (a, b) in enumerate(zip(sources, targets))]
    for copy in copies:
        copy.start()
    return copies


def finished(copies):
    for copy in copies:
        copy.wait()


def split_rows(rows):
    left = rows[:, :128].reshape(-1, 8, 128)
    right = rows[:, 128:].reshape(-1, 8, 128)
    low = iota(left.shape, 1) < 4
    even = jnp.where(low, left, pltpu.roll(right, 4, 1))
    odd = jnp.where(low, pltpu.roll(left, 4, 1), right)
    return jnp.stack([even, odd], axis=1).reshape(-1, 8, 128)


def join_rows(tiles):
    pairs = tiles.reshape(-1, 2, 8, 128)
    even, odd = pairs[:, 0], pairs[:, 1]
    low = iota(even.shape, 1) < 4
    left = jnp.where(low, even, pltpu.roll(odd, 4, 1)).reshape(-1, 128)
    right = jnp.where(low, pltpu.roll(even, 4, 1), odd).reshape(-1, 128)
    return left, right


def hot_rows(send_t, count):
    own = (iota((HALF, MEMBERS), 0) >> 3) == iota((HALF, MEMBERS), 1)
    spread = lax.dot_general(
        own.astype(F32).astype(BF), send_t.astype(F32).astype(BF), OVER_COLS, preferred_element_type=F32
    )
    live = jnp.sum(jnp.where(own, count.astype(F32), 0.0), axis=1, keepdims=True)
    lane = iota((HALF, SLOTS), 1)
    slot = iota((HALF, SLOTS), 0) & 7
    place = (iota((HALF, 1), 0) & 7).astype(F32)
    nodes = iota((HALF, NODES), 1).astype(F32)
    hot = []
    for a in range(2):
        row = jnp.sum(jnp.where(lane == slot + 8 * a, spread, 0.0), axis=1, keepdims=True)
        row = jnp.where(place + 8.0 * a < live, row, -1.0)
        hot.append((nodes == row).astype(F32).astype(BF))
    return hot


def hub_ids(hub, shape, h):
    return jnp.broadcast_to(jnp.sum(jnp.where(iota(hub.shape, 1) == h, hub, 0), axis=1, keepdims=True), shape)


def outgoing_rows(hub, send_t, count, features, out, hub_v, send_v, count_v, f_v, out_v, sems):
    copies = send((hub, send_t, count, features), (hub_v, send_v, count_v, f_v), sems)
    finished(copies)
    f = f_v[...]
    which = iota((16, NODES), 0) & 3
    ids = jnp.full((16, NODES), -1, I32)
    for h in range(HUBS):
        ids = jnp.where(which == h, hub_ids(hub_v[...], ids.shape, h), ids)
    rows = dot((ids == iota((16, NODES), 1)).astype(F32).astype(BF), f)
    tile = jnp.where(iota((8, 128), 0) < 4, rows[:8, :128], rows[:8, 128:])
    out_v[:, 2 * D :] = jnp.broadcast_to(tile[None], (MEMBERS, 8, 128)).reshape(HALF, 128).astype(BF)
    lanes = [slice(2 * D, 2 * D + 128), slice(0, D), slice(D, 2 * D)]
    copies = send([out_v.at[:, lanes[0]]], [out.at[:, lanes[0]]], sems, 4)
    for a, hot in enumerate(hot_rows(send_v[...], count_v[...])):
        out_v[:, lanes[a + 1]] = dot(hot, f).astype(BF)
        copies += send([out_v.at[:, lanes[a + 1]]], [out.at[:, lanes[a + 1]]], sems, 5 + a)
    finished(copies)


def table_row(n, core):
    b = n - NODES
    h = b - MEMBERS * SLOTS
    border = NODES + ((b >> 3) & 1) * HALF + (b >> 4) * 8 + (b & 7)
    side = ((h >> 8) & 1) ^ core
    hub = BORDER + side * SIDE + (h >> 9) * 256 + (h & 255)
    return jnp.where(b < 0, n, jnp.where(h < 0, border, hub))


def count_rows(core, near_t, send_t, count, features, w_self, after, counts, counts_t, home, pre_self):
    row_t = table_row(near_t[...], core[0])
    step = 32

    @pl.loop(0, TABLE // step)
    def _(i):
        base = pl.multiple_of(i * step, step)
        ids = iota((step, NODES), 0) + base
        total = jnp.zeros((step, NODES), F32)
        for f in range(FAN):
            total = total + jnp.where(ids == row_t[f : f + 1, :], 1.0, 0.0)
        counts_t[pl.ds(base, step), :] = total.astype(BF)

    eye = (iota((NODES, NODES), 0) == iota((NODES, NODES), 1)).astype(F32).astype(BF)
    for t in range(TABLE // 256):
        block = lax.dot_general(eye, counts_t[t * 256 : (t + 1) * 256, :], OVER_COLS, preferred_element_type=F32)
        counts[:, t * 256 : (t + 1) * 256] = block.astype(BF)
    for a, hot in enumerate(hot_rows(send_t[...], count[...])):
        block = lax.dot_general(eye, hot, OVER_COLS, preferred_element_type=F32)
        home[:, a * HALF : (a + 1) * HALF] = block.astype(BF)
    pre_self[...] = dot(features[...], w_self[...])


def own_hubs(incoming, after, out):
    left, right = join_rows(incoming[:, 2 * D :].astype(F32).reshape(MEMBERS, 8, 128))
    left, right = left.astype(BF), right.astype(BF)
    for x in range(XS):
        out[x * 256 : (x + 1) * 256, :128] = left
        out[x * 256 : (x + 1) * 256, 128:] = right


def forward(
    counts, counts_t, features, incoming, mine, other, pre_self, w_nbr, cotangent, w_self,
    outward, theirs, hubs, own, out_v, theirs_v, hubs_v, own_v, sems,
):
    f = features[...]
    total = dot(counts[:, :NODES], f)
    total += dot(counts[:, NODES : NODES + HALF], incoming[:, :D])
    total += dot(counts[:, NODES + HALF : BORDER], incoming[:, D : 2 * D])
    total += dot(counts[:, BORDER : BORDER + SIDE], mine[...])
    total += dot(counts[:, BORDER + SIDE :], other[...])
    agg = (total / FAN).astype(BF)
    pre = pre_self[...] + dot(agg, w_nbr[...])
    sigma = 1.0 / (1.0 + jnp.exp(-pre))
    dpre = (cotangent[...].astype(F32) * sigma * (1.0 + pre * (1.0 - sigma))).astype(BF)
    dagg = (lax.dot_general(dpre, w_nbr[...], OVER_COLS, preferred_element_type=F32) / FAN).astype(BF)

    out_v[:, :D] = dot(counts_t[NODES : NODES + HALF, :], dagg).astype(BF)
    out_v[:, D : 2 * D] = dot(counts_t[NODES + HALF : BORDER, :], dagg).astype(BF)
    copies = send([out_v.at[:, : 2 * D]], [outward.at[:, : 2 * D]], sems)
    out_v[:D, 2 * D :] = lax.dot_general(f, dpre, OVER_ROWS, preferred_element_type=F32).astype(BF)
    out_v[D:, 2 * D :] = lax.dot_general(agg, dpre, OVER_ROWS, preferred_element_type=F32).astype(BF)
    copies += send([out_v.at[:, 2 * D :]], [outward.at[:, 2 * D :]], sems, 1)
    theirs_v[...] = dot(counts_t[BORDER + SIDE :, :], dagg).astype(BF)
    copies += send([theirs_v], [theirs], sems, 2)
    hubs_v[...] = dot(counts_t[BORDER : BORDER + SIDE, :], dagg).astype(BF)
    own_v[...] = dot(counts_t[:NODES, :], dagg) + lax.dot_general(
        dpre, w_self[...], OVER_COLS, preferred_element_type=F32
    )
    copies += send([hubs_v, own_v], [hubs, own], sems, 3)
    finished(copies)


def pair_hubs(x, hubs, met, kept, *to):
    for k, out in enumerate((kept,) + to):
        place = lax.rem(x[0] + k, XS)
        rows = pl.ds(pl.multiple_of(place * 256, 256), 256)
        out[...] = (hubs[rows, :].astype(F32) + met[rows, :].astype(F32)).astype(BF)


def sum_hubs(kept, a, b, c, out):
    total = kept[...].astype(F32) + a[...].astype(F32) + b[...].astype(F32) + c[...].astype(F32)
    out[...] = split_rows(total).reshape(HALF, 128).astype(BF)


def sum_weights(returned, out):
    total = jnp.sum(returned[:, 2 * D :].astype(F32).reshape(MEMBERS, 8, D), axis=0)
    out[...] = jnp.broadcast_to(total[None], (GROUPS, 8, D)).reshape(GROUPS * 8, D).astype(BF)


def add_returned(returned, home, own, out):
    total = own[...] + dot(home[:, :HALF], returned[:, :D])
    out[...] = total + dot(home[:, HALF:], returned[:, D : 2 * D])


def last_message(weights, hubs, out):
    total = jnp.sum(weights[...].astype(F32).reshape(GROUPS, 8, D), axis=0) * SCALE
    out[:, :D] = jnp.broadcast_to(total[None], (MEMBERS, 8, D)).reshape(HALF, D).astype(BF)
    out[:, D:] = hubs[...]


def finish(hub, last, partial, grad_self, grad_nbr, grad, weights_v, grad_v, sems):
    weights_v[...] = last[:, :D].astype(F32)
    copies = send([weights_v.at[:D, :], weights_v.at[D:, :]], [grad_self, grad_nbr], sems)
    tile = jnp.sum(last[:, D:].astype(F32).reshape(MEMBERS, 8, 128), axis=0)
    total = partial[...]
    node = iota((NODES, D), 0)
    for h in range(HUBS):
        row = jnp.concatenate([tile[h : h + 1], tile[h + 4 : h + 5]], axis=1)
        total = total + jnp.where(node == hub_ids(hub[...], (NODES, D), h), row, 0.0)
    grad_v[...] = total.astype(BF)
    copies += send([grad_v], [grad], sems, 2)
    finished(copies)


def exchange(array, axes, parts):
    block = array.reshape(parts, -1, array.shape[1])
    return lax.all_to_all(block, axes, split_axis=0, concat_axis=0, tiled=True).reshape(array.shape)


def local(features, neighbours, send_rows, block_counts, hub_rows, w_self, w_nbr, cotangent):
    core = lax.axis_index("core").reshape(1)
    x = lax.axis_index("x").reshape(1)
    send_t = send_rows.T
    live = block_counts.reshape(1, MEMBERS)
    side = ((SIDE, D), BF)
    (outgoing,) = call(
        outgoing_rows, "outgoing_rows", [((HALF, 640), BF)], 2**27, 2**20,
        hub_rows, send_t, live, features,
        kept=range(4), to_hbm=(0,),
        scratch=[
            pltpu.VMEM((1, HUBS), I32), pltpu.VMEM((SLOTS, MEMBERS), I32), pltpu.VMEM((1, MEMBERS), I32),
            pltpu.VMEM((NODES, D), BF), pltpu.VMEM((HALF, 640), BF), pltpu.SemaphoreType.DMA((7,)),
        ],
    )
    incoming = exchange(outgoing, MEMBER, MEMBERS)
    counts, counts_t, home, pre_self = call(
        count_rows, "count_rows",
        [((NODES, TABLE), BF), ((TABLE, NODES), BF), ((NODES, 2 * HALF), BF), ((NODES, D), F32)], 2**30, 2**22,
        core, neighbours.T, send_t, live, features, w_self, outgoing,
        smem=(0,), unread=(6,),
    )
    (mine,) = call(own_hubs, "own_hubs", [side], 2**16, 2**19, incoming, pre_self, unread=(1,))
    mine = exchange(mine, "x", XS)
    swap = [(0, 1), (1, 0)]
    other = lax.ppermute(mine, "core", swap)
    outward, theirs, hubs, own = call(
        forward, "forward", [((HALF, 768), BF), side, side, ((NODES, D), F32)], 2**30, 2**23,
        counts, counts_t, features, incoming, mine, other, pre_self, w_nbr, cotangent, w_self,
        to_hbm=range(4),
        scratch=[
            pltpu.VMEM((HALF, 768), BF), pltpu.VMEM((SIDE, D), BF), pltpu.VMEM((SIDE, D), BF),
            pltpu.VMEM((NODES, D), F32), pltpu.SemaphoreType.DMA((5,)),
        ],
    )
    returned = exchange(outward, MEMBER, MEMBERS)

    met = lax.ppermute(theirs, "core", swap)
    block = ((NODES, D), BF)
    kept, *to = call(pair_hubs, "pair_hubs", [block] * XS, 2**18, 2**20, x, hubs, met, smem=(0,))
    came = [lax.ppermute(to[k - 1], "x", [(i, (i + k) % XS) for i in range(XS)]) for k in range(1, XS)]
    (hub_tiles,) = call(sum_hubs, "sum_hubs", [((HALF, 128), BF)], 2**18, 2**20, kept, *came)

    (weights,) = call(sum_weights, "sum_weights", [((GROUPS * 8, D), BF)], 2**17, 2**18, returned)
    weights = exchange(weights, GROUP, GROUPS)
    (partial,) = call(add_returned, "add_returned", [((NODES, D), F32)], 2**27, 2**20, returned, home, own)
    (message,) = call(last_message, "last_message", [((HALF, 384), BF)], 2**17, 2**18, weights, hub_tiles)
    last = exchange(message, MEMBER, MEMBERS)
    return tuple(
        call(
            finish, "finish", [((D, D), F32), ((D, D), F32), ((NODES, D), BF)], 2**18, 2**20, hub_rows, last, partial,
            to_hbm=range(3),
            scratch=[pltpu.VMEM((2 * D, D), F32), pltpu.VMEM((NODES, D), BF), pltpu.SemaphoreType.DMA((3,))],
        )
    )


def solution(mesh):
    split = Mesh(mesh.devices.reshape(XS, 2, 8, 8), ALL)
    rows = P(ALL, None)
    in_specs = (rows, rows, rows, P(ALL), rows, P(), P(), rows)
    out_specs = (P(), P(), rows)
    return jax.shard_map(local, mesh=split, in_specs=in_specs, out_specs=out_specs, check_vma=False)
```

time: 137 us -> 127 us (0.927)
  blocking collectives: 50.8 us -> 12.3 us
  waiting for transfers between devices: 31.5 us -> 51.7 us
  starting transfers between devices: 28.3 us -> 45 us
  local copies, waits for them, and re-layouts: 9.78 us -> 2.34 us
    all_to_all x2 -> x1, blocking collectives: 50.8 us -> 12.3 us  [exchange(): lax.all_to_all(block, axes, split_axis=0, concat_axis=0, tiled=True)]
    all_to_all x3 -> x4, waiting for transfers between devices: 30.6 us -> 47.8 us  [exchange(): lax.all_to_all(block, axes, split_axis=0, concat_axis=0, tiled=True)]
    all_to_all x3 -> x4, starting transfers between devices: 15.3 us -> 31.9 us  [exchange(): lax.all_to_all(block, axes, split_axis=0, concat_axis=0, tiled=True)]
    unnamed x36 -> x26, local copies, waits for them, and re-layouts: 9.78 us -> 2.34 us
    ppermute x1, waiting for transfers between devices: 0.01 us -> 1.88 us  [local(): other = lax.ppermute(mine, 'core', swap)]
    pallas_call x12 -> x10, Pallas kernels: 14.7 us -> 14 us  [call(): pl.pallas_call(body, name=name, out_shape=[(pltpu.HBM if i in to_hbm else...]
  transfers between devices with their start and end apart: 8 -> 9, of which waited for: 4 -> 6; matrix products, arithmetic and copies ran while one was open for 0% -> 0% of each run, Pallas kernels for 6% -> 5%
where the time goes in v3:
time: 127 us; the launch traced here: 126 us
  waiting for transfers between devices  51.7 us (41%)
  starting transfers between devices  45 us (35%)
  Pallas kernels  14 us (11%)
  blocking collectives  12.3 us (10%)
  local copies, waits for them, and re-layouts  2.34 us (2%)
    all_to_all x4, waiting for transfers between devices, exchange(): lax.all_to_all(block, axes, split_axis=0, concat_axis=0, tiled=True)  47.8 us
    all_to_all x4, starting transfers between devices, exchange(): lax.all_to_all(block, axes, split_axis=0, concat_axis=0, tiled=True)  31.9 us
    pallas_call x10, Pallas kernels, call(): pl.pallas_call(body, name=name, out_shape=[(pltpu.HBM if i in to_hbm else...  14 us
    all_to_all x1, blocking collectives, exchange(): lax.all_to_all(block, axes, split_axis=0, concat_axis=0, tiled=True)  12.3 us
    ppermute x3, starting transfers between devices, local(): lax.ppermute(to[k - 1], 'x', [(i, (i + k) % XS) for i in range(XS)])  9.31 us
  transfers between devices with their start and end apart: 9, of which 6 were waited for; matrix products, arithmetic and copies ran while one was open for 0% of the time, Pallas kernels for 5%

profile of v3, /device:TPU:16, one launch (start us, length us, event | category | flops | bytes accessed | tf_op | source)
XLA Modules:
  0.0 126.3 jit_solution(7988068842817818141)
XLA Ops:
  0.6 0.0 copy-start.3
  0.6 0.0 copy-start.11
  0.7 0.0 copy-start.9
  0.7 0.0 copy-start.6
  0.7 0.0 copy-start.12
  0.7 2.4 %outgoing_rows.1.after = bf16[512,640]{1,0:T(8,128)(2,1)} custom-call(s32[1,4]{1,0:T(1,128)} %hub.3, s32[16,64]{1,0:T(8,128)} %bitcast.25, s32[1,64]{1,0:T(1,128)} %bitcast.27, bf16[256,256]{1,0:T(8,128)(2,1)} %features.5), custom_call_target="tpu_custom_call" | custom-call | flops 134217728 | bytes 1048576 | tf_op jit(solution)/shard_map/outgoing_rows/pallas_call | solution.py:49
  3.1 16.5 %all-to-all-start = ((bf16[64,8,640]{2,1,0:T(8,128)(2,1)}), bf16[64,8,640]{2,1,0:T(8,128)(2,1)S(1)}, u32[]{:S(2)}, u32[]{:S(2)}) async-start(bf16[64,8,640]{2,1,0:T(8,128)(2,1)} %bitcast.19), calls=%async_computation | async-start | bytes 1310720 | tf_op jit(solution)/shard_map/all_to_all | solution.py:248
  19.6 0.0 copy-done.3
  19.6 0.0 copy-done.11
  19.6 0.0 copy-done.9
  19.7 0.0 copy-done.6
  19.7 0.0 copy-done.12
  19.7 0.0 copy-start
  19.7 1.1 copy-done
  20.8 5.2 %count_rows.1 = (bf16[256,3328]{1,0:T(8,128)(2,1)S(1)}, bf16[3328,256]{1,0:T(8,128)(2,1)S(1)}, bf16[256,1024]{1,0:T(8,128)(2,1)S(1)}, f32[256,256]{1,0:T(8,128)S(1)}) custom-call(s32[1]{0:T(128)} %bitcast.core, s32[10,256]{1,0:T(8,128)S(1)} %bitcast.29, s32[16,64]{1,0:T(8,128)S(1)} %bitcast.26, s32[1,64]{1,0:T(1,128)S(1)} %bitcast.28, ...), custom_call_target="tpu_custom_call" | custom-call | flops 1073741824 | bytes 4194304 | tf_op jit(solution)/shard_map/count_rows/pallas_call | solution.py:49
  26.0 0.0 copy-start.1
  26.0 1.2 copy-done.1
  27.2 0.0 copy-start.7
  27.2 14.6 %all-to-all-done = bf16[64,8,640]{2,1,0:T(8,128)(2,1)S(1)} async-done(((bf16[64,8,640]{2,1,0:T(8,128)(2,1)}), bf16[64,8,640]{2,1,0:T(8,128)(2,1)S(1)}, u32[]{:S(2)}, u32[]{:S(2)}) %all-to-all-start) | async-done | bytes 655392 | tf_op jit(solution)/shard_map/all_to_all | solution.py:248
  41.8 0.0 copy-start.2
  41.8 0.0 copy-start.8
  41.8 0.1 own_hubs.1
  41.9 12.3 %all_to_all.25 = bf16[4,256,256]{2,1,0:T(8,128)(2,1)S(1)} all-to-all(bf16[4,256,256]{2,1,0:T(8,128)(2,1)S(1)} %bitcast.22), channel_id=1, replica_groups=mesh['x'=4,'core'=2,'y'=8,'z'=8] {'x'}, dimensions={0} | all-to-all | bytes 1048576 | tf_op jit(solution)/shard_map/all_to_all | solution.py:248
  54.2 1.9 %collective-permute-start = (bf16[1024,256]{1,0:T(8,128)(2,1)S(1)}, bf16[1024,256]{1,0:T(8,128)(2,1)S(1)}, u32[]{:S(2)}, u32[]{:S(2)}) collective-permute-start(bf16[1024,256]{1,0:T(8,128)(2,1)S(1)} %bitcast.20), channel_id=1, source_target_pairs={{0,64},{64,0},{1,65},{65,1},{2,66},{66,2},{3,67},{67,3},{4,68},{68... | collective-permute-start | bytes 1572872 | tf_op jit(solution)/shard_map/ppermute | solution.py:276
  56.1 1.9 %collective-permute-done.other = bf16[1024,256]{1,0:T(8,128)(2,1)S(1)} collective-permute-done((bf16[1024,256]{1,0:T(8,128)(2,1)S(1)}, bf16[1024,256]{1,0:T(8,128)(2,1)S(1)}, u32[]{:S(2)}, u32[]{:S(2)}) %collective-permute-start) | collective-permute-done | bytes 524320 | tf_op jit(solution)/shard_map/ppermute | solution.py:276
  58.0 0.0 copy-done.7
  58.0 0.0 copy-done.2
  58.0 0.0 copy-done.8
  58.0 3.4 %forward.1 = (bf16[512,768]{1,0:T(8,128)(2,1)}, bf16[1024,256]{1,0:T(8,128)(2,1)}, bf16[1024,256]{1,0:T(8,128)(2,1)}, f32[256,256]{1,0:T(8,128)}) custom-call(bf16[256,3328]{1,0:T(8,128)(2,1)S(1)} %get-tuple-element.15.counts, bf16[3328,256]{1,0:T(8,128)(2,1)S(1)} %copy-done.2, bf16[256,256]{1,0:T(8,128)(2,1)S(1)} %copy-done.3, ...), custom_call_target="tpu_custom_call" | custom-call | flops 1073741824 | bytes 8388608 | tf_op jit(solution)/shard_map/forward/pallas_call | solution.py:49
  61.4 0.0 copy-start.4
  61.4 6.6 %all-to-all-start.2 = ((bf16[64,8,768]{2,1,0:T(8,128)(2,1)}), bf16[64,8,768]{2,1,0:T(8,128)(2,1)S(1)}, u32[]{:S(2)}, u32[]{:S(2)}) async-start(bf16[64,8,768]{2,1,0:T(8,128)(2,1)} %bitcast.30), calls=%async_computation.2 | async-start | bytes 1572864 | tf_op jit(solution)/shard_map/all_to_all | solution.py:248
  68.1 1.9 %collective-permute-start.1 = (bf16[1024,256]{1,0:T(8,128)(2,1)}, bf16[1024,256]{1,0:T(8,128)(2,1)S(1)}, u32[]{:S(2)}, u32[]{:S(2)}) collective-permute-start(bf16[1024,256]{1,0:T(8,128)(2,1)} %get-tuple-element.20), channel_id=1, source_target_pairs={{0,64},{64,0},{1,65},{65,1},{2,66},{66,2},{3,67},{67,3},{4,68},{68... | collective-permute-start | bytes 1572872 | tf_op jit(solution)/shard_map/ppermute | solution.py:288
  70.0 2.1 %collective-permute-done.1.met = bf16[1024,256]{1,0:T(8,128)(2,1)S(1)} collective-permute-done((bf16[1024,256]{1,0:T(8,128)(2,1)}, bf16[1024,256]{1,0:T(8,128)(2,1)S(1)}, u32[]{:S(2)}, u32[]{:S(2)}) %collective-permute-start.1) | collective-permute-done | bytes 524320 | tf_op jit(solution)/shard_map/ppermute | solution.py:288
  72.1 0.0 copy-done.4
  72.1 0.1 pair_hubs.1
  72.2 0.0 copy-start.5
  72.2 2.6 %collective-permute-start.2 = (bf16[256,256]{1,0:T(8,128)(2,1)S(1)}, bf16[256,256]{1,0:T(8,128)(2,1)S(1)}, u32[]{:S(2)}, u32[]{:S(2)}) collective-permute-start(bf16[256,256]{1,0:T(8,128)(2,1)S(1)} %get-tuple-element.22), channel_id=1, source_target_pairs={{0,128},{128,256},{256,384},{384,0},{1,129},{129,257},{257,385},{3... | collective-permute-start | bytes 393224 | tf_op jit(solution)/shard_map/ppermute | solution.py:291
  74.8 4.0 %collective-permute-start.3 = (bf16[256,256]{1,0:T(8,128)(2,1)S(1)}, bf16[256,256]{1,0:T(8,128)(2,1)S(1)}, u32[]{:S(2)}, u32[]{:S(2)}) collective-permute-start(bf16[256,256]{1,0:T(8,128)(2,1)S(1)} %get-tuple-element.23), channel_id=1, source_target_pairs={{0,256},{128,384},{256,0},{384,128},{1,257},{129,385},{257,1},{385... | collective-permute-start | bytes 393224 | tf_op jit(solution)/shard_map/ppermute | solution.py:291
  78.8 2.7 %collective-permute-start.4 = (bf16[256,256]{1,0:T(8,128)(2,1)S(1)}, bf16[256,256]{1,0:T(8,128)(2,1)S(1)}, u32[]{:S(2)}, u32[]{:S(2)}) collective-permute-start(bf16[256,256]{1,0:T(8,128)(2,1)S(1)} %get-tuple-element.24), channel_id=1, source_target_pairs={{0,384},{128,0},{256,128},{384,256},{1,385},{129,1},{257,129},{385... | collective-permute-start | bytes 393224 | tf_op jit(solution)/shard_map/ppermute | solution.py:291
  81.5 11.7 %all-to-all-done.2 = bf16[64,8,768]{2,1,0:T(8,128)(2,1)S(1)} async-done(((bf16[64,8,768]{2,1,0:T(8,128)(2,1)}), bf16[64,8,768]{2,1,0:T(8,128)(2,1)S(1)}, u32[]{:S(2)}, u32[]{:S(2)}) %all-to-all-start.2) | async-done | bytes 786464 | tf_op jit(solution)/shard_map/all_to_all | solution.py:248
  93.2 0.7 sum_weights.1
  93.9 3.3 %all-to-all-start.3 = ((bf16[8,8,256]{2,1,0:T(8,128)(2,1)}), bf16[8,8,256]{2,1,0:T(8,128)(2,1)S(1)}, u32[]{:S(2)}, u32[]{:S(2)}) async-start(bf16[8,8,256]{2,1,0:T(8,128)(2,1)} %bitcast.10), calls=%async_computation.3 | async-start | bytes 65536 | tf_op jit(solution)/shard_map/all_to_all | solution.py:248
  97.2 0.0 collective-permute-done.2.a
  97.2 0.0 collective-permute-done.3.b
  97.3 0.0 collective-permute-done.4.c
  97.3 0.1 sum_hubs.1.hubs
  97.4 0.0 copy-start.10
  97.4 5.2 %all-to-all-done.3 = bf16[8,8,256]{2,1,0:T(8,128)(2,1)S(1)} async-done(((bf16[8,8,256]{2,1,0:T(8,128)(2,1)}), bf16[8,8,256]{2,1,0:T(8,128)(2,1)S(1)}, u32[]{:S(2)}, u32[]{:S(2)}) %all-to-all-start.3) | async-done | bytes 32800 | tf_op jit(solution)/shard_map/all_to_all | solution.py:248
  102.6 0.8 last_message.1
  103.4 5.4 %all-to-all-start.4 = ((bf16[64,8,384]{2,1,0:T(8,128)(2,1)}), bf16[64,8,384]{2,1,0:T(8,128)(2,1)S(1)}, u32[]{:S(2)}, u32[]{:S(2)}) async-start(bf16[64,8,384]{2,1,0:T(8,128)(2,1)} %bitcast.13), calls=%async_computation.4 | async-start | bytes 786432 | tf_op jit(solution)/shard_map/all_to_all | solution.py:248
  108.8 0.0 copy-done.5
  108.9 0.3 add_returned.1.partial
  109.2 16.3 %all-to-all-done.4 = bf16[64,8,384]{2,1,0:T(8,128)(2,1)S(1)} async-done(((bf16[64,8,384]{2,1,0:T(8,128)(2,1)}), bf16[64,8,384]{2,1,0:T(8,128)(2,1)S(1)}, u32[]{:S(2)}, u32[]{:S(2)}) %all-to-all-start.4) | async-done | bytes 393248 | tf_op jit(solution)/shard_map/all_to_all | solution.py:248
  125.4 0.0 copy-done.10
  125.4 0.9 finish.1
Async XLA Ops:
  0.6 19.0 %copy-start.3 = (bf16[256,256]{1,0:T(8,128)(2,1)S(1)}, bf16[256,256]{1,0:T(8,128)(2,1)}, u32[]{:S(2)}) copy-start(bf16[256,256]{1,0:T(8,128)(2,1)} %features.5) | copy-start | bytes 393220
  0.6 19.0 %copy-start.11 = (s32[64]{0:T(128)S(1)}, s32[64]{0:T(128)}, u32[]{:S(2)}) copy-start(s32[64]{0:T(128)} %param.11) | copy-start | bytes 772
  0.7 19.0 %copy-start.9 = (s32[64,16]{0,1:T(8,128)S(1)}, s32[64,16]{0,1:T(8,128)}, u32[]{:S(2)}) copy-start(s32[64,16]{0,1:T(8,128)} %param.10) | copy-start | bytes 12292
  0.7 19.0 %copy-start.6 = (bf16[256,256]{1,0:T(8,128)(2,1)S(1)}, bf16[256,256]{1,0:T(8,128)(2,1)}, u32[]{:S(2)}) copy-start(bf16[256,256]{1,0:T(8,128)(2,1)} %w_self.3) | copy-start | bytes 393220
  0.7 19.0 %copy-start.12 = (s32[256,10]{0,1:T(8,128)S(1)}, s32[256,10]{0,1:T(8,128)}, u32[]{:S(2)}) copy-start(s32[256,10]{0,1:T(8,128)} %param.9) | copy-start | bytes 30724
  3.1 38.7 %all-to-all-start = ((bf16[64,8,640]{2,1,0:T(8,128)(2,1)}), bf16[64,8,640]{2,1,0:T(8,128)(2,1)S(1)}, u32[]{:S(2)}, u32[]{:S(2)}) async-start(bf16[64,8,640]{2,1,0:T(8,128)(2,1)} %bitcast.19), calls=%async_computation | async-start | bytes 1310720 | tf_op jit(solution)/shard_map/all_to_all | solution.py:248
  19.7 1.1 copy-start
  26.0 1.2 copy-start.1
  27.2 30.8 %copy-start.7 = (bf16[256,256]{1,0:T(8,128)(2,1)S(1)}, bf16[256,256]{1,0:T(8,128)(2,1)}, u32[]{:S(2)}) copy-start(bf16[256,256]{1,0:T(8,128)(2,1)} %w_nbr.1) | copy-start | bytes 393220
  41.8 16.2 %copy-start.2 = (bf16[3328,256]{1,0:T(8,128)(2,1)S(1)}, bf16[3328,256]{1,0:T(8,128)(2,1)}, u32[]{:S(2)}) copy-start(bf16[3328,256]{1,0:T(8,128)(2,1)} %copy-done.1) | copy-start | bytes 5111812
  41.8 16.2 %copy-start.8 = (bf16[256,256]{1,0:T(8,128)(2,1)S(1)}, bf16[256,256]{1,0:T(8,128)(2,1)}, u32[]{:S(2)}) copy-start(bf16[256,256]{1,0:T(8,128)(2,1)} %cotangent.1) | copy-start | bytes 393220
  54.2 3.8 %collective-permute-start = (bf16[1024,256]{1,0:T(8,128)(2,1)S(1)}, bf16[1024,256]{1,0:T(8,128)(2,1)S(1)}, u32[]{:S(2)}, u32[]{:S(2)}) collective-permute-start(bf16[1024,256]{1,0:T(8,128)(2,1)S(1)} %bitcast.20), channel_id=1, source_target_pairs={{0,64},{64,0},{1,65},{65,1},{2,66},{66,2},{3,67},{67,3},{4,68},{68... | collective-permute-start | bytes 1572872 | tf_op jit(solution)/shard_map/ppermute | solution.py:276
  61.4 10.7 %copy-start.4 = (bf16[1024,256]{1,0:T(8,128)(2,1)S(1)}, bf16[1024,256]{1,0:T(8,128)(2,1)}, u32[]{:S(2)}) copy-start(bf16[1024,256]{1,0:T(8,128)(2,1)} %get-tuple-element.19.hubs) | copy-start | bytes 1572868
  61.4 31.8 %all-to-all-start.2 = ((bf16[64,8,768]{2,1,0:T(8,128)(2,1)}), bf16[64,8,768]{2,1,0:T(8,128)(2,1)S(1)}, u32[]{:S(2)}, u32[]{:S(2)}) async-start(bf16[64,8,768]{2,1,0:T(8,128)(2,1)} %bitcast.30), calls=%async_computation.2 | async-start | bytes 1572864 | tf_op jit(solution)/shard_map/all_to_all | solution.py:248
  68.1 4.0 %collective-permute-start.1 = (bf16[1024,256]{1,0:T(8,128)(2,1)}, bf16[1024,256]{1,0:T(8,128)(2,1)S(1)}, u32[]{:S(2)}, u32[]{:S(2)}) collective-permute-start(bf16[1024,256]{1,0:T(8,128)(2,1)} %get-tuple-element.20), channel_id=1, source_target_pairs={{0,64},{64,0},{1,65},{65,1},{2,66},{66,2},{3,67},{67,3},{4,68},{68... | collective-permute-start | bytes 1572872 | tf_op jit(solution)/shard_map/ppermute | solution.py:288
  72.2 36.6 %copy-start.5 = (f32[256,256]{1,0:T(8,128)S(1)}, f32[256,256]{1,0:T(8,128)}, u32[]{:S(2)}) copy-start(f32[256,256]{1,0:T(8,128)} %get-tuple-element.26.own) | copy-start | bytes 786436
  72.2 25.0 %collective-permute-start.2 = (bf16[256,256]{1,0:T(8,128)(2,1)S(1)}, bf16[256,256]{1,0:T(8,128)(2,1)S(1)}, u32[]{:S(2)}, u32[]{:S(2)}) collective-permute-start(bf16[256,256]{1,0:T(8,128)(2,1)S(1)} %get-tuple-element.22), channel_id=1, source_target_pairs={{0,128},{128,256},{256,384},{384,0},{1,129},{129,257},{257,385},{3... | collective-permute-start | bytes 393224 | tf_op jit(solution)/shard_map/ppermute | solution.py:291
  74.8 22.4 %collective-permute-start.3 = (bf16[256,256]{1,0:T(8,128)(2,1)S(1)}, bf16[256,256]{1,0:T(8,128)(2,1)S(1)}, u32[]{:S(2)}, u32[]{:S(2)}) collective-permute-start(bf16[256,256]{1,0:T(8,128)(2,1)S(1)} %get-tuple-element.23), channel_id=1, source_target_pairs={{0,256},{128,384},{256,0},{384,128},{1,257},{129,385},{257,1},{385... | collective-permute-start | bytes 393224 | tf_op jit(solution)/shard_map/ppermute | solution.py:291
  78.8 18.5 %collective-permute-start.4 = (bf16[256,256]{1,0:T(8,128)(2,1)S(1)}, bf16[256,256]{1,0:T(8,128)(2,1)S(1)}, u32[]{:S(2)}, u32[]{:S(2)}) collective-permute-start(bf16[256,256]{1,0:T(8,128)(2,1)S(1)} %get-tuple-element.24), channel_id=1, source_target_pairs={{0,384},{128,0},{256,128},{384,256},{1,385},{129,1},{257,129},{385... | collective-permute-start | bytes 393224 | tf_op jit(solution)/shard_map/ppermute | solution.py:291
  93.9 8.7 %all-to-all-start.3 = ((bf16[8,8,256]{2,1,0:T(8,128)(2,1)}), bf16[8,8,256]{2,1,0:T(8,128)(2,1)S(1)}, u32[]{:S(2)}, u32[]{:S(2)}) async-start(bf16[8,8,256]{2,1,0:T(8,128)(2,1)} %bitcast.10), calls=%async_computation.3 | async-start | bytes 65536 | tf_op jit(solution)/shard_map/all_to_all | solution.py:248
  97.4 28.1 %copy-start.10 = (s32[1,4]{1,0:T(1,128)S(1)}, s32[1,4]{1,0:T(1,128)}, u32[]{:S(2)}) copy-start(s32[1,4]{1,0:T(1,128)} %hub.3) | copy-start | bytes 52
  103.4 22.0 %all-to-all-start.4 = ((bf16[64,8,384]{2,1,0:T(8,128)(2,1)}), bf16[64,8,384]{2,1,0:T(8,128)(2,1)S(1)}, u32[]{:S(2)}, u32[]{:S(2)}) async-start(bf16[64,8,384]{2,1,0:T(8,128)(2,1)} %bitcast.13), calls=%async_computation.4 | async-start | bytes 786432 | tf_op jit(solution)/shard_map/all_to_all | solution.py:248

commit v4 on v3

--- a/solution.py
+++ b/solution.py
@@ -44,7 +44,7 @@
     return jnp.dot(a, b, preferred_element_type=F32)
 
 
-def call(body, name, outs, flops, moved, *args, kept=(), smem=(), unread=(), to_hbm=(), scratch=()):
+def call(body, name, outs, flops, moved, *args, kept=(), smem=(), unread=(), to_hbm=(), scratch=(), alias={}):
     places = [HBM if i in kept else SMEM if i in smem else ANY if i in unread else VMEM for i in range(len(args))]
     return pl.pallas_call(
         body,
@@ -53,7 +53,8 @@
         in_specs=places,
         out_specs=[HBM if i in to_hbm else VMEM for i in range(len(outs))],
         scratch_shapes=list(scratch),
-        compiler_params=pltpu.CompilerParams(vmem_limit_bytes=40 * 1024 * 1024),
+        input_output_aliases=alias,
+        compiler_params=pltpu.CompilerParams(vmem_limit_bytes=16 * 1024 * 1024),
         cost_estimate=pl.CostEstimate(flops=flops, bytes_accessed=moved, transcendentals=0),
     )(*[pltpu.with_memory_space_constraint(a, pltpu.HBM) if i in kept else a for i, a in enumerate(args)])
 
@@ -111,8 +112,10 @@
 
 
 def outgoing_rows(hub, send_t, count, features, out, hub_v, send_v, count_v, f_v, out_v, sems):
-    copies = send((hub, send_t, count, features), (hub_v, send_v, count_v, f_v), sems)
-    finished(copies)
+    copies = send((send_t, count, hub, features), (send_v, count_v, hub_v, f_v), sems)
+    finished(copies[:2])
+    hot = hot_rows(send_v[...], count_v[...])
+    finished(copies[2:])
     f = f_v[...]
     which = iota((16, NODES), 0) & 3
     ids = jnp.full((16, NODES), -1, I32)
@@ -121,11 +124,11 @@
     rows = dot((ids == iota((16, NODES), 1)).astype(F32).astype(BF), f)
     tile = jnp.where(iota((8, 128), 0) < 4, rows[:8, :128], rows[:8, 128:])
     out_v[:, 2 * D :] = jnp.broadcast_to(tile[None], (MEMBERS, 8, 128)).reshape(HALF, 128).astype(BF)
-    lanes = [slice(2 * D, 2 * D + 128), slice(0, D), slice(D, 2 * D)]
-    copies = send([out_v.at[:, lanes[0]]], [out.at[:, lanes[0]]], sems, 4)
-    for a, hot in enumerate(hot_rows(send_v[...], count_v[...])):
-        out_v[:, lanes[a + 1]] = dot(hot, f).astype(BF)
-        copies += send([out_v.at[:, lanes[a + 1]]], [out.at[:, lanes[a + 1]]], sems, 5 + a)
+    copies = send([out_v.at[:, 2 * D :]], [out.at[:, 2 * D :]], sems, 4)
+    for a in range(2):
+        lanes = slice(a * D, (a + 1) * D)
+        out_v[:, lanes] = dot(hot[a], f).astype(BF)
+        copies += send([out_v.at[:, lanes]], [out.at[:, lanes]], sems, 5 + a)
     finished(copies)
 
 
@@ -138,7 +141,7 @@
     return jnp.where(b < 0, n, jnp.where(h < 0, border, hub))
 
 
-def count_rows(core, near_t, send_t, count, features, w_self, after, counts, counts_t, home, pre_self):
+def count_rows(core, near_t, send_t, count, features, w_self, after, counts, counts_t, home, pre_self, done):
     row_t = table_row(near_t[...], core[0])
     step = 32
 
@@ -159,46 +162,56 @@
         block = lax.dot_general(eye, hot, OVER_COLS, preferred_element_type=F32)
         home[:, a * HALF : (a + 1) * HALF] = block.astype(BF)
     pre_self[...] = dot(features[...], w_self[...])
-
-
-def own_hubs(incoming, after, out):
-    left, right = join_rows(incoming[:, 2 * D :].astype(F32).reshape(MEMBERS, 8, 128))
+    done[...] = jnp.zeros((8, 128), F32)
+
+
+def own_hubs(incoming, after, out, tiles, sems):
+    finished(send([incoming.at[:, 2 * D :]], [tiles], sems))
+    left, right = join_rows(tiles[...].astype(F32).reshape(MEMBERS, 8, 128))
     left, right = left.astype(BF), right.astype(BF)
     for x in range(XS):
         out[x * 256 : (x + 1) * 256, :128] = left
         out[x * 256 : (x + 1) * 256, 128:] = right
 
 
-def forward(
-    counts, counts_t, features, incoming, mine, other, pre_self, w_nbr, cotangent, w_self,
-    outward, theirs, hubs, own, out_v, theirs_v, hubs_v, own_v, sems,
-):
-    f = features[...]
-    total = dot(counts[:, :NODES], f)
+def near_sum(counts, features, incoming, mine, out):
+    total = dot(counts[:, :NODES], features[...])
     total += dot(counts[:, NODES : NODES + HALF], incoming[:, :D])
     total += dot(counts[:, NODES + HALF : BORDER], incoming[:, D : 2 * D])
-    total += dot(counts[:, BORDER : BORDER + SIDE], mine[...])
-    total += dot(counts[:, BORDER + SIDE :], other[...])
+    out[...] = total + dot(counts[:, BORDER : BORDER + SIDE], mine[...])
+
+
+def forward(
+    counts, counts_t, features, near, other, pre_self, w_nbr, cotangent, outward, both, out_v, both_v, sems
+):
+    total = near[...] + dot(counts[:, BORDER + SIDE :], other[...])
     agg = (total / FAN).astype(BF)
     pre = pre_self[...] + dot(agg, w_nbr[...])
     sigma = 1.0 / (1.0 + jnp.exp(-pre))
     dpre = (cotangent[...].astype(F32) * sigma * (1.0 + pre * (1.0 - sigma))).astype(BF)
     dagg = (lax.dot_general(dpre, w_nbr[...], OVER_COLS, preferred_element_type=F32) / FAN).astype(BF)
-
+    both_v[:NODES, :] = dagg
+    both_v[NODES:, :] = dpre
+    copies = send([both_v], [both], sems)
     out_v[:, :D] = dot(counts_t[NODES : NODES + HALF, :], dagg).astype(BF)
     out_v[:, D : 2 * D] = dot(counts_t[NODES + HALF : BORDER, :], dagg).astype(BF)
-    copies = send([out_v.at[:, : 2 * D]], [outward.at[:, : 2 * D]], sems)
-    out_v[:D, 2 * D :] = lax.dot_general(f, dpre, OVER_ROWS, preferred_element_type=F32).astype(BF)
+    copies += send([out_v.at[:, : 2 * D]], [outward.at[:, : 2 * D]], sems, 1)
+    out_v[:D, 2 * D :] = lax.dot_general(features[...], dpre, OVER_ROWS, preferred_element_type=F32).astype(BF)
     out_v[D:, 2 * D :] = lax.dot_general(agg, dpre, OVER_ROWS, preferred_element_type=F32).astype(BF)
-    copies += send([out_v.at[:, 2 * D :]], [outward.at[:, 2 * D :]], sems, 1)
-    theirs_v[...] = dot(counts_t[BORDER + SIDE :, :], dagg).astype(BF)
-    copies += send([theirs_v], [theirs], sems, 2)
-    hubs_v[...] = dot(counts_t[BORDER : BORDER + SIDE, :], dagg).astype(BF)
-    own_v[...] = dot(counts_t[:NODES, :], dagg) + lax.dot_general(
-        dpre, w_self[...], OVER_COLS, preferred_element_type=F32
-    )
-    copies += send([hubs_v, own_v], [hubs, own], sems, 3)
+    copies += send([out_v.at[:, 2 * D :]], [outward.at[:, 2 * D :]], sems, 2)
     finished(copies)
+
+
+def other_hubs(counts_t, both, out):
+    out[...] = dot(counts_t[BORDER + SIDE :, :], both[:NODES, :]).astype(BF)
+
+
+def mine_and_own(counts_t, both, w_self, hubs, own):
+    dagg = both[:NODES, :]
+    hubs[...] = dot(counts_t[BORDER : BORDER + SIDE, :], dagg).astype(BF)
+    own[...] = dot(counts_t[:NODES, :], dagg) + lax.dot_general(
+        both[NODES:, :], w_self[...], OVER_COLS, preferred_element_type=F32
+    )
 
 
 def pair_hubs(x, hubs, met, kept, *to):
@@ -208,9 +221,10 @@
         out[...] = (hubs[rows, :].astype(F32) + met[rows, :].astype(F32)).astype(BF)
 
 
-def sum_hubs(kept, a, b, c, out):
+def sum_hubs(kept, a, b, c, message, tiles, sems):
     total = kept[...].astype(F32) + a[...].astype(F32) + b[...].astype(F32) + c[...].astype(F32)
-    out[...] = split_rows(total).reshape(HALF, 128).astype(BF)
+    tiles[...] = split_rows(total).reshape(HALF, 128).astype(BF)
+    finished(send([tiles], [message.at[:, D:]], sems))
 
 
 def sum_weights(returned, out):
@@ -223,10 +237,10 @@
     out[...] = total + dot(home[:, HALF:], returned[:, D : 2 * D])
 
 
-def last_message(weights, hubs, out):
+def last_message(weights, hubs, message, rows, sems):
     total = jnp.sum(weights[...].astype(F32).reshape(GROUPS, 8, D), axis=0) * SCALE
-    out[:, :D] = jnp.broadcast_to(total[None], (MEMBERS, 8, D)).reshape(HALF, D).astype(BF)
-    out[:, D:] = hubs[...]
+    rows[...] = jnp.broadcast_to(total[None], (MEMBERS, 8, D)).reshape(HALF, D).astype(BF)
+    finished(send([rows], [message.at[:, :D]], sems))
 
 
 def finish(hub, last, partial, grad_self, grad_nbr, grad, weights_v, grad_v, sems):
@@ -264,37 +278,46 @@
         ],
     )
     incoming = exchange(outgoing, MEMBER, MEMBERS)
-    counts, counts_t, home, pre_self = call(
+    counts, counts_t, home, pre_self, counted = call(
         count_rows, "count_rows",
-        [((NODES, TABLE), BF), ((TABLE, NODES), BF), ((NODES, 2 * HALF), BF), ((NODES, D), F32)], 2**30, 2**22,
+        [((NODES, TABLE), BF), ((TABLE, NODES), BF), ((NODES, 2 * HALF), BF), ((NODES, D), F32), ((8, 128), F32)],
+        2**30, 2**22,
         core, neighbours.T, send_t, live, features, w_self, outgoing,
         smem=(0,), unread=(6,),
     )
-    (mine,) = call(own_hubs, "own_hubs", [side], 2**16, 2**19, incoming, pre_self, unread=(1,))
+    (mine,) = call(
+        own_hubs, "own_hubs", [side], 2**16, 2**19, incoming, counted,
+        kept=(0,), unread=(1,), scratch=[pltpu.VMEM((HALF, 128), BF), pltpu.SemaphoreType.DMA((1,))],
+    )
     mine = exchange(mine, "x", XS)
     swap = [(0, 1), (1, 0)]
     other = lax.ppermute(mine, "core", swap)
-    outward, theirs, hubs, own = call(
-        forward, "forward", [((HALF, 768), BF), side, side, ((NODES, D), F32)], 2**30, 2**23,
-        counts, counts_t, features, incoming, mine, other, pre_self, w_nbr, cotangent, w_self,
-        to_hbm=range(4),
-        scratch=[
-            pltpu.VMEM((HALF, 768), BF), pltpu.VMEM((SIDE, D), BF), pltpu.VMEM((SIDE, D), BF),
-            pltpu.VMEM((NODES, D), F32), pltpu.SemaphoreType.DMA((5,)),
-        ],
+    (near,) = call(near_sum, "near_sum", [((NODES, D), F32)], 2**28, 2**21, counts, features, incoming, mine)
+    outward, both = call(
+        forward, "forward", [((HALF, 768), BF), ((2 * NODES, D), BF)], 2**29, 2**22,
+        counts, counts_t, features, near, other, pre_self, w_nbr, cotangent,
+        to_hbm=range(2),
+        scratch=[pltpu.VMEM((HALF, 768), BF), pltpu.VMEM((2 * NODES, D), BF), pltpu.SemaphoreType.DMA((3,))],
     )
     returned = exchange(outward, MEMBER, MEMBERS)
 
+    (theirs,) = call(other_hubs, "other_hubs", [side], 2**27, 2**20, counts_t, both)
     met = lax.ppermute(theirs, "core", swap)
+    hubs, own = call(mine_and_own, "mine_and_own", [side, ((NODES, D), F32)], 2**28, 2**21, counts_t, both, w_self)
     block = ((NODES, D), BF)
     kept, *to = call(pair_hubs, "pair_hubs", [block] * XS, 2**18, 2**20, x, hubs, met, smem=(0,))
     came = [lax.ppermute(to[k - 1], "x", [(i, (i + k) % XS) for i in range(XS)]) for k in range(1, XS)]
-    (hub_tiles,) = call(sum_hubs, "sum_hubs", [((HALF, 128), BF)], 2**18, 2**20, kept, *came)
-
+    (hub_tiles,) = call(
+        sum_hubs, "sum_hubs", [((HALF, 384), BF)], 2**18, 2**20, kept, *came,
+        to_hbm=(0,), scratch=[pltpu.VMEM((HALF, 128), BF), pltpu.SemaphoreType.DMA((1,))],
+    )
     (weights,) = call(sum_weights, "sum_weights", [((GROUPS * 8, D), BF)], 2**17, 2**18, returned)
     weights = exchange(weights, GROUP, GROUPS)
     (partial,) = call(add_returned, "add_returned", [((NODES, D), F32)], 2**27, 2**20, returned, home, own)
-    (message,) = call(last_message, "last_message", [((HALF, 384), BF)], 2**17, 2**18, weights, hub_tiles)
+    (message,) = call(
+        last_message, "last_message", [((HALF, 384), BF)], 2**17, 2**18, weights, hub_tiles,
+        kept=(1,), to_hbm=(0,), alias={1: 0}, scratch=[pltpu.VMEM((HALF, D), BF), pltpu.SemaphoreType.DMA((1,))],
+    )
     last = exchange(message, MEMBER, MEMBERS)
     return tuple(
         call(

time: 127 us -> 127 us (level)
  waiting for transfers between devices: 51.7 us -> 45.2 us
  Pallas kernels: 14 us -> 17.3 us
  local copies, waits for them, and re-layouts: 2.34 us -> 5.17 us
    all_to_all x4, waiting for transfers between devices: 47.8 us -> 44.2 us  [exchange(): lax.all_to_all(block, axes, split_axis=0, concat_axis=0, tiled=True)]
    pallas_call x10 -> x13, Pallas kernels: 14 us -> 17.3 us  [call(): pl.pallas_call(body, name=name, out_shape=[(pltpu.HBM if i in to_hbm else...]
    unnamed x26 -> x30, local copies, waits for them, and re-layouts: 2.34 us -> 5.17 us
    ppermute x1, waiting for transfers between devices: 1.88 us -> 0.3 us  [local(): other = lax.ppermute(mine, 'core', swap)]
    ppermute x1, waiting for transfers between devices: 2.08 us -> 0.72 us  [local(): met = lax.ppermute(theirs, 'core', swap)]
  transfers between devices with their start and end apart: 9 -> 9, of which waited for: 6 -> 6; matrix products, arithmetic and copies ran while one was open for 0% -> 0% of each run, Pallas kernels for 5% -> 8%
where the time goes in v4:
time: 127 us; the launch traced here: 126 us
  waiting for transfers between devices  45.2 us (36%)
  starting transfers between devices  45.1 us (36%)
  Pallas kernels  17.3 us (14%)
  blocking collectives  12.2 us (10%)
  local copies, waits for them, and re-layouts  5.17 us (4%)
    all_to_all x4, waiting for transfers between devices, exchange(): lax.all_to_all(block, axes, split_axis=0, concat_axis=0, tiled=True)  44.2 us
    all_to_all x4, starting transfers between devices, exchange(): lax.all_to_all(block, axes, split_axis=0, concat_axis=0, tiled=True)  32 us
    pallas_call x13, Pallas kernels, call(): pl.pallas_call(body, name=name, out_shape=[(pltpu.HBM if i in to_hbm else...  17.3 us
    all_to_all x1, blocking collectives, exchange(): lax.all_to_all(block, axes, split_axis=0, concat_axis=0, tiled=True)  12.2 us
    ppermute x3, starting transfers between devices, local(): lax.ppermute(to[k - 1], 'x', [(i, (i + k) % XS) for i in range(XS)])  9.18 us
    unnamed x30, local copies, waits for them, and re-layouts  5.17 us
  transfers between devices with their start and end apart: 9, of which 6 were waited for; matrix products, arithmetic and copies ran while one was open for 0% of the time, Pallas kernels for 8%

profile of v4, /device:TPU:16, one launch (start us, length us, event | category | flops | bytes accessed | tf_op | source)
XLA Modules:
  0.0 125.9 jit_solution(18295899399117344154)
XLA Ops:
  0.6 0.0 copy-start.1
  0.6 0.0 copy-start.13
  0.7 0.0 copy-start.11
  0.7 2.4 %outgoing_rows.1.after = bf16[512,640]{1,0:T(8,128)(2,1)} custom-call(s32[1,4]{1,0:T(1,128)} %hub.3, s32[16,64]{1,0:T(8,128)} %bitcast.23, s32[1,64]{1,0:T(1,128)} %bitcast.25, bf16[256,256]{1,0:T(8,128)(2,1)} %features.7), custom_call_target="tpu_custom_call" | custom-call | flops 134217728 | bytes 1048576 | tf_op jit(solution)/shard_map/outgoing_rows/pallas_call | solution.py:49
  3.0 16.7 %all-to-all-start = ((bf16[64,8,640]{2,1,0:T(8,128)(2,1)}), bf16[64,8,640]{2,1,0:T(8,128)(2,1)}, u32[]{:S(2)}, u32[]{:S(2)}) async-start(bf16[64,8,640]{2,1,0:T(8,128)(2,1)} %bitcast.17), calls=%async_computation | async-start | bytes 1310720 | tf_op jit(solution)/shard_map/all_to_all | solution.py:262
  19.7 0.0 copy-done.1
  19.7 0.0 copy-done.13
  19.7 0.0 copy-done.11
  19.7 0.0 copy-start
  19.7 1.1 copy-done
  20.9 0.0 copy-start.9
  20.9 0.9 copy-done.9
  21.8 0.0 copy-start.14
  21.8 0.7 copy-done.14
  22.5 5.2 %count_rows.1 = (bf16[256,3328]{1,0:T(8,128)(2,1)S(1)}, bf16[3328,256]{1,0:T(8,128)(2,1)S(1)}, bf16[256,1024]{1,0:T(8,128)(2,1)S(1)}, f32[256,256]{1,0:T(8,128)S(1)}, f32[8,128]{1,0:T(8,128)S(1)}) custom-call(s32[1]{0:T(128)} %bitcast.core, s32[10,256]{1,0:T(8,128)S(1)} %bitcast.27, s32[16,64]{1,0:T(8,128)S(1)} %bitcast.24, s32[1,64]{1,0:T(1,128)S(1)} %bitcast.26, ...), custom_call_target="tpu_custom_call" | custom-call | flops 1073741824 | bytes 4194304 | tf_op jit(solution)/shard_map/count_rows/pallas_call | solution.py:49
  27.7 0.0 copy-start.3
  27.7 0.8 copy-done.3
  28.5 0.0 copy-start.5
  28.5 0.7 copy-done.5
  29.2 12.6 %all-to-all-done = bf16[64,8,640]{2,1,0:T(8,128)(2,1)} async-done(((bf16[64,8,640]{2,1,0:T(8,128)(2,1)}), bf16[64,8,640]{2,1,0:T(8,128)(2,1)}, u32[]{:S(2)}, u32[]{:S(2)}) %all-to-all-start) | async-done | bytes 655392 | tf_op jit(solution)/shard_map/all_to_all | solution.py:262
  41.9 1.0 own_hubs.1
  42.9 12.2 %all_to_all.25 = bf16[4,256,256]{2,1,0:T(8,128)(2,1)S(1)} all-to-all(bf16[4,256,256]{2,1,0:T(8,128)(2,1)S(1)} %bitcast.20), channel_id=1, replica_groups=mesh['x'=4,'core'=2,'y'=8,'z'=8] {'x'}, dimensions={0} | all-to-all | bytes 1048576 | tf_op jit(solution)/shard_map/all_to_all | solution.py:262
  55.0 0.0 copy-start.6
  55.0 0.0 copy-start.7
  55.0 0.0 copy-start.8
  55.0 2.0 %collective-permute-start = (bf16[1024,256]{1,0:T(8,128)(2,1)S(1)}, bf16[1024,256]{1,0:T(8,128)(2,1)S(1)}, u32[]{:S(2)}, u32[]{:S(2)}) collective-permute-start(bf16[1024,256]{1,0:T(8,128)(2,1)S(1)} %bitcast.18), channel_id=1, source_target_pairs={{0,64},{64,0},{1,65},{65,1},{2,66},{66,2},{3,67},{67,3},{4,68},{68... | collective-permute-start | bytes 1572872 | tf_op jit(solution)/shard_map/ppermute | solution.py:294
  57.1 1.6 %near_sum.1.near = f32[256,256]{1,0:T(8,128)S(1)} custom-call(bf16[256,3328]{1,0:T(8,128)(2,1)S(1)} %get-tuple-element.16.counts, bf16[256,256]{1,0:T(8,128)(2,1)S(1)} %copy-done.1, bf16[512,640]{1,0:T(8,128)(2,1)} %bitcast.5.incoming, bf16[1024,256]{1,0:T(8,128)(2,1)S(1)} %bitcast.19), custom_call_target="tpu_custom_call" | custom-call | flops 268435456 | bytes 2097152 | tf_op jit(solution)/shard_map/near_sum/pallas_call | solution.py:49
  58.7 0.3 collective-permute-done.other
  59.0 0.0 copy-done.6
  59.0 0.0 copy-done.7
  59.0 0.0 copy-done.8
  59.0 1.9 %forward.1 = (bf16[512,768]{1,0:T(8,128)(2,1)}, bf16[512,256]{1,0:T(8,128)(2,1)}) custom-call(bf16[256,3328]{1,0:T(8,128)(2,1)S(1)} %get-tuple-element.16.counts, bf16[3328,256]{1,0:T(8,128)(2,1)S(1)} %get-tuple-element.17.counts_t, bf16[256,256]{1,0:T(8,128)(2,1)S(1)} %copy-done.1, f32[256,256]{1,0:T(8,128)S(1)} %near_sum.1.near, ...), custom_call_target="tpu_custom_call" | custom-call | flops 536870912 | bytes 4194304 | tf_op jit(solution)/shard_map/forward/pallas_call | solution.py:49
  60.9 0.0 copy-start.2
  60.9 6.6 %all-to-all-start.2 = ((bf16[64,8,768]{2,1,0:T(8,128)(2,1)}), bf16[64,8,768]{2,1,0:T(8,128)(2,1)S(1)}, u32[]{:S(2)}, u32[]{:S(2)}) async-start(bf16[64,8,768]{2,1,0:T(8,128)(2,1)} %bitcast.29), calls=%async_computation.2 | async-start | bytes 1572864 | tf_op jit(solution)/shard_map/all_to_all | solution.py:262
  67.6 0.0 copy-done.2
  67.6 0.3 other_hubs.1
  67.9 1.9 %collective-permute-start.1 = (bf16[1024,256]{1,0:T(8,128)(2,1)S(1)}, bf16[1024,256]{1,0:T(8,128)(2,1)}, u32[]{:S(2)}, u32[]{:S(2)}) collective-permute-start(bf16[1024,256]{1,0:T(8,128)(2,1)S(1)} %other_hubs.1), channel_id=1, source_target_pairs={{0,64},{64,0},{1,65},{65,1},{2,66},{66,2},{3,67},{67,3},{4,68},{68... | collective-permute-start | bytes 1572872 | tf_op jit(solution)/shard_map/ppermute | solution.py:305
  69.8 0.0 copy-start.10
  69.8 0.9 copy-done.10
  70.7 0.4 mine_and_own.1
  71.1 0.7 collective-permute-done.1.met
  71.8 1.2 pair_hubs.1
  73.0 2.5 %collective-permute-start.2 = (bf16[256,256]{1,0:T(8,128)(2,1)S(1)}, bf16[256,256]{1,0:T(8,128)(2,1)S(1)}, u32[]{:S(2)}, u32[]{:S(2)}) collective-permute-start(bf16[256,256]{1,0:T(8,128)(2,1)S(1)} %get-tuple-element.24), channel_id=1, source_target_pairs={{0,128},{128,256},{256,384},{384,0},{1,129},{129,257},{257,385},{3... | collective-permute-start | bytes 393224 | tf_op jit(solution)/shard_map/ppermute | solution.py:309
  75.5 4.0 %collective-permute-start.3 = (bf16[256,256]{1,0:T(8,128)(2,1)S(1)}, bf16[256,256]{1,0:T(8,128)(2,1)S(1)}, u32[]{:S(2)}, u32[]{:S(2)}) collective-permute-start(bf16[256,256]{1,0:T(8,128)(2,1)S(1)} %get-tuple-element.25), channel_id=1, source_target_pairs={{0,256},{128,384},{256,0},{384,128},{1,257},{129,385},{257,1},{385... | collective-permute-start | bytes 393224 | tf_op jit(solution)/shard_map/ppermute | solution.py:309
  79.4 2.7 %collective-permute-start.4 = (bf16[256,256]{1,0:T(8,128)(2,1)S(1)}, bf16[256,256]{1,0:T(8,128)(2,1)S(1)}, u32[]{:S(2)}, u32[]{:S(2)}) collective-permute-start(bf16[256,256]{1,0:T(8,128)(2,1)S(1)} %get-tuple-element.26), channel_id=1, source_target_pairs={{0,384},{128,0},{256,128},{384,256},{1,385},{129,1},{257,129},{385... | collective-permute-start | bytes 393224 | tf_op jit(solution)/shard_map/ppermute | solution.py:309
  82.2 10.7 %all-to-all-done.2 = bf16[64,8,768]{2,1,0:T(8,128)(2,1)S(1)} async-done(((bf16[64,8,768]{2,1,0:T(8,128)(2,1)}), bf16[64,8,768]{2,1,0:T(8,128)(2,1)S(1)}, u32[]{:S(2)}, u32[]{:S(2)}) %all-to-all-start.2) | async-done | bytes 786464 | tf_op jit(solution)/shard_map/all_to_all | solution.py:262
  92.9 0.0 copy-start.4
  92.9 0.7 sum_weights.1
  93.6 3.3 %all-to-all-start.3 = ((bf16[8,8,256]{2,1,0:T(8,128)(2,1)}), bf16[8,8,256]{2,1,0:T(8,128)(2,1)S(1)}, u32[]{:S(2)}, u32[]{:S(2)}) async-start(bf16[8,8,256]{2,1,0:T(8,128)(2,1)} %bitcast.10), calls=%async_computation.3 | async-start | bytes 65536 | tf_op jit(solution)/shard_map/all_to_all | solution.py:262
  96.9 0.0 collective-permute-done.2.a
  96.9 0.0 collective-permute-done.3.b
  96.9 0.0 collective-permute-done.4.c
  96.9 0.8 sum_hubs.1.hubs
  97.7 4.6 %all-to-all-done.3 = bf16[8,8,256]{2,1,0:T(8,128)(2,1)S(1)} async-done(((bf16[8,8,256]{2,1,0:T(8,128)(2,1)}), bf16[8,8,256]{2,1,0:T(8,128)(2,1)S(1)}, u32[]{:S(2)}, u32[]{:S(2)}) %all-to-all-start.3) | async-done | bytes 32800 | tf_op jit(solution)/shard_map/all_to_all | solution.py:262
  102.3 0.0 copy-start.12
  102.3 0.8 last_message.1
  103.0 5.4 %all-to-all-start.4 = ((bf16[64,8,384]{2,1,0:T(8,128)(2,1)}), bf16[64,8,384]{2,1,0:T(8,128)(2,1)S(1)}, u32[]{:S(2)}, u32[]{:S(2)}) async-start(bf16[64,8,384]{2,1,0:T(8,128)(2,1)} %bitcast.28), calls=%async_computation.4 | async-start | bytes 786432 | tf_op jit(solution)/shard_map/all_to_all | solution.py:262
  108.4 0.0 copy-done.4
  108.4 0.3 add_returned.1.partial
  108.7 16.3 %all-to-all-done.4 = bf16[64,8,384]{2,1,0:T(8,128)(2,1)S(1)} async-done(((bf16[64,8,384]{2,1,0:T(8,128)(2,1)}), bf16[64,8,384]{2,1,0:T(8,128)(2,1)S(1)}, u32[]{:S(2)}, u32[]{:S(2)}) %all-to-all-start.4) | async-done | bytes 393248 | tf_op jit(solution)/shard_map/all_to_all | solution.py:262
  125.0 0.0 copy-done.12
  125.0 0.9 finish.1
Async XLA Ops:
  0.6 19.1 %copy-start.1 = (bf16[256,256]{1,0:T(8,128)(2,1)S(1)}, bf16[256,256]{1,0:T(8,128)(2,1)}, u32[]{:S(2)}) copy-start(bf16[256,256]{1,0:T(8,128)(2,1)} %features.7) | copy-start | bytes 393220
  0.6 19.1 %copy-start.13 = (s32[64]{0:T(128)S(1)}, s32[64]{0:T(128)}, u32[]{:S(2)}) copy-start(s32[64]{0:T(128)} %param.11) | copy-start | bytes 772
  0.7 19.1 %copy-start.11 = (s32[64,16]{0,1:T(8,128)S(1)}, s32[64,16]{0,1:T(8,128)}, u32[]{:S(2)}) copy-start(s32[64,16]{0,1:T(8,128)} %param.10) | copy-start | bytes 12292
  3.0 38.8 %all-to-all-start = ((bf16[64,8,640]{2,1,0:T(8,128)(2,1)}), bf16[64,8,640]{2,1,0:T(8,128)(2,1)}, u32[]{:S(2)}, u32[]{:S(2)}) async-start(bf16[64,8,640]{2,1,0:T(8,128)(2,1)} %bitcast.17), calls=%async_computation | async-start | bytes 1310720 | tf_op jit(solution)/shard_map/all_to_all | solution.py:262
  19.7 1.1 copy-start
  20.9 0.9 copy-start.9
  21.8 0.7 copy-start.14
  27.7 0.8 copy-start.3
  28.5 0.7 copy-start.5
  55.0 3.9 %copy-start.6 = (f32[256,256]{1,0:T(8,128)S(1)}, f32[256,256]{1,0:T(8,128)}, u32[]{:S(2)}) copy-start(f32[256,256]{1,0:T(8,128)} %copy-done.5) | copy-start | bytes 786436
  55.0 3.9 %copy-start.7 = (bf16[256,256]{1,0:T(8,128)(2,1)S(1)}, bf16[256,256]{1,0:T(8,128)(2,1)}, u32[]{:S(2)}) copy-start(bf16[256,256]{1,0:T(8,128)(2,1)} %w_nbr.1) | copy-start | bytes 393220
  55.0 3.9 %copy-start.8 = (bf16[256,256]{1,0:T(8,128)(2,1)S(1)}, bf16[256,256]{1,0:T(8,128)(2,1)}, u32[]{:S(2)}) copy-start(bf16[256,256]{1,0:T(8,128)(2,1)} %cotangent.1) | copy-start | bytes 393220
  55.0 3.9 %collective-permute-start = (bf16[1024,256]{1,0:T(8,128)(2,1)S(1)}, bf16[1024,256]{1,0:T(8,128)(2,1)S(1)}, u32[]{:S(2)}, u32[]{:S(2)}) collective-permute-start(bf16[1024,256]{1,0:T(8,128)(2,1)S(1)} %bitcast.18), channel_id=1, source_target_pairs={{0,64},{64,0},{1,65},{65,1},{2,66},{66,2},{3,67},{67,3},{4,68},{68... | collective-permute-start | bytes 1572872 | tf_op jit(solution)/shard_map/ppermute | solution.py:294
  60.9 6.7 %copy-start.2 = (bf16[512,256]{1,0:T(8,128)(2,1)S(1)}, bf16[512,256]{1,0:T(8,128)(2,1)}, u32[]{:S(2)}) copy-start(bf16[512,256]{1,0:T(8,128)(2,1)} %get-tuple-element.21.both) | copy-start | bytes 786436
  60.9 31.9 %all-to-all-start.2 = ((bf16[64,8,768]{2,1,0:T(8,128)(2,1)}), bf16[64,8,768]{2,1,0:T(8,128)(2,1)S(1)}, u32[]{:S(2)}, u32[]{:S(2)}) async-start(bf16[64,8,768]{2,1,0:T(8,128)(2,1)} %bitcast.29), calls=%async_computation.2 | async-start | bytes 1572864 | tf_op jit(solution)/shard_map/all_to_all | solution.py:262
  67.9 3.9 %collective-permute-start.1 = (bf16[1024,256]{1,0:T(8,128)(2,1)S(1)}, bf16[1024,256]{1,0:T(8,128)(2,1)}, u32[]{:S(2)}, u32[]{:S(2)}) collective-permute-start(bf16[1024,256]{1,0:T(8,128)(2,1)S(1)} %other_hubs.1), channel_id=1, source_target_pairs={{0,64},{64,0},{1,65},{65,1},{2,66},{66,2},{3,67},{67,3},{4,68},{68... | collective-permute-start | bytes 1572872 | tf_op jit(solution)/shard_map/ppermute | solution.py:305
  69.8 0.9 copy-start.10
  73.0 23.9 %collective-permute-start.2 = (bf16[256,256]{1,0:T(8,128)(2,1)S(1)}, bf16[256,256]{1,0:T(8,128)(2,1)S(1)}, u32[]{:S(2)}, u32[]{:S(2)}) collective-permute-start(bf16[256,256]{1,0:T(8,128)(2,1)S(1)} %get-tuple-element.24), channel_id=1, source_target_pairs={{0,128},{128,256},{256,384},{384,0},{1,129},{129,257},{257,385},{3... | collective-permute-start | bytes 393224 | tf_op jit(solution)/shard_map/ppermute | solution.py:309
  75.5 21.5 %collective-permute-start.3 = (bf16[256,256]{1,0:T(8,128)(2,1)S(1)}, bf16[256,256]{1,0:T(8,128)(2,1)S(1)}, u32[]{:S(2)}, u32[]{:S(2)}) collective-permute-start(bf16[256,256]{1,0:T(8,128)(2,1)S(1)} %get-tuple-element.25), channel_id=1, source_target_pairs={{0,256},{128,384},{256,0},{384,128},{1,257},{129,385},{257,1},{385... | collective-permute-start | bytes 393224 | tf_op jit(solution)/shard_map/ppermute | solution.py:309
  79.4 17.5 %collective-permute-start.4 = (bf16[256,256]{1,0:T(8,128)(2,1)S(1)}, bf16[256,256]{1,0:T(8,128)(2,1)S(1)}, u32[]{:S(2)}, u32[]{:S(2)}) collective-permute-start(bf16[256,256]{1,0:T(8,128)(2,1)S(1)} %get-tuple-element.26), channel_id=1, source_target_pairs={{0,384},{128,0},{256,128},{384,256},{1,385},{129,1},{257,129},{385... | collective-permute-start | bytes 393224 | tf_op jit(solution)/shard_map/ppermute | solution.py:309
  92.9 15.5 %copy-start.4 = (bf16[256,1024]{1,0:T(8,128)(2,1)S(1)}, bf16[256,1024]{1,0:T(8,128)(2,1)}, u32[]{:S(2)}) copy-start(bf16[256,1024]{1,0:T(8,128)(2,1)} %copy-done.3) | copy-start | bytes 1572868
  93.6 8.7 %all-to-all-start.3 = ((bf16[8,8,256]{2,1,0:T(8,128)(2,1)}), bf16[8,8,256]{2,1,0:T(8,128)(2,1)S(1)}, u32[]{:S(2)}, u32[]{:S(2)}) async-start(bf16[8,8,256]{2,1,0:T(8,128)(2,1)} %bitcast.10), calls=%async_computation.3 | async-start | bytes 65536 | tf_op jit(solution)/shard_map/all_to_all | solution.py:262
  102.3 22.7 %copy-start.12 = (s32[1,4]{1,0:T(1,128)S(1)}, s32[1,4]{1,0:T(1,128)}, u32[]{:S(2)}) copy-start(s32[1,4]{1,0:T(1,128)} %hub.3) | copy-start | bytes 52
  103.0 22.0 %all-to-all-start.4 = ((bf16[64,8,384]{2,1,0:T(8,128)(2,1)}), bf16[64,8,384]{2,1,0:T(8,128)(2,1)S(1)}, u32[]{:S(2)}, u32[]{:S(2)}) async-start(bf16[64,8,384]{2,1,0:T(8,128)(2,1)} %bitcast.28), calls=%async_computation.4 | async-start | bytes 786432 | tf_op jit(solution)/shard_map/all_to_all | solution.py:262

commit v5 on v4

--- a/solution.py
+++ b/solution.py
@@ -141,7 +141,7 @@
     return jnp.where(b < 0, n, jnp.where(h < 0, border, hub))
 
 
-def count_rows(core, near_t, send_t, count, features, w_self, after, counts, counts_t, home, pre_self, done):
+def count_rows(core, near_t, send_t, count, features, w_self, after, counts, counts_out, home, pre_self, done, counts_t, sems):
     row_t = table_row(near_t[...], core[0])
     step = 32
 
@@ -154,6 +154,7 @@
             total = total + jnp.where(ids == row_t[f : f + 1, :], 1.0, 0.0)
         counts_t[pl.ds(base, step), :] = total.astype(BF)
 
+    copies = send([counts_t], [counts_out], sems)
     eye = (iota((NODES, NODES), 0) == iota((NODES, NODES), 1)).astype(F32).astype(BF)
     for t in range(TABLE // 256):
         block = lax.dot_general(eye, counts_t[t * 256 : (t + 1) * 256, :], OVER_COLS, preferred_element_type=F32)
@@ -163,26 +164,28 @@
         home[:, a * HALF : (a + 1) * HALF] = block.astype(BF)
     pre_self[...] = dot(features[...], w_self[...])
     done[...] = jnp.zeros((8, 128), F32)
-
-
-def own_hubs(incoming, after, out, tiles, sems):
-    finished(send([incoming.at[:, 2 * D :]], [tiles], sems))
-    left, right = join_rows(tiles[...].astype(F32).reshape(MEMBERS, 8, 128))
+    finished(copies)
+
+
+def own_hubs(incoming, after, out):
+    left, right = join_rows(incoming[:, 2 * D :].astype(F32).reshape(MEMBERS, 8, 128))
     left, right = left.astype(BF), right.astype(BF)
     for x in range(XS):
         out[x * 256 : (x + 1) * 256, :128] = left
         out[x * 256 : (x + 1) * 256, 128:] = right
 
 
-def near_sum(counts, features, incoming, mine, out):
+def near_sum(counts, counts_t, features, incoming, mine, out, back, sems):
+    fetch = send([counts_t.at[NODES:BORDER, :]], [back], sems)
     total = dot(counts[:, :NODES], features[...])
     total += dot(counts[:, NODES : NODES + HALF], incoming[:, :D])
     total += dot(counts[:, NODES + HALF : BORDER], incoming[:, D : 2 * D])
     out[...] = total + dot(counts[:, BORDER : BORDER + SIDE], mine[...])
+    finished(fetch)
 
 
 def forward(
-    counts, counts_t, features, near, other, pre_self, w_nbr, cotangent, outward, both, out_v, both_v, sems
+    counts, back, features, near, other, pre_self, w_nbr, cotangent, outward, both, out_v, both_v, sems
 ):
     total = near[...] + dot(counts[:, BORDER + SIDE :], other[...])
     agg = (total / FAN).astype(BF)
@@ -193,8 +196,8 @@
     both_v[:NODES, :] = dagg
     both_v[NODES:, :] = dpre
     copies = send([both_v], [both], sems)
-    out_v[:, :D] = dot(counts_t[NODES : NODES + HALF, :], dagg).astype(BF)
-    out_v[:, D : 2 * D] = dot(counts_t[NODES + HALF : BORDER, :], dagg).astype(BF)
+    out_v[:, :D] = dot(back[:HALF, :], dagg).astype(BF)
+    out_v[:, D : 2 * D] = dot(back[HALF:, :], dagg).astype(BF)
     copies += send([out_v.at[:, : 2 * D]], [outward.at[:, : 2 * D]], sems, 1)
     out_v[:D, 2 * D :] = lax.dot_general(features[...], dpre, OVER_ROWS, preferred_element_type=F32).astype(BF)
     out_v[D:, 2 * D :] = lax.dot_general(agg, dpre, OVER_ROWS, preferred_element_type=F32).astype(BF)
@@ -202,14 +205,16 @@
     finished(copies)
 
 
-def other_hubs(counts_t, both, out):
-    out[...] = dot(counts_t[BORDER + SIDE :, :], both[:NODES, :]).astype(BF)
-
-
-def mine_and_own(counts_t, both, w_self, hubs, own):
+def other_hubs(counts_t, both, out, rows, sems):
+    finished(send([counts_t.at[BORDER + SIDE :, :]], [rows], sems))
+    out[...] = dot(rows[...], both[:NODES, :]).astype(BF)
+
+
+def mine_and_own(counts_t, both, w_self, hubs, own, rows, near, sems):
+    finished(send([counts_t.at[BORDER : BORDER + SIDE, :], counts_t.at[:NODES, :]], [rows, near], sems))
     dagg = both[:NODES, :]
-    hubs[...] = dot(counts_t[BORDER : BORDER + SIDE, :], dagg).astype(BF)
-    own[...] = dot(counts_t[:NODES, :], dagg) + lax.dot_general(
+    hubs[...] = dot(rows[...], dagg).astype(BF)
+    own[...] = dot(near[...], dagg) + lax.dot_general(
         both[NODES:, :], w_self[...], OVER_COLS, preferred_element_type=F32
     )
 
@@ -269,7 +274,7 @@
     live = block_counts.reshape(1, MEMBERS)
     side = ((SIDE, D), BF)
     (outgoing,) = call(
-        outgoing_rows, "outgoing_rows", [((HALF, 640), BF)], 2**27, 2**20,
+        outgoing_rows, "outgoing_rows", [((HALF, 640), BF)], 2**20, 2**23,
         hub_rows, send_t, live, features,
         kept=range(4), to_hbm=(0,),
         scratch=[
@@ -281,47 +286,55 @@
     counts, counts_t, home, pre_self, counted = call(
         count_rows, "count_rows",
         [((NODES, TABLE), BF), ((TABLE, NODES), BF), ((NODES, 2 * HALF), BF), ((NODES, D), F32), ((8, 128), F32)],
-        2**30, 2**22,
+        2**20, 2**23,
         core, neighbours.T, send_t, live, features, w_self, outgoing,
-        smem=(0,), unread=(6,),
-    )
-    (mine,) = call(
-        own_hubs, "own_hubs", [side], 2**16, 2**19, incoming, counted,
-        kept=(0,), unread=(1,), scratch=[pltpu.VMEM((HALF, 128), BF), pltpu.SemaphoreType.DMA((1,))],
-    )
+        smem=(0,), kept=(6,), to_hbm=(1,), scratch=[pltpu.VMEM((TABLE, NODES), BF), pltpu.SemaphoreType.DMA((1,))],
+    )
+    (mine,) = call(own_hubs, "own_hubs", [side], 2**20, 2**23, incoming, counted, unread=(1,))
     mine = exchange(mine, "x", XS)
     swap = [(0, 1), (1, 0)]
     other = lax.ppermute(mine, "core", swap)
-    (near,) = call(near_sum, "near_sum", [((NODES, D), F32)], 2**28, 2**21, counts, features, incoming, mine)
+    near, back = call(
+        near_sum, "near_sum", [((NODES, D), F32), ((2 * HALF, NODES), BF)], 2**20, 2**23,
+        counts, counts_t, features, incoming, mine,
+        kept=(1,), scratch=[pltpu.SemaphoreType.DMA((1,))],
+    )
     outward, both = call(
-        forward, "forward", [((HALF, 768), BF), ((2 * NODES, D), BF)], 2**29, 2**22,
-        counts, counts_t, features, near, other, pre_self, w_nbr, cotangent,
+        forward, "forward", [((HALF, 768), BF), ((2 * NODES, D), BF)], 2**20, 2**23,
+        counts, back, features, near, other, pre_self, w_nbr, cotangent,
         to_hbm=range(2),
         scratch=[pltpu.VMEM((HALF, 768), BF), pltpu.VMEM((2 * NODES, D), BF), pltpu.SemaphoreType.DMA((3,))],
     )
     returned = exchange(outward, MEMBER, MEMBERS)
 
-    (theirs,) = call(other_hubs, "other_hubs", [side], 2**27, 2**20, counts_t, both)
+    rows = pltpu.VMEM((SIDE, NODES), BF)
+    (theirs,) = call(
+        other_hubs, "other_hubs", [side], 2**20, 2**23, counts_t, both,
+        kept=(0,), scratch=[rows, pltpu.SemaphoreType.DMA((1,))],
+    )
     met = lax.ppermute(theirs, "core", swap)
-    hubs, own = call(mine_and_own, "mine_and_own", [side, ((NODES, D), F32)], 2**28, 2**21, counts_t, both, w_self)
+    hubs, own = call(
+        mine_and_own, "mine_and_own", [side, ((NODES, D), F32)], 2**20, 2**23, counts_t, both, w_self,
+        kept=(0,), scratch=[rows, pltpu.VMEM((NODES, NODES), BF), pltpu.SemaphoreType.DMA((2,))],
+    )
     block = ((NODES, D), BF)
-    kept, *to = call(pair_hubs, "pair_hubs", [block] * XS, 2**18, 2**20, x, hubs, met, smem=(0,))
+    kept, *to = call(pair_hubs, "pair_hubs", [block] * XS, 2**20, 2**23, x, hubs, met, smem=(0,))
     came = [lax.ppermute(to[k - 1], "x", [(i, (i + k) % XS) for i in range(XS)]) for k in range(1, XS)]
     (hub_tiles,) = call(
-        sum_hubs, "sum_hubs", [((HALF, 384), BF)], 2**18, 2**20, kept, *came,
+        sum_hubs, "sum_hubs", [((HALF, 384), BF)], 2**20, 2**23, kept, *came,
         to_hbm=(0,), scratch=[pltpu.VMEM((HALF, 128), BF), pltpu.SemaphoreType.DMA((1,))],
     )
-    (weights,) = call(sum_weights, "sum_weights", [((GROUPS * 8, D), BF)], 2**17, 2**18, returned)
+    (weights,) = call(sum_weights, "sum_weights", [((GROUPS * 8, D), BF)], 2**20, 2**23, returned)
     weights = exchange(weights, GROUP, GROUPS)
-    (partial,) = call(add_returned, "add_returned", [((NODES, D), F32)], 2**27, 2**20, returned, home, own)
+    (partial,) = call(add_returned, "add_returned", [((NODES, D), F32)], 2**20, 2**23, returned, home, own)
     (message,) = call(
-        last_message, "last_message", [((HALF, 384), BF)], 2**17, 2**18, weights, hub_tiles,
+        last_message, "last_message", [((HALF, 384), BF)], 2**20, 2**23, weights, hub_tiles,
         kept=(1,), to_hbm=(0,), alias={1: 0}, scratch=[pltpu.VMEM((HALF, D), BF), pltpu.SemaphoreType.DMA((1,))],
     )
     last = exchange(message, MEMBER, MEMBERS)
     return tuple(
         call(
-            finish, "finish", [((D, D), F32), ((D, D), F32), ((NODES, D), BF)], 2**18, 2**20, hub_rows, last, partial,
+            finish, "finish", [((D, D), F32), ((D, D), F32), ((NODES, D), BF)], 2**20, 2**23, hub_rows, last, partial,
             to_hbm=range(3),
             scratch=[pltpu.VMEM((2 * D, D), F32), pltpu.VMEM((NODES, D), BF), pltpu.SemaphoreType.DMA((3,))],
         )

time: 127 us -> 125 us (0.984)
  local copies, waits for them, and re-layouts: 5.17 us -> 0.04 us
  waiting for transfers between devices: 45.2 us -> 48.5 us
    unnamed x30 -> x18, local copies, waits for them, and re-layouts: 5.17 us -> 0.04 us
    all_to_all x4, waiting for transfers between devices: 44.2 us -> 47.3 us  [exchange(): lax.all_to_all(block, axes, split_axis=0, concat_axis=0, tiled=True)]
  transfers between devices with their start and end apart: 9 -> 9, of which waited for: 6 -> 6; matrix products, arithmetic and copies ran while one was open for 0% -> 0% of each run, Pallas kernels for 8% -> 10%
where the time goes in v5:
time: 125 us
  waiting for transfers between devices  48.5 us (39%)
  starting transfers between devices  44.9 us (36%)
  Pallas kernels  18.1 us (14%)
  blocking collectives  12.2 us (10%)
    all_to_all x4, waiting for transfers between devices, exchange(): lax.all_to_all(block, axes, split_axis=0, concat_axis=0, tiled=True)  47.3 us
    all_to_all x4, starting transfers between devices, exchange(): lax.all_to_all(block, axes, split_axis=0, concat_axis=0, tiled=True)  31.9 us
    pallas_call x13, Pallas kernels, call(): pl.pallas_call(body, name=name, out_shape=[(pltpu.HBM if i in to_hbm else...  18.1 us
    all_to_all x1, blocking collectives, exchange(): lax.all_to_all(block, axes, split_axis=0, concat_axis=0, tiled=True)  12.2 us
    ppermute x3, starting transfers between devices, local(): lax.ppermute(to[k - 1], 'x', [(i, (i + k) % XS) for i in range(XS)])  9.18 us
  transfers between devices with their start and end apart: 9, of which 6 were waited for; matrix products, arithmetic and copies ran while one was open for 0% of the time, Pallas kernels for 10%

profile of v5, /device:TPU:16, one launch (start us, length us, event | category | flops | bytes accessed | tf_op | source)
XLA Modules:
  0.0 124.7 jit_solution(15608701065317508371)
XLA Ops:
  0.6 0.0 copy-start
  0.6 0.0 copy-start.7
  0.7 0.0 copy-start.5
  0.7 0.0 copy-start.2
  0.7 0.0 copy-start.6
  0.7 2.4 %outgoing_rows.1.after = bf16[512,640]{1,0:T(8,128)(2,1)} custom-call(s32[1,4]{1,0:T(1,128)} %hub.3, s32[16,64]{1,0:T(8,128)} %bitcast.24, s32[1,64]{1,0:T(1,128)} %bitcast.27, bf16[256,256]{1,0:T(8,128)(2,1)} %features.7), custom_call_target="tpu_custom_call" | custom-call | flops 1048576 | bytes 8388608 | tf_op jit(solution)/shard_map/outgoing_rows/pallas_call | solution.py:49
  3.1 16.5 %all-to-all-start = ((bf16[64,8,640]{2,1,0:T(8,128)(2,1)}), bf16[64,8,640]{2,1,0:T(8,128)(2,1)S(1)}, u32[]{:S(2)}, u32[]{:S(2)}) async-start(bf16[64,8,640]{2,1,0:T(8,128)(2,1)} %bitcast.29), calls=%async_computation | async-start | bytes 1310720 | tf_op jit(solution)/shard_map/all_to_all | solution.py:267
  19.6 0.0 copy-done
  19.6 0.0 copy-done.7
  19.6 0.0 copy-done.5
  19.6 0.0 copy-done.2
  19.6 0.0 copy-done.6
  19.6 6.3 %count_rows.1 = (bf16[256,3328]{1,0:T(8,128)(2,1)S(1)}, bf16[3328,256]{1,0:T(8,128)(2,1)}, bf16[256,1024]{1,0:T(8,128)(2,1)S(1)}, f32[256,256]{1,0:T(8,128)S(1)}, f32[8,128]{1,0:T(8,128)S(1)}) custom-call(s32[1]{0:T(128)} %bitcast.core, s32[10,256]{1,0:T(8,128)S(1)} %bitcast.26, s32[16,64]{1,0:T(8,128)S(1)} %bitcast.25, s32[1,64]{1,0:T(1,128)S(1)} %bitcast.28, ...), custom_call_target="tpu_custom_call" | custom-call | flops 1048576 | bytes 8388608 | tf_op jit(solution)/shard_map/count_rows/pallas_call | solution.py:49
  25.9 15.8 %all-to-all-done = bf16[64,8,640]{2,1,0:T(8,128)(2,1)S(1)} async-done(((bf16[64,8,640]{2,1,0:T(8,128)(2,1)}), bf16[64,8,640]{2,1,0:T(8,128)(2,1)S(1)}, u32[]{:S(2)}, u32[]{:S(2)}) %all-to-all-start) | async-done | bytes 655392 | tf_op jit(solution)/shard_map/all_to_all | solution.py:267
  41.8 0.1 own_hubs.1
  41.9 12.2 %all_to_all.25 = bf16[4,256,256]{2,1,0:T(8,128)(2,1)S(1)} all-to-all(bf16[4,256,256]{2,1,0:T(8,128)(2,1)S(1)} %bitcast.21), channel_id=1, replica_groups=mesh['x'=4,'core'=2,'y'=8,'z'=8] {'x'}, dimensions={0} | all-to-all | bytes 1048576 | tf_op jit(solution)/shard_map/all_to_all | solution.py:267
  54.0 1.9 %collective-permute-start = (bf16[1024,256]{1,0:T(8,128)(2,1)S(1)}, bf16[1024,256]{1,0:T(8,128)(2,1)S(1)}, u32[]{:S(2)}, u32[]{:S(2)}) collective-permute-start(bf16[1024,256]{1,0:T(8,128)(2,1)S(1)} %bitcast.19), channel_id=1, source_target_pairs={{0,64},{64,0},{1,65},{65,1},{2,66},{66,2},{3,67},{67,3},{4,68},{68... | collective-permute-start | bytes 1572872 | tf_op jit(solution)/shard_map/ppermute | solution.py:296
  56.0 0.0 copy-start.3
  56.0 0.0 copy-start.4
  56.0 1.1 near_sum.1
  57.1 0.7 collective-permute-done.other
  57.8 0.0 copy-done.3
  57.8 0.0 copy-done.4
  57.8 1.9 %forward.1 = (bf16[512,768]{1,0:T(8,128)(2,1)}, bf16[512,256]{1,0:T(8,128)(2,1)}) custom-call(bf16[256,3328]{1,0:T(8,128)(2,1)S(1)} %get-tuple-element.18.counts, bf16[1024,256]{1,0:T(8,128)(2,1)S(1)} %get-tuple-element.21.back, bf16[256,256]{1,0:T(8,128)(2,1)S(1)} %copy-done, f32[256,256]{1,0:T(8,128)S(1)} %get-tuple-element.22.near, ...), custom_call_target="tpu_custom_call" | custom-call | flops 1048576 | bytes 8388608 | tf_op jit(solution)/shard_map/forward/pallas_call | solution.py:49
  59.8 0.0 copy-start.1
  59.8 6.6 %all-to-all-start.2 = ((bf16[64,8,768]{2,1,0:T(8,128)(2,1)}), bf16[64,8,768]{2,1,0:T(8,128)(2,1)S(1)}, u32[]{:S(2)}, u32[]{:S(2)}) async-start(bf16[64,8,768]{2,1,0:T(8,128)(2,1)} %bitcast.31), calls=%async_computation.2 | async-start | bytes 1572864 | tf_op jit(solution)/shard_map/all_to_all | solution.py:267
  66.4 0.0 copy-done.1
  66.4 1.3 %other_hubs.1 = bf16[1024,256]{1,0:T(8,128)(2,1)S(1)} custom-call(bf16[3328,256]{1,0:T(8,128)(2,1)} %get-tuple-element.19.counts_t, bf16[512,256]{1,0:T(8,128)(2,1)S(1)} %copy-done.1), custom_call_target="tpu_custom_call" | custom-call | flops 1048576 | bytes 8388608 | tf_op jit(solution)/shard_map/other_hubs/pallas_call | solution.py:49
  67.8 1.9 %collective-permute-start.1 = (bf16[1024,256]{1,0:T(8,128)(2,1)S(1)}, bf16[1024,256]{1,0:T(8,128)(2,1)S(1)}, u32[]{:S(2)}, u32[]{:S(2)}) collective-permute-start(bf16[1024,256]{1,0:T(8,128)(2,1)S(1)} %other_hubs.1), channel_id=1, source_target_pairs={{0,64},{64,0},{1,65},{65,1},{2,66},{66,2},{3,67},{67,3},{4,68},{68... | collective-permute-start | bytes 1572872 | tf_op jit(solution)/shard_map/ppermute | solution.py:315
  69.7 1.4 %mine_and_own.1 = (bf16[1024,256]{1,0:T(8,128)(2,1)S(1)}, f32[256,256]{1,0:T(8,128)S(1)}) custom-call(bf16[3328,256]{1,0:T(8,128)(2,1)} %get-tuple-element.19.counts_t, bf16[512,256]{1,0:T(8,128)(2,1)S(1)} %copy-done.1, bf16[256,256]{1,0:T(8,128)(2,1)S(1)} %copy-done.2), custom_call_target="tpu_custom_call" | custom-call | flops 1048576 | bytes 8388608 | tf_op jit(solution)/shard_map/mine_and_own/pallas_call | solution.py:49
  71.2 0.4 collective-permute-done.1.met
  71.6 0.1 pair_hubs.1
  71.7 2.5 %collective-permute-start.2 = (bf16[256,256]{1,0:T(8,128)(2,1)S(1)}, bf16[256,256]{1,0:T(8,128)(2,1)S(1)}, u32[]{:S(2)}, u32[]{:S(2)}) collective-permute-start(bf16[256,256]{1,0:T(8,128)(2,1)S(1)} %get-tuple-element.28), channel_id=1, source_target_pairs={{0,128},{128,256},{256,384},{384,0},{1,129},{129,257},{257,385},{3... | collective-permute-start | bytes 393224 | tf_op jit(solution)/shard_map/ppermute | solution.py:322
  74.2 4.0 %collective-permute-start.3 = (bf16[256,256]{1,0:T(8,128)(2,1)S(1)}, bf16[256,256]{1,0:T(8,128)(2,1)S(1)}, u32[]{:S(2)}, u32[]{:S(2)}) collective-permute-start(bf16[256,256]{1,0:T(8,128)(2,1)S(1)} %get-tuple-element.29), channel_id=1, source_target_pairs={{0,256},{128,384},{256,0},{384,128},{1,257},{129,385},{257,1},{385... | collective-permute-start | bytes 393224 | tf_op jit(solution)/shard_map/ppermute | solution.py:322
  78.2 2.7 %collective-permute-start.4 = (bf16[256,256]{1,0:T(8,128)(2,1)S(1)}, bf16[256,256]{1,0:T(8,128)(2,1)S(1)}, u32[]{:S(2)}, u32[]{:S(2)}) collective-permute-start(bf16[256,256]{1,0:T(8,128)(2,1)S(1)} %get-tuple-element.30), channel_id=1, source_target_pairs={{0,384},{128,0},{256,128},{384,256},{1,385},{129,1},{257,129},{385... | collective-permute-start | bytes 393224 | tf_op jit(solution)/shard_map/ppermute | solution.py:322
  80.9 10.6 %all-to-all-done.2 = bf16[64,8,768]{2,1,0:T(8,128)(2,1)S(1)} async-done(((bf16[64,8,768]{2,1,0:T(8,128)(2,1)}), bf16[64,8,768]{2,1,0:T(8,128)(2,1)S(1)}, u32[]{:S(2)}, u32[]{:S(2)}) %all-to-all-start.2) | async-done | bytes 786464 | tf_op jit(solution)/shard_map/all_to_all | solution.py:267
  91.6 0.7 sum_weights.1
  92.2 3.3 %all-to-all-start.3 = ((bf16[8,8,256]{2,1,0:T(8,128)(2,1)}), bf16[8,8,256]{2,1,0:T(8,128)(2,1)S(1)}, u32[]{:S(2)}, u32[]{:S(2)}) async-start(bf16[8,8,256]{2,1,0:T(8,128)(2,1)} %bitcast.10), calls=%async_computation.3 | async-start | bytes 65536 | tf_op jit(solution)/shard_map/all_to_all | solution.py:267
  95.6 0.0 collective-permute-done.2.a
  95.6 0.0 collective-permute-done.3.b
  95.6 0.0 collective-permute-done.4.c
  95.6 0.8 sum_hubs.1.hubs
  96.4 4.6 %all-to-all-done.3 = bf16[8,8,256]{2,1,0:T(8,128)(2,1)S(1)} async-done(((bf16[8,8,256]{2,1,0:T(8,128)(2,1)}), bf16[8,8,256]{2,1,0:T(8,128)(2,1)S(1)}, u32[]{:S(2)}, u32[]{:S(2)}) %all-to-all-start.3) | async-done | bytes 32800 | tf_op jit(solution)/shard_map/all_to_all | solution.py:267
  101.0 0.0 copy-start.8
  101.0 0.7 last_message.1
  101.7 5.5 %all-to-all-start.4 = ((bf16[64,8,384]{2,1,0:T(8,128)(2,1)}), bf16[64,8,384]{2,1,0:T(8,128)(2,1)S(1)}, u32[]{:S(2)}, u32[]{:S(2)}) async-start(bf16[64,8,384]{2,1,0:T(8,128)(2,1)} %bitcast.30), calls=%async_computation.4 | async-start | bytes 786432 | tf_op jit(solution)/shard_map/all_to_all | solution.py:267
  107.2 0.3 add_returned.1.partial
  107.5 16.3 %all-to-all-done.4 = bf16[64,8,384]{2,1,0:T(8,128)(2,1)S(1)} async-done(((bf16[64,8,384]{2,1,0:T(8,128)(2,1)}), bf16[64,8,384]{2,1,0:T(8,128)(2,1)S(1)}, u32[]{:S(2)}, u32[]{:S(2)}) %all-to-all-start.4) | async-done | bytes 393248 | tf_op jit(solution)/shard_map/all_to_all | solution.py:267
  123.8 0.0 copy-done.8
  123.8 0.9 finish.1
Async XLA Ops:
  0.6 18.9 %copy-start = (bf16[256,256]{1,0:T(8,128)(2,1)S(1)}, bf16[256,256]{1,0:T(8,128)(2,1)}, u32[]{:S(2)}) copy-start(bf16[256,256]{1,0:T(8,128)(2,1)} %features.7) | copy-start | bytes 393220
  0.6 18.9 %copy-start.7 = (s32[64]{0:T(128)S(1)}, s32[64]{0:T(128)}, u32[]{:S(2)}) copy-start(s32[64]{0:T(128)} %param.11) | copy-start | bytes 772
  0.7 18.9 %copy-start.5 = (s32[64,16]{0,1:T(8,128)S(1)}, s32[64,16]{0,1:T(8,128)}, u32[]{:S(2)}) copy-start(s32[64,16]{0,1:T(8,128)} %param.10) | copy-start | bytes 12292
  0.7 18.9 %copy-start.2 = (bf16[256,256]{1,0:T(8,128)(2,1)S(1)}, bf16[256,256]{1,0:T(8,128)(2,1)}, u32[]{:S(2)}) copy-start(bf16[256,256]{1,0:T(8,128)(2,1)} %w_self.3) | copy-start | bytes 393220
  0.7 18.9 %copy-start.6 = (s32[256,10]{0,1:T(8,128)S(1)}, s32[256,10]{0,1:T(8,128)}, u32[]{:S(2)}) copy-start(s32[256,10]{0,1:T(8,128)} %param.9) | copy-start | bytes 30724
  3.1 38.7 %all-to-all-start = ((bf16[64,8,640]{2,1,0:T(8,128)(2,1)}), bf16[64,8,640]{2,1,0:T(8,128)(2,1)S(1)}, u32[]{:S(2)}, u32[]{:S(2)}) async-start(bf16[64,8,640]{2,1,0:T(8,128)(2,1)} %bitcast.29), calls=%async_computation | async-start | bytes 1310720 | tf_op jit(solution)/shard_map/all_to_all | solution.py:267
  54.0 3.8 %collective-permute-start = (bf16[1024,256]{1,0:T(8,128)(2,1)S(1)}, bf16[1024,256]{1,0:T(8,128)(2,1)S(1)}, u32[]{:S(2)}, u32[]{:S(2)}) collective-permute-start(bf16[1024,256]{1,0:T(8,128)(2,1)S(1)} %bitcast.19), channel_id=1, source_target_pairs={{0,64},{64,0},{1,65},{65,1},{2,66},{66,2},{3,67},{67,3},{4,68},{68... | collective-permute-start | bytes 1572872 | tf_op jit(solution)/shard_map/ppermute | solution.py:296
  56.0 1.9 %copy-start.3 = (bf16[256,256]{1,0:T(8,128)(2,1)S(1)}, bf16[256,256]{1,0:T(8,128)(2,1)}, u32[]{:S(2)}) copy-start(bf16[256,256]{1,0:T(8,128)(2,1)} %w_nbr.1) | copy-start | bytes 393220
  56.0 1.9 %copy-start.4 = (bf16[256,256]{1,0:T(8,128)(2,1)S(1)}, bf16[256,256]{1,0:T(8,128)(2,1)}, u32[]{:S(2)}) copy-start(bf16[256,256]{1,0:T(8,128)(2,1)} %cotangent.1) | copy-start | bytes 393220
  59.8 6.7 %copy-start.1 = (bf16[512,256]{1,0:T(8,128)(2,1)S(1)}, bf16[512,256]{1,0:T(8,128)(2,1)}, u32[]{:S(2)}) copy-start(bf16[512,256]{1,0:T(8,128)(2,1)} %get-tuple-element.25.both) | copy-start | bytes 786436
  59.8 31.8 %all-to-all-start.2 = ((bf16[64,8,768]{2,1,0:T(8,128)(2,1)}), bf16[64,8,768]{2,1,0:T(8,128)(2,1)S(1)}, u32[]{:S(2)}, u32[]{:S(2)}) async-start(bf16[64,8,768]{2,1,0:T(8,128)(2,1)} %bitcast.31), calls=%async_computation.2 | async-start | bytes 1572864 | tf_op jit(solution)/shard_map/all_to_all | solution.py:267
  67.8 3.8 %collective-permute-start.1 = (bf16[1024,256]{1,0:T(8,128)(2,1)S(1)}, bf16[1024,256]{1,0:T(8,128)(2,1)S(1)}, u32[]{:S(2)}, u32[]{:S(2)}) collective-permute-start(bf16[1024,256]{1,0:T(8,128)(2,1)S(1)} %other_hubs.1), channel_id=1, source_target_pairs={{0,64},{64,0},{1,65},{65,1},{2,66},{66,2},{3,67},{67,3},{4,68},{68... | collective-permute-start | bytes 1572872 | tf_op jit(solution)/shard_map/ppermute | solution.py:315
  71.7 23.9 %collective-permute-start.2 = (bf16[256,256]{1,0:T(8,128)(2,1)S(1)}, bf16[256,256]{1,0:T(8,128)(2,1)S(1)}, u32[]{:S(2)}, u32[]{:S(2)}) collective-permute-start(bf16[256,256]{1,0:T(8,128)(2,1)S(1)} %get-tuple-element.28), channel_id=1, source_target_pairs={{0,128},{128,256},{256,384},{384,0},{1,129},{129,257},{257,385},{3... | collective-permute-start | bytes 393224 | tf_op jit(solution)/shard_map/ppermute | solution.py:322
  74.2 21.4 %collective-permute-start.3 = (bf16[256,256]{1,0:T(8,128)(2,1)S(1)}, bf16[256,256]{1,0:T(8,128)(2,1)S(1)}, u32[]{:S(2)}, u32[]{:S(2)}) collective-permute-start(bf16[256,256]{1,0:T(8,128)(2,1)S(1)} %get-tuple-element.29), channel_id=1, source_target_pairs={{0,256},{128,384},{256,0},{384,128},{1,257},{129,385},{257,1},{385... | collective-permute-start | bytes 393224 | tf_op jit(solution)/shard_map/ppermute | solution.py:322
  78.2 17.5 %collective-permute-start.4 = (bf16[256,256]{1,0:T(8,128)(2,1)S(1)}, bf16[256,256]{1,0:T(8,128)(2,1)S(1)}, u32[]{:S(2)}, u32[]{:S(2)}) collective-permute-start(bf16[256,256]{1,0:T(8,128)(2,1)S(1)} %get-tuple-element.30), channel_id=1, source_target_pairs={{0,384},{128,0},{256,128},{384,256},{1,385},{129,1},{257,129},{385... | collective-permute-start | bytes 393224 | tf_op jit(solution)/shard_map/ppermute | solution.py:322
  92.2 8.7 %all-to-all-start.3 = ((bf16[8,8,256]{2,1,0:T(8,128)(2,1)}), bf16[8,8,256]{2,1,0:T(8,128)(2,1)S(1)}, u32[]{:S(2)}, u32[]{:S(2)}) async-start(bf16[8,8,256]{2,1,0:T(8,128)(2,1)} %bitcast.10), calls=%async_computation.3 | async-start | bytes 65536 | tf_op jit(solution)/shard_map/all_to_all | solution.py:267
  101.0 22.8 %copy-start.8 = (s32[1,4]{1,0:T(1,128)S(1)}, s32[1,4]{1,0:T(1,128)}, u32[]{:S(2)}) copy-start(s32[1,4]{1,0:T(1,128)} %hub.3) | copy-start | bytes 52
  101.7 22.1 %all-to-all-start.4 = ((bf16[64,8,384]{2,1,0:T(8,128)(2,1)}), bf16[64,8,384]{2,1,0:T(8,128)(2,1)S(1)}, u32[]{:S(2)}, u32[]{:S(2)}) async-start(bf16[64,8,384]{2,1,0:T(8,128)(2,1)} %bitcast.30), calls=%async_computation.4 | async-start | bytes 786432 | tf_op jit(solution)/shard_map/all_to_all | solution.py:267

commit v6 on v5

--- a/solution.py
+++ b/solution.py
@@ -44,7 +44,7 @@
     return jnp.dot(a, b, preferred_element_type=F32)
 
 
-def call(body, name, outs, flops, moved, *args, kept=(), smem=(), unread=(), to_hbm=(), scratch=(), alias={}):
+def call(body, name, outs, flops, moved, *args, kept=(), smem=(), unread=(), to_hbm=(), scratch=()):
     places = [HBM if i in kept else SMEM if i in smem else ANY if i in unread else VMEM for i in range(len(args))]
     return pl.pallas_call(
         body,
@@ -53,7 +53,6 @@
         in_specs=places,
         out_specs=[HBM if i in to_hbm else VMEM for i in range(len(outs))],
         scratch_shapes=list(scratch),
-        input_output_aliases=alias,
         compiler_params=pltpu.CompilerParams(vmem_limit_bytes=16 * 1024 * 1024),
         cost_estimate=pl.CostEstimate(flops=flops, bytes_accessed=moved, transcendentals=0),
     )(*[pltpu.with_memory_space_constraint(a, pltpu.HBM) if i in kept else a for i, a in enumerate(args)])
@@ -175,12 +174,15 @@
         out[x * 256 : (x + 1) * 256, 128:] = right
 
 
-def near_sum(counts, counts_t, features, incoming, mine, out, back, sems):
-    fetch = send([counts_t.at[NODES:BORDER, :]], [back], sems)
+def border_sum(counts, features, incoming, out):
     total = dot(counts[:, :NODES], features[...])
     total += dot(counts[:, NODES : NODES + HALF], incoming[:, :D])
-    total += dot(counts[:, NODES + HALF : BORDER], incoming[:, D : 2 * D])
-    out[...] = total + dot(counts[:, BORDER : BORDER + SIDE], mine[...])
+    out[...] = total + dot(counts[:, NODES + HALF : BORDER], incoming[:, D : 2 * D])
+
+
+def near_sum(counts, counts_t, border, mine, out, back, sems):
+    fetch = send([counts_t.at[NODES:BORDER, :]], [back], sems)
+    out[...] = border[...] + dot(counts[:, BORDER : BORDER + SIDE], mine[...])
     finished(fetch)
 
 
@@ -226,10 +228,9 @@
         out[...] = (hubs[rows, :].astype(F32) + met[rows, :].astype(F32)).astype(BF)
 
 
-def sum_hubs(kept, a, b, c, message, tiles, sems):
+def sum_hubs(kept, a, b, c, out):
     total = kept[...].astype(F32) + a[...].astype(F32) + b[...].astype(F32) + c[...].astype(F32)
-    tiles[...] = split_rows(total).reshape(HALF, 128).astype(BF)
-    finished(send([tiles], [message.at[:, D:]], sems))
+    out[...] = split_rows(total).reshape(HALF, 128).astype(BF)
 
 
 def sum_weights(returned, out):
@@ -242,10 +243,10 @@
     out[...] = total + dot(home[:, HALF:], returned[:, D : 2 * D])
 
 
-def last_message(weights, hubs, message, rows, sems):
+def last_message(weights, hubs, after, out):
     total = jnp.sum(weights[...].astype(F32).reshape(GROUPS, 8, D), axis=0) * SCALE
-    rows[...] = jnp.broadcast_to(total[None], (MEMBERS, 8, D)).reshape(HALF, D).astype(BF)
-    finished(send([rows], [message.at[:, :D]], sems))
+    out[:, :D] = jnp.broadcast_to(total[None], (MEMBERS, 8, D)).reshape(HALF, D).astype(BF)
+    out[:, D:] = hubs[...]
 
 
 def finish(hub, last, partial, grad_self, grad_nbr, grad, weights_v, grad_v, sems):
@@ -294,9 +295,10 @@
     mine = exchange(mine, "x", XS)
     swap = [(0, 1), (1, 0)]
     other = lax.ppermute(mine, "core", swap)
+    (border,) = call(border_sum, "border_sum", [((NODES, D), F32)], 2**20, 2**23, counts, features, incoming)
     near, back = call(
         near_sum, "near_sum", [((NODES, D), F32), ((2 * HALF, NODES), BF)], 2**20, 2**23,
-        counts, counts_t, features, incoming, mine,
+        counts, counts_t, border, mine,
         kept=(1,), scratch=[pltpu.SemaphoreType.DMA((1,))],
     )
     outward, both = call(
@@ -320,16 +322,13 @@
     block = ((NODES, D), BF)
     kept, *to = call(pair_hubs, "pair_hubs", [block] * XS, 2**20, 2**23, x, hubs, met, smem=(0,))
     came = [lax.ppermute(to[k - 1], "x", [(i, (i + k) % XS) for i in range(XS)]) for k in range(1, XS)]
-    (hub_tiles,) = call(
-        sum_hubs, "sum_hubs", [((HALF, 384), BF)], 2**20, 2**23, kept, *came,
-        to_hbm=(0,), scratch=[pltpu.VMEM((HALF, 128), BF), pltpu.SemaphoreType.DMA((1,))],
-    )
+    (hub_tiles,) = call(sum_hubs, "sum_hubs", [((HALF, 128), BF)], 2**20, 2**23, kept, *came)
+
     (weights,) = call(sum_weights, "sum_weights", [((GROUPS * 8, D), BF)], 2**20, 2**23, returned)
     weights = exchange(weights, GROUP, GROUPS)
     (partial,) = call(add_returned, "add_returned", [((NODES, D), F32)], 2**20, 2**23, returned, home, own)
     (message,) = call(
-        last_message, "last_message", [((HALF, 384), BF)], 2**20, 2**23, weights, hub_tiles,
-        kept=(1,), to_hbm=(0,), alias={1: 0}, scratch=[pltpu.VMEM((HALF, D), BF), pltpu.SemaphoreType.DMA((1,))],
+        last_message, "last_message", [((HALF, 384), BF)], 2**20, 2**23, weights, hub_tiles, partial, unread=(2,)
     )
     last = exchange(message, MEMBER, MEMBERS)
     return tuple(

time: 125 us -> 124 us (level)
  blocking collectives: 12.2 us -> 34 us
  waiting for transfers between devices: 48.5 us -> 32.2 us
  starting transfers between devices: 44.9 us -> 39.5 us
    all_to_all x1 -> x2, blocking collectives: 12.2 us -> 34 us  [exchange(): lax.all_to_all(block, axes, split_axis=0, concat_axis=0, tiled=True)]
    all_to_all x4 -> x3, waiting for transfers between devices: 47.3 us -> 31.4 us  [exchange(): lax.all_to_all(block, axes, split_axis=0, concat_axis=0, tiled=True)]
    all_to_all x4 -> x3, starting transfers between devices: 31.9 us -> 26.5 us  [exchange(): lax.all_to_all(block, axes, split_axis=0, concat_axis=0, tiled=True)]
    pallas_call x13 -> x14, Pallas kernels: 18.1 us -> 17.1 us  [call(): pl.pallas_call(body, name=name, out_shape=[(pltpu.HBM if i in to_hbm else...]
  transfers between devices with their start and end apart: 9 -> 8, of which waited for: 6 -> 5; matrix products, arithmetic and copies ran while one was open for 0% -> 0% of each run, Pallas kernels for 10% -> 10%
where the time goes in v6:
time: 124 us
  starting transfers between devices  39.5 us (32%)
  blocking collectives  34 us (27%)
  waiting for transfers between devices  32.2 us (26%)
  Pallas kernels  17.1 us (14%)
    all_to_all x2, blocking collectives, exchange(): lax.all_to_all(block, axes, split_axis=0, concat_axis=0, tiled=True)  34 us
    all_to_all x3, waiting for transfers between devices, exchange(): lax.all_to_all(block, axes, split_axis=0, concat_axis=0, tiled=True)  31.4 us
    all_to_all x3, starting transfers between devices, exchange(): lax.all_to_all(block, axes, split_axis=0, concat_axis=0, tiled=True)  26.5 us
    pallas_call x14, Pallas kernels, call(): pl.pallas_call(body, name=name, out_shape=[(pltpu.HBM if i in to_hbm else...  17.1 us
    ppermute x3, starting transfers between devices, local(): lax.ppermute(to[k - 1], 'x', [(i, (i + k) % XS) for i in range(XS)])  9.17 us
  transfers between devices with their start and end apart: 8, of which 5 were waited for; matrix products, arithmetic and copies ran while one was open for 0% of the time, Pallas kernels for 10%

profile of v6, /device:TPU:16, one launch (start us, length us, event | category | flops | bytes accessed | tf_op | source)
XLA Modules:
  0.0 123.8 jit_solution(5392060365217849911)
XLA Ops:
  0.6 0.0 copy-start
  0.6 0.0 copy-start.7
  0.7 0.0 copy-start.5
  0.7 0.0 copy-start.2
  0.7 0.0 copy-start.6
  0.7 2.4 %outgoing_rows.1.after = bf16[512,640]{1,0:T(8,128)(2,1)} custom-call(s32[1,4]{1,0:T(1,128)} %hub.3, s32[16,64]{1,0:T(8,128)} %bitcast.25, s32[1,64]{1,0:T(1,128)} %bitcast.28, bf16[256,256]{1,0:T(8,128)(2,1)} %features.7), custom_call_target="tpu_custom_call" | custom-call | flops 1048576 | bytes 8388608 | tf_op jit(solution)/shard_map/outgoing_rows/pallas_call | solution.py:49
  3.1 16.5 %all-to-all-start = ((bf16[64,8,640]{2,1,0:T(8,128)(2,1)}), bf16[64,8,640]{2,1,0:T(8,128)(2,1)S(1)}, u32[]{:S(2)}, u32[]{:S(2)}) async-start(bf16[64,8,640]{2,1,0:T(8,128)(2,1)} %bitcast.30), calls=%async_computation | async-start | bytes 1310720 | tf_op jit(solution)/shard_map/all_to_all | solution.py:268
  19.6 0.0 copy-done
  19.6 0.0 copy-done.7
  19.6 0.0 copy-done.5
  19.6 0.0 copy-done.2
  19.6 0.0 copy-done.6
  19.6 6.3 %count_rows.1 = (bf16[256,3328]{1,0:T(8,128)(2,1)S(1)}, bf16[3328,256]{1,0:T(8,128)(2,1)}, bf16[256,1024]{1,0:T(8,128)(2,1)S(1)}, f32[256,256]{1,0:T(8,128)S(1)}, f32[8,128]{1,0:T(8,128)S(1)}) custom-call(s32[1]{0:T(128)} %bitcast.core, s32[10,256]{1,0:T(8,128)S(1)} %bitcast.27, s32[16,64]{1,0:T(8,128)S(1)} %bitcast.26, s32[1,64]{1,0:T(1,128)S(1)} %bitcast.29, ...), custom_call_target="tpu_custom_call" | custom-call | flops 1048576 | bytes 8388608 | tf_op jit(solution)/shard_map/count_rows/pallas_call | solution.py:49
  25.9 15.8 %all-to-all-done = bf16[64,8,640]{2,1,0:T(8,128)(2,1)S(1)} async-done(((bf16[64,8,640]{2,1,0:T(8,128)(2,1)}), bf16[64,8,640]{2,1,0:T(8,128)(2,1)S(1)}, u32[]{:S(2)}, u32[]{:S(2)}) %all-to-all-start) | async-done | bytes 655392 | tf_op jit(solution)/shard_map/all_to_all | solution.py:268
  41.8 0.1 own_hubs.1
  41.9 12.2 %all_to_all.25 = bf16[4,256,256]{2,1,0:T(8,128)(2,1)S(1)} all-to-all(bf16[4,256,256]{2,1,0:T(8,128)(2,1)S(1)} %bitcast.19), channel_id=1, replica_groups=mesh['x'=4,'core'=2,'y'=8,'z'=8] {'x'}, dimensions={0} | all-to-all | bytes 1048576 | tf_op jit(solution)/shard_map/all_to_all | solution.py:268
  54.0 1.9 %collective-permute-start = (bf16[1024,256]{1,0:T(8,128)(2,1)S(1)}, bf16[1024,256]{1,0:T(8,128)(2,1)S(1)}, u32[]{:S(2)}, u32[]{:S(2)}) collective-permute-start(bf16[1024,256]{1,0:T(8,128)(2,1)S(1)} %bitcast.20), channel_id=1, source_target_pairs={{0,64},{64,0},{1,65},{65,1},{2,66},{66,2},{3,67},{67,3},{4,68},{68... | collective-permute-start | bytes 1572872 | tf_op jit(solution)/shard_map/ppermute | solution.py:297
  56.0 0.3 border_sum.1.border
  56.3 0.0 copy-start.3
  56.3 0.0 copy-start.4
  56.3 1.1 near_sum.1
  57.5 0.4 collective-permute-done.other
  57.8 0.0 copy-done.3
  57.8 0.0 copy-done.4
  57.8 1.9 %forward.1 = (bf16[512,768]{1,0:T(8,128)(2,1)}, bf16[512,256]{1,0:T(8,128)(2,1)}) custom-call(bf16[256,3328]{1,0:T(8,128)(2,1)S(1)} %get-tuple-element.18.counts, bf16[1024,256]{1,0:T(8,128)(2,1)S(1)} %get-tuple-element.21.back, bf16[256,256]{1,0:T(8,128)(2,1)S(1)} %copy-done, f32[256,256]{1,0:T(8,128)S(1)} %get-tuple-element.22.near, ...), custom_call_target="tpu_custom_call" | custom-call | flops 1048576 | bytes 8388608 | tf_op jit(solution)/shard_map/forward/pallas_call | solution.py:49
  59.8 0.0 copy-start.1
  59.8 6.6 %all-to-all-start.2 = ((bf16[64,8,768]{2,1,0:T(8,128)(2,1)}), bf16[64,8,768]{2,1,0:T(8,128)(2,1)S(1)}, u32[]{:S(2)}, u32[]{:S(2)}) async-start(bf16[64,8,768]{2,1,0:T(8,128)(2,1)} %bitcast.31), calls=%async_computation.2 | async-start | bytes 1572864 | tf_op jit(solution)/shard_map/all_to_all | solution.py:268
  66.4 0.0 copy-done.1
  66.4 1.3 %other_hubs.1 = bf16[1024,256]{1,0:T(8,128)(2,1)S(1)} custom-call(bf16[3328,256]{1,0:T(8,128)(2,1)} %get-tuple-element.19.counts_t, bf16[512,256]{1,0:T(8,128)(2,1)S(1)} %copy-done.1), custom_call_target="tpu_custom_call" | custom-call | flops 1048576 | bytes 8388608 | tf_op jit(solution)/shard_map/other_hubs/pallas_call | solution.py:49
  67.8 1.9 %collective-permute-start.1 = (bf16[1024,256]{1,0:T(8,128)(2,1)S(1)}, bf16[1024,256]{1,0:T(8,128)(2,1)S(1)}, u32[]{:S(2)}, u32[]{:S(2)}) collective-permute-start(bf16[1024,256]{1,0:T(8,128)(2,1)S(1)} %other_hubs.1), channel_id=1, source_target_pairs={{0,64},{64,0},{1,65},{65,1},{2,66},{66,2},{3,67},{67,3},{4,68},{68... | collective-permute-start | bytes 1572872 | tf_op jit(solution)/shard_map/ppermute | solution.py:317
  69.7 1.4 %mine_and_own.1 = (bf16[1024,256]{1,0:T(8,128)(2,1)S(1)}, f32[256,256]{1,0:T(8,128)S(1)}) custom-call(bf16[3328,256]{1,0:T(8,128)(2,1)} %get-tuple-element.19.counts_t, bf16[512,256]{1,0:T(8,128)(2,1)S(1)} %copy-done.1, bf16[256,256]{1,0:T(8,128)(2,1)S(1)} %copy-done.2), custom_call_target="tpu_custom_call" | custom-call | flops 1048576 | bytes 8388608 | tf_op jit(solution)/shard_map/mine_and_own/pallas_call | solution.py:49
  71.2 0.4 collective-permute-done.1.met
  71.6 0.1 pair_hubs.1
  71.7 2.5 %collective-permute-start.2 = (bf16[256,256]{1,0:T(8,128)(2,1)S(1)}, bf16[256,256]{1,0:T(8,128)(2,1)S(1)}, u32[]{:S(2)}, u32[]{:S(2)}) collective-permute-start(bf16[256,256]{1,0:T(8,128)(2,1)S(1)} %get-tuple-element.28), channel_id=1, source_target_pairs={{0,128},{128,256},{256,384},{384,0},{1,129},{129,257},{257,385},{3... | collective-permute-start | bytes 393224 | tf_op jit(solution)/shard_map/ppermute | solution.py:324
  74.2 4.0 %collective-permute-start.3 = (bf16[256,256]{1,0:T(8,128)(2,1)S(1)}, bf16[256,256]{1,0:T(8,128)(2,1)S(1)}, u32[]{:S(2)}, u32[]{:S(2)}) collective-permute-start(bf16[256,256]{1,0:T(8,128)(2,1)S(1)} %get-tuple-element.29), channel_id=1, source_target_pairs={{0,256},{128,384},{256,0},{384,128},{1,257},{129,385},{257,1},{385... | collective-permute-start | bytes 393224 | tf_op jit(solution)/shard_map/ppermute | solution.py:324
  78.2 2.7 %collective-permute-start.4 = (bf16[256,256]{1,0:T(8,128)(2,1)S(1)}, bf16[256,256]{1,0:T(8,128)(2,1)S(1)}, u32[]{:S(2)}, u32[]{:S(2)}) collective-permute-start(bf16[256,256]{1,0:T(8,128)(2,1)S(1)} %get-tuple-element.30), channel_id=1, source_target_pairs={{0,384},{128,0},{256,128},{384,256},{1,385},{129,1},{257,129},{385... | collective-permute-start | bytes 393224 | tf_op jit(solution)/shard_map/ppermute | solution.py:324
  80.9 10.7 %all-to-all-done.2 = bf16[64,8,768]{2,1,0:T(8,128)(2,1)S(1)} async-done(((bf16[64,8,768]{2,1,0:T(8,128)(2,1)}), bf16[64,8,768]{2,1,0:T(8,128)(2,1)S(1)}, u32[]{:S(2)}, u32[]{:S(2)}) %all-to-all-start.2) | async-done | bytes 786464 | tf_op jit(solution)/shard_map/all_to_all | solution.py:268
  91.6 0.7 sum_weights.1
  92.3 3.3 %all-to-all-start.3 = ((bf16[8,8,256]{2,1,0:T(8,128)(2,1)}), bf16[8,8,256]{2,1,0:T(8,128)(2,1)S(1)}, u32[]{:S(2)}, u32[]{:S(2)}) async-start(bf16[8,8,256]{2,1,0:T(8,128)(2,1)} %bitcast.10), calls=%async_computation.3 | async-start | bytes 65536 | tf_op jit(solution)/shard_map/all_to_all | solution.py:268
  95.6 0.0 collective-permute-done.2.a
  95.7 0.0 collective-permute-done.3.b
  95.7 0.0 collective-permute-done.4.c
  95.7 0.1 sum_hubs.1.hubs
  95.8 0.0 copy-start.8
  95.8 0.3 add_returned.1.after.partial
  96.1 4.9 %all-to-all-done.3 = bf16[8,8,256]{2,1,0:T(8,128)(2,1)S(1)} async-done(((bf16[8,8,256]{2,1,0:T(8,128)(2,1)}), bf16[8,8,256]{2,1,0:T(8,128)(2,1)S(1)}, u32[]{:S(2)}, u32[]{:S(2)}) %all-to-all-start.3) | async-done | bytes 32800 | tf_op jit(solution)/shard_map/all_to_all | solution.py:268
  101.1 21.8 %all_to_all.26 = bf16[64,8,384]{2,1,0:T(8,128)(2,1)S(1)} all-to-all(bf16[64,8,384]{2,1,0:T(8,128)(2,1)S(1)} %bitcast.23), channel_id=1, replica_groups=mesh['x'=4,'core'=2,'y'=8,'z'=8] {'y','z'}, dimensions={0} | all-to-all | bytes 786432 | tf_op jit(solution)/shard_map/all_to_all | solution.py:268
  122.9 0.0 copy-done.8
  122.9 0.9 finish.1
  (1 shorter events, 0.0 us)
Async XLA Ops:
  0.6 18.9 %copy-start = (bf16[256,256]{1,0:T(8,128)(2,1)S(1)}, bf16[256,256]{1,0:T(8,128)(2,1)}, u32[]{:S(2)}) copy-start(bf16[256,256]{1,0:T(8,128)(2,1)} %features.7) | copy-start | bytes 393220
  0.6 18.9 %copy-start.7 = (s32[64]{0:T(128)S(1)}, s32[64]{0:T(128)}, u32[]{:S(2)}) copy-start(s32[64]{0:T(128)} %param.11) | copy-start | bytes 772
  0.7 18.9 %copy-start.5 = (s32[64,16]{0,1:T(8,128)S(1)}, s32[64,16]{0,1:T(8,128)}, u32[]{:S(2)}) copy-start(s32[64,16]{0,1:T(8,128)} %param.10) | copy-start | bytes 12292
  0.7 18.9 %copy-start.2 = (bf16[256,256]{1,0:T(8,128)(2,1)S(1)}, bf16[256,256]{1,0:T(8,128)(2,1)}, u32[]{:S(2)}) copy-start(bf16[256,256]{1,0:T(8,128)(2,1)} %w_self.3) | copy-start | bytes 393220
  0.7 18.9 %copy-start.6 = (s32[256,10]{0,1:T(8,128)S(1)}, s32[256,10]{0,1:T(8,128)}, u32[]{:S(2)}) copy-start(s32[256,10]{0,1:T(8,128)} %param.9) | copy-start | bytes 30724
  3.1 38.7 %all-to-all-start = ((bf16[64,8,640]{2,1,0:T(8,128)(2,1)}), bf16[64,8,640]{2,1,0:T(8,128)(2,1)S(1)}, u32[]{:S(2)}, u32[]{:S(2)}) async-start(bf16[64,8,640]{2,1,0:T(8,128)(2,1)} %bitcast.30), calls=%async_computation | async-start | bytes 1310720 | tf_op jit(solution)/shard_map/all_to_all | solution.py:268
  54.0 3.8 %collective-permute-start = (bf16[1024,256]{1,0:T(8,128)(2,1)S(1)}, bf16[1024,256]{1,0:T(8,128)(2,1)S(1)}, u32[]{:S(2)}, u32[]{:S(2)}) collective-permute-start(bf16[1024,256]{1,0:T(8,128)(2,1)S(1)} %bitcast.20), channel_id=1, source_target_pairs={{0,64},{64,0},{1,65},{65,1},{2,66},{66,2},{3,67},{67,3},{4,68},{68... | collective-permute-start | bytes 1572872 | tf_op jit(solution)/shard_map/ppermute | solution.py:297
  56.3 1.5 %copy-start.3 = (bf16[256,256]{1,0:T(8,128)(2,1)S(1)}, bf16[256,256]{1,0:T(8,128)(2,1)}, u32[]{:S(2)}) copy-start(bf16[256,256]{1,0:T(8,128)(2,1)} %w_nbr.1) | copy-start | bytes 393220
  56.3 1.5 %copy-start.4 = (bf16[256,256]{1,0:T(8,128)(2,1)S(1)}, bf16[256,256]{1,0:T(8,128)(2,1)}, u32[]{:S(2)}) copy-start(bf16[256,256]{1,0:T(8,128)(2,1)} %cotangent.1) | copy-start | bytes 393220
  59.8 6.7 %copy-start.1 = (bf16[512,256]{1,0:T(8,128)(2,1)S(1)}, bf16[512,256]{1,0:T(8,128)(2,1)}, u32[]{:S(2)}) copy-start(bf16[512,256]{1,0:T(8,128)(2,1)} %get-tuple-element.25.both) | copy-start | bytes 786436
  59.8 31.8 %all-to-all-start.2 = ((bf16[64,8,768]{2,1,0:T(8,128)(2,1)}), bf16[64,8,768]{2,1,0:T(8,128)(2,1)S(1)}, u32[]{:S(2)}, u32[]{:S(2)}) async-start(bf16[64,8,768]{2,1,0:T(8,128)(2,1)} %bitcast.31), calls=%async_computation.2 | async-start | bytes 1572864 | tf_op jit(solution)/shard_map/all_to_all | solution.py:268
  67.8 3.8 %collective-permute-start.1 = (bf16[1024,256]{1,0:T(8,128)(2,1)S(1)}, bf16[1024,256]{1,0:T(8,128)(2,1)S(1)}, u32[]{:S(2)}, u32[]{:S(2)}) collective-permute-start(bf16[1024,256]{1,0:T(8,128)(2,1)S(1)} %other_hubs.1), channel_id=1, source_target_pairs={{0,64},{64,0},{1,65},{65,1},{2,66},{66,2},{3,67},{67,3},{4,68},{68... | collective-permute-start | bytes 1572872 | tf_op jit(solution)/shard_map/ppermute | solution.py:317
  71.7 23.9 %collective-permute-start.2 = (bf16[256,256]{1,0:T(8,128)(2,1)S(1)}, bf16[256,256]{1,0:T(8,128)(2,1)S(1)}, u32[]{:S(2)}, u32[]{:S(2)}) collective-permute-start(bf16[256,256]{1,0:T(8,128)(2,1)S(1)} %get-tuple-element.28), channel_id=1, source_target_pairs={{0,128},{128,256},{256,384},{384,0},{1,129},{129,257},{257,385},{3... | collective-permute-start | bytes 393224 | tf_op jit(solution)/shard_map/ppermute | solution.py:324
  74.2 21.4 %collective-permute-start.3 = (bf16[256,256]{1,0:T(8,128)(2,1)S(1)}, bf16[256,256]{1,0:T(8,128)(2,1)S(1)}, u32[]{:S(2)}, u32[]{:S(2)}) collective-permute-start(bf16[256,256]{1,0:T(8,128)(2,1)S(1)} %get-tuple-element.29), channel_id=1, source_target_pairs={{0,256},{128,384},{256,0},{384,128},{1,257},{129,385},{257,1},{385... | collective-permute-start | bytes 393224 | tf_op jit(solution)/shard_map/ppermute | solution.py:324
  78.2 17.5 %collective-permute-start.4 = (bf16[256,256]{1,0:T(8,128)(2,1)S(1)}, bf16[256,256]{1,0:T(8,128)(2,1)S(1)}, u32[]{:S(2)}, u32[]{:S(2)}) collective-permute-start(bf16[256,256]{1,0:T(8,128)(2,1)S(1)} %get-tuple-element.30), channel_id=1, source_target_pairs={{0,384},{128,0},{256,128},{384,256},{1,385},{129,1},{257,129},{385... | collective-permute-start | bytes 393224 | tf_op jit(solution)/shard_map/ppermute | solution.py:324
  92.3 8.7 %all-to-all-start.3 = ((bf16[8,8,256]{2,1,0:T(8,128)(2,1)}), bf16[8,8,256]{2,1,0:T(8,128)(2,1)S(1)}, u32[]{:S(2)}, u32[]{:S(2)}) async-start(bf16[8,8,256]{2,1,0:T(8,128)(2,1)} %bitcast.10), calls=%async_computation.3 | async-start | bytes 65536 | tf_op jit(solution)/shard_map/all_to_all | solution.py:268
  95.8 27.1 %copy-start.8 = (s32[1,4]{1,0:T(1,128)S(1)}, s32[1,4]{1,0:T(1,128)}, u32[]{:S(2)}) copy-start(s32[1,4]{1,0:T(1,128)} %hub.3) | copy-start | bytes 52

commit v7 on v6

--- a/solution.py
+++ b/solution.py
@@ -63,6 +63,12 @@
     for copy in copies:
         copy.start()
     return copies
+
+
+def send_rows_out(source, target, sems, first, parts):
+    rows = source.shape[0] // parts
+    cuts = [slice(i * rows, (i + 1) * rows) for i in range(parts)]
+    return send([source.at[c, :] for c in cuts], [target.at[c, :] for c in cuts], sems, first)
 
 
 def finished(copies):
@@ -127,7 +133,7 @@
     for a in range(2):
         lanes = slice(a * D, (a + 1) * D)
         out_v[:, lanes] = dot(hot[a], f).astype(BF)
-        copies += send([out_v.at[:, lanes]], [out.at[:, lanes]], sems, 5 + a)
+        copies += send_rows_out(out_v.at[:, lanes], out.at[:, lanes], sems, 5 + 4 * a, 4)
     finished(copies)
 
 
@@ -200,10 +206,10 @@
     copies = send([both_v], [both], sems)
     out_v[:, :D] = dot(back[:HALF, :], dagg).astype(BF)
     out_v[:, D : 2 * D] = dot(back[HALF:, :], dagg).astype(BF)
-    copies += send([out_v.at[:, : 2 * D]], [outward.at[:, : 2 * D]], sems, 1)
+    copies += send_rows_out(out_v.at[:, : 2 * D], outward.at[:, : 2 * D], sems, 1, 4)
     out_v[:D, 2 * D :] = lax.dot_general(features[...], dpre, OVER_ROWS, preferred_element_type=F32).astype(BF)
     out_v[D:, 2 * D :] = lax.dot_general(agg, dpre, OVER_ROWS, preferred_element_type=F32).astype(BF)
-    copies += send([out_v.at[:, 2 * D :]], [outward.at[:, 2 * D :]], sems, 2)
+    copies += send_rows_out(out_v.at[:, 2 * D :], outward.at[:, 2 * D :], sems, 5, 4)
     finished(copies)
 
 
@@ -280,7 +286,7 @@
         kept=range(4), to_hbm=(0,),
         scratch=[
             pltpu.VMEM((1, HUBS), I32), pltpu.VMEM((SLOTS, MEMBERS), I32), pltpu.VMEM((1, MEMBERS), I32),
-            pltpu.VMEM((NODES, D), BF), pltpu.VMEM((HALF, 640), BF), pltpu.SemaphoreType.DMA((7,)),
+            pltpu.VMEM((NODES, D), BF), pltpu.VMEM((HALF, 640), BF), pltpu.SemaphoreType.DMA((13,)),
         ],
     )
     incoming = exchange(outgoing, MEMBER, MEMBERS)
@@ -305,7 +311,7 @@
         forward, "forward", [((HALF, 768), BF), ((2 * NODES, D), BF)], 2**20, 2**23,
         counts, back, features, near, other, pre_self, w_nbr, cotangent,
         to_hbm=range(2),
-        scratch=[pltpu.VMEM((HALF, 768), BF), pltpu.VMEM((2 * NODES, D), BF), pltpu.SemaphoreType.DMA((3,))],
+        scratch=[pltpu.VMEM((HALF, 768), BF), pltpu.VMEM((2 * NODES, D), BF), pltpu.SemaphoreType.DMA((9,))],
     )
     returned = exchange(outward, MEMBER, MEMBERS)
 

time: 124 us -> 125 us (level)
  no operation moved by 1% of the time
where the time goes in v7:
time: 125 us; the launch traced here: 124 us
  starting transfers between devices  39.5 us (32%)
  blocking collectives  34 us (27%)
  waiting for transfers between devices  32.2 us (26%)
  Pallas kernels  17.2 us (14%)
    all_to_all x2, blocking collectives, exchange(): lax.all_to_all(block, axes, split_axis=0, concat_axis=0, tiled=True)  34 us
    all_to_all x3, waiting for transfers between devices, exchange(): lax.all_to_all(block, axes, split_axis=0, concat_axis=0, tiled=True)  31.4 us
    all_to_all x3, starting transfers between devices, exchange(): lax.all_to_all(block, axes, split_axis=0, concat_axis=0, tiled=True)  26.5 us
    pallas_call x14, Pallas kernels, call(): pl.pallas_call(body, name=name, out_shape=[(pltpu.HBM if i in to_hbm else...  17.2 us
    ppermute x3, starting transfers between devices, local(): lax.ppermute(to[k - 1], 'x', [(i, (i + k) % XS) for i in range(XS)])  9.18 us
  transfers between devices with their start and end apart: 8, of which 5 were waited for; matrix products, arithmetic and copies ran while one was open for 0% of the time, Pallas kernels for 10%

profile of v7, /device:TPU:16, one launch (start us, length us, event | category | flops | bytes accessed | tf_op | source)
XLA Modules:
  0.0 123.8 jit_solution(17461790050979046771)
XLA Ops:
  0.6 0.0 copy-start
  0.6 0.0 copy-start.7
  0.7 0.0 copy-start.5
  0.7 0.0 copy-start.2
  0.7 0.0 copy-start.6
  0.7 2.4 %outgoing_rows.1.after = bf16[512,640]{1,0:T(8,128)(2,1)} custom-call(s32[1,4]{1,0:T(1,128)} %hub.3, s32[16,64]{1,0:T(8,128)} %bitcast.25, s32[1,64]{1,0:T(1,128)} %bitcast.28, bf16[256,256]{1,0:T(8,128)(2,1)} %features.7), custom_call_target="tpu_custom_call" | custom-call | flops 1048576 | bytes 8388608 | tf_op jit(solution)/shard_map/outgoing_rows/pallas_call | solution.py:49
  3.1 16.5 %all-to-all-start = ((bf16[64,8,640]{2,1,0:T(8,128)(2,1)}), bf16[64,8,640]{2,1,0:T(8,128)(2,1)S(1)}, u32[]{:S(2)}, u32[]{:S(2)}) async-start(bf16[64,8,640]{2,1,0:T(8,128)(2,1)} %bitcast.30), calls=%async_computation | async-start | bytes 1310720 | tf_op jit(solution)/shard_map/all_to_all | solution.py:274
  19.6 0.0 copy-done
  19.6 0.0 copy-done.7
  19.6 0.0 copy-done.5
  19.7 0.0 copy-done.2
  19.7 0.0 copy-done.6
  19.7 6.3 %count_rows.1 = (bf16[256,3328]{1,0:T(8,128)(2,1)S(1)}, bf16[3328,256]{1,0:T(8,128)(2,1)}, bf16[256,1024]{1,0:T(8,128)(2,1)S(1)}, f32[256,256]{1,0:T(8,128)S(1)}, f32[8,128]{1,0:T(8,128)S(1)}) custom-call(s32[1]{0:T(128)} %bitcast.core, s32[10,256]{1,0:T(8,128)S(1)} %bitcast.27, s32[16,64]{1,0:T(8,128)S(1)} %bitcast.26, s32[1,64]{1,0:T(1,128)S(1)} %bitcast.29, ...), custom_call_target="tpu_custom_call" | custom-call | flops 1048576 | bytes 8388608 | tf_op jit(solution)/shard_map/count_rows/pallas_call | solution.py:49
  26.0 15.8 %all-to-all-done = bf16[64,8,640]{2,1,0:T(8,128)(2,1)S(1)} async-done(((bf16[64,8,640]{2,1,0:T(8,128)(2,1)}), bf16[64,8,640]{2,1,0:T(8,128)(2,1)S(1)}, u32[]{:S(2)}, u32[]{:S(2)}) %all-to-all-start) | async-done | bytes 655392 | tf_op jit(solution)/shard_map/all_to_all | solution.py:274
  41.8 0.1 own_hubs.1
  41.9 12.2 %all_to_all.25 = bf16[4,256,256]{2,1,0:T(8,128)(2,1)S(1)} all-to-all(bf16[4,256,256]{2,1,0:T(8,128)(2,1)S(1)} %bitcast.19), channel_id=1, replica_groups=mesh['x'=4,'core'=2,'y'=8,'z'=8] {'x'}, dimensions={0} | all-to-all | bytes 1048576 | tf_op jit(solution)/shard_map/all_to_all | solution.py:274
  54.1 1.9 %collective-permute-start = (bf16[1024,256]{1,0:T(8,128)(2,1)S(1)}, bf16[1024,256]{1,0:T(8,128)(2,1)S(1)}, u32[]{:S(2)}, u32[]{:S(2)}) collective-permute-start(bf16[1024,256]{1,0:T(8,128)(2,1)S(1)} %bitcast.20), channel_id=1, source_target_pairs={{0,64},{64,0},{1,65},{65,1},{2,66},{66,2},{3,67},{67,3},{4,68},{68... | collective-permute-start | bytes 1572872 | tf_op jit(solution)/shard_map/ppermute | solution.py:303
  56.0 0.3 border_sum.1.border
  56.4 0.0 copy-start.3
  56.4 0.0 copy-start.4
  56.4 1.1 near_sum.1
  57.5 0.4 collective-permute-done.other
  57.9 0.0 copy-done.3
  57.9 0.0 copy-done.4
  57.9 1.9 %forward.1 = (bf16[512,768]{1,0:T(8,128)(2,1)}, bf16[512,256]{1,0:T(8,128)(2,1)}) custom-call(bf16[256,3328]{1,0:T(8,128)(2,1)S(1)} %get-tuple-element.18.counts, bf16[1024,256]{1,0:T(8,128)(2,1)S(1)} %get-tuple-element.21.back, bf16[256,256]{1,0:T(8,128)(2,1)S(1)} %copy-done, f32[256,256]{1,0:T(8,128)S(1)} %get-tuple-element.22.near, ...), custom_call_target="tpu_custom_call" | custom-call | flops 1048576 | bytes 8388608 | tf_op jit(solution)/shard_map/forward/pallas_call | solution.py:49
  59.8 0.0 copy-start.1
  59.8 6.6 %all-to-all-start.2 = ((bf16[64,8,768]{2,1,0:T(8,128)(2,1)}), bf16[64,8,768]{2,1,0:T(8,128)(2,1)S(1)}, u32[]{:S(2)}, u32[]{:S(2)}) async-start(bf16[64,8,768]{2,1,0:T(8,128)(2,1)} %bitcast.31), calls=%async_computation.2 | async-start | bytes 1572864 | tf_op jit(solution)/shard_map/all_to_all | solution.py:274
  66.5 0.0 copy-done.1
  66.5 1.4 %other_hubs.1 = bf16[1024,256]{1,0:T(8,128)(2,1)S(1)} custom-call(bf16[3328,256]{1,0:T(8,128)(2,1)} %get-tuple-element.19.counts_t, bf16[512,256]{1,0:T(8,128)(2,1)S(1)} %copy-done.1), custom_call_target="tpu_custom_call" | custom-call | flops 1048576 | bytes 8388608 | tf_op jit(solution)/shard_map/other_hubs/pallas_call | solution.py:49
  67.9 1.9 %collective-permute-start.1 = (bf16[1024,256]{1,0:T(8,128)(2,1)S(1)}, bf16[1024,256]{1,0:T(8,128)(2,1)S(1)}, u32[]{:S(2)}, u32[]{:S(2)}) collective-permute-start(bf16[1024,256]{1,0:T(8,128)(2,1)S(1)} %other_hubs.1), channel_id=1, source_target_pairs={{0,64},{64,0},{1,65},{65,1},{2,66},{66,2},{3,67},{67,3},{4,68},{68... | collective-permute-start | bytes 1572872 | tf_op jit(solution)/shard_map/ppermute | solution.py:323
  69.8 1.4 %mine_and_own.1 = (bf16[1024,256]{1,0:T(8,128)(2,1)S(1)}, f32[256,256]{1,0:T(8,128)S(1)}) custom-call(bf16[3328,256]{1,0:T(8,128)(2,1)} %get-tuple-element.19.counts_t, bf16[512,256]{1,0:T(8,128)(2,1)S(1)} %copy-done.1, bf16[256,256]{1,0:T(8,128)(2,1)S(1)} %copy-done.2), custom_call_target="tpu_custom_call" | custom-call | flops 1048576 | bytes 8388608 | tf_op jit(solution)/shard_map/mine_and_own/pallas_call | solution.py:49
  71.3 0.4 collective-permute-done.1.met
  71.7 0.1 pair_hubs.1
  71.8 2.5 %collective-permute-start.2 = (bf16[256,256]{1,0:T(8,128)(2,1)S(1)}, bf16[256,256]{1,0:T(8,128)(2,1)S(1)}, u32[]{:S(2)}, u32[]{:S(2)}) collective-permute-start(bf16[256,256]{1,0:T(8,128)(2,1)S(1)} %get-tuple-element.28), channel_id=1, source_target_pairs={{0,128},{128,256},{256,384},{384,0},{1,129},{129,257},{257,385},{3... | collective-permute-start | bytes 393224 | tf_op jit(solution)/shard_map/ppermute | solution.py:330
  74.3 4.0 %collective-permute-start.3 = (bf16[256,256]{1,0:T(8,128)(2,1)S(1)}, bf16[256,256]{1,0:T(8,128)(2,1)S(1)}, u32[]{:S(2)}, u32[]{:S(2)}) collective-permute-start(bf16[256,256]{1,0:T(8,128)(2,1)S(1)} %get-tuple-element.29), channel_id=1, source_target_pairs={{0,256},{128,384},{256,0},{384,128},{1,257},{129,385},{257,1},{385... | collective-permute-start | bytes 393224 | tf_op jit(solution)/shard_map/ppermute | solution.py:330
  78.2 2.7 %collective-permute-start.4 = (bf16[256,256]{1,0:T(8,128)(2,1)S(1)}, bf16[256,256]{1,0:T(8,128)(2,1)S(1)}, u32[]{:S(2)}, u32[]{:S(2)}) collective-permute-start(bf16[256,256]{1,0:T(8,128)(2,1)S(1)} %get-tuple-element.30), channel_id=1, source_target_pairs={{0,384},{128,0},{256,128},{384,256},{1,385},{129,1},{257,129},{385... | collective-permute-start | bytes 393224 | tf_op jit(solution)/shard_map/ppermute | solution.py:330
  81.0 10.7 %all-to-all-done.2 = bf16[64,8,768]{2,1,0:T(8,128)(2,1)S(1)} async-done(((bf16[64,8,768]{2,1,0:T(8,128)(2,1)}), bf16[64,8,768]{2,1,0:T(8,128)(2,1)S(1)}, u32[]{:S(2)}, u32[]{:S(2)}) %all-to-all-start.2) | async-done | bytes 786464 | tf_op jit(solution)/shard_map/all_to_all | solution.py:274
  91.7 0.7 sum_weights.1
  92.3 3.3 %all-to-all-start.3 = ((bf16[8,8,256]{2,1,0:T(8,128)(2,1)}), bf16[8,8,256]{2,1,0:T(8,128)(2,1)S(1)}, u32[]{:S(2)}, u32[]{:S(2)}) async-start(bf16[8,8,256]{2,1,0:T(8,128)(2,1)} %bitcast.10), calls=%async_computation.3 | async-start | bytes 65536 | tf_op jit(solution)/shard_map/all_to_all | solution.py:274
  95.7 0.0 collective-permute-done.2.a
  95.7 0.0 collective-permute-done.3.b
  95.7 0.0 collective-permute-done.4.c
  95.7 0.1 sum_hubs.1.hubs
  95.8 0.0 copy-start.8
  95.8 0.3 add_returned.1.after.partial
  96.1 4.9 %all-to-all-done.3 = bf16[8,8,256]{2,1,0:T(8,128)(2,1)S(1)} async-done(((bf16[8,8,256]{2,1,0:T(8,128)(2,1)}), bf16[8,8,256]{2,1,0:T(8,128)(2,1)S(1)}, u32[]{:S(2)}, u32[]{:S(2)}) %all-to-all-start.3) | async-done | bytes 32800 | tf_op jit(solution)/shard_map/all_to_all | solution.py:274
  101.1 21.8 %all_to_all.26 = bf16[64,8,384]{2,1,0:T(8,128)(2,1)S(1)} all-to-all(bf16[64,8,384]{2,1,0:T(8,128)(2,1)S(1)} %bitcast.23), channel_id=1, replica_groups=mesh['x'=4,'core'=2,'y'=8,'z'=8] {'y','z'}, dimensions={0} | all-to-all | bytes 786432 | tf_op jit(solution)/shard_map/all_to_all | solution.py:274
  122.9 0.0 copy-done.8
  122.9 0.9 finish.1
  (1 shorter events, 0.0 us)
Async XLA Ops:
  0.6 19.0 %copy-start = (bf16[256,256]{1,0:T(8,128)(2,1)S(1)}, bf16[256,256]{1,0:T(8,128)(2,1)}, u32[]{:S(2)}) copy-start(bf16[256,256]{1,0:T(8,128)(2,1)} %features.7) | copy-start | bytes 393220
  0.6 19.0 %copy-start.7 = (s32[64]{0:T(128)S(1)}, s32[64]{0:T(128)}, u32[]{:S(2)}) copy-start(s32[64]{0:T(128)} %param.11) | copy-start | bytes 772
  0.7 19.0 %copy-start.5 = (s32[64,16]{0,1:T(8,128)S(1)}, s32[64,16]{0,1:T(8,128)}, u32[]{:S(2)}) copy-start(s32[64,16]{0,1:T(8,128)} %param.10) | copy-start | bytes 12292
  0.7 19.0 %copy-start.2 = (bf16[256,256]{1,0:T(8,128)(2,1)S(1)}, bf16[256,256]{1,0:T(8,128)(2,1)}, u32[]{:S(2)}) copy-start(bf16[256,256]{1,0:T(8,128)(2,1)} %w_self.3) | copy-start | bytes 393220
  0.7 19.0 %copy-start.6 = (s32[256,10]{0,1:T(8,128)S(1)}, s32[256,10]{0,1:T(8,128)}, u32[]{:S(2)}) copy-start(s32[256,10]{0,1:T(8,128)} %param.9) | copy-start | bytes 30724
  3.1 38.7 %all-to-all-start = ((bf16[64,8,640]{2,1,0:T(8,128)(2,1)}), bf16[64,8,640]{2,1,0:T(8,128)(2,1)S(1)}, u32[]{:S(2)}, u32[]{:S(2)}) async-start(bf16[64,8,640]{2,1,0:T(8,128)(2,1)} %bitcast.30), calls=%async_computation | async-start | bytes 1310720 | tf_op jit(solution)/shard_map/all_to_all | solution.py:274
  54.1 3.8 %collective-permute-start = (bf16[1024,256]{1,0:T(8,128)(2,1)S(1)}, bf16[1024,256]{1,0:T(8,128)(2,1)S(1)}, u32[]{:S(2)}, u32[]{:S(2)}) collective-permute-start(bf16[1024,256]{1,0:T(8,128)(2,1)S(1)} %bitcast.20), channel_id=1, source_target_pairs={{0,64},{64,0},{1,65},{65,1},{2,66},{66,2},{3,67},{67,3},{4,68},{68... | collective-permute-start | bytes 1572872 | tf_op jit(solution)/shard_map/ppermute | solution.py:303
  56.4 1.5 %copy-start.3 = (bf16[256,256]{1,0:T(8,128)(2,1)S(1)}, bf16[256,256]{1,0:T(8,128)(2,1)}, u32[]{:S(2)}) copy-start(bf16[256,256]{1,0:T(8,128)(2,1)} %w_nbr.1) | copy-start | bytes 393220
  56.4 1.5 %copy-start.4 = (bf16[256,256]{1,0:T(8,128)(2,1)S(1)}, bf16[256,256]{1,0:T(8,128)(2,1)}, u32[]{:S(2)}) copy-start(bf16[256,256]{1,0:T(8,128)(2,1)} %cotangent.1) | copy-start | bytes 393220
  59.8 6.7 %copy-start.1 = (bf16[512,256]{1,0:T(8,128)(2,1)S(1)}, bf16[512,256]{1,0:T(8,128)(2,1)}, u32[]{:S(2)}) copy-start(bf16[512,256]{1,0:T(8,128)(2,1)} %get-tuple-element.25.both) | copy-start | bytes 786436
  59.8 31.8 %all-to-all-start.2 = ((bf16[64,8,768]{2,1,0:T(8,128)(2,1)}), bf16[64,8,768]{2,1,0:T(8,128)(2,1)S(1)}, u32[]{:S(2)}, u32[]{:S(2)}) async-start(bf16[64,8,768]{2,1,0:T(8,128)(2,1)} %bitcast.31), calls=%async_computation.2 | async-start | bytes 1572864 | tf_op jit(solution)/shard_map/all_to_all | solution.py:274
  67.9 3.8 %collective-permute-start.1 = (bf16[1024,256]{1,0:T(8,128)(2,1)S(1)}, bf16[1024,256]{1,0:T(8,128)(2,1)S(1)}, u32[]{:S(2)}, u32[]{:S(2)}) collective-permute-start(bf16[1024,256]{1,0:T(8,128)(2,1)S(1)} %other_hubs.1), channel_id=1, source_target_pairs={{0,64},{64,0},{1,65},{65,1},{2,66},{66,2},{3,67},{67,3},{4,68},{68... | collective-permute-start | bytes 1572872 | tf_op jit(solution)/shard_map/ppermute | solution.py:323
  71.8 23.9 %collective-permute-start.2 = (bf16[256,256]{1,0:T(8,128)(2,1)S(1)}, bf16[256,256]{1,0:T(8,128)(2,1)S(1)}, u32[]{:S(2)}, u32[]{:S(2)}) collective-permute-start(bf16[256,256]{1,0:T(8,128)(2,1)S(1)} %get-tuple-element.28), channel_id=1, source_target_pairs={{0,128},{128,256},{256,384},{384,0},{1,129},{129,257},{257,385},{3... | collective-permute-start | bytes 393224 | tf_op jit(solution)/shard_map/ppermute | solution.py:330
  74.3 21.4 %collective-permute-start.3 = (bf16[256,256]{1,0:T(8,128)(2,1)S(1)}, bf16[256,256]{1,0:T(8,128)(2,1)S(1)}, u32[]{:S(2)}, u32[]{:S(2)}) collective-permute-start(bf16[256,256]{1,0:T(8,128)(2,1)S(1)} %get-tuple-element.29), channel_id=1, source_target_pairs={{0,256},{128,384},{256,0},{384,128},{1,257},{129,385},{257,1},{385... | collective-permute-start | bytes 393224 | tf_op jit(solution)/shard_map/ppermute | solution.py:330
  78.2 17.5 %collective-permute-start.4 = (bf16[256,256]{1,0:T(8,128)(2,1)S(1)}, bf16[256,256]{1,0:T(8,128)(2,1)S(1)}, u32[]{:S(2)}, u32[]{:S(2)}) collective-permute-start(bf16[256,256]{1,0:T(8,128)(2,1)S(1)} %get-tuple-element.30), channel_id=1, source_target_pairs={{0,384},{128,0},{256,128},{384,256},{1,385},{129,1},{257,129},{385... | collective-permute-start | bytes 393224 | tf_op jit(solution)/shard_map/ppermute | solution.py:330
  92.3 8.7 %all-to-all-start.3 = ((bf16[8,8,256]{2,1,0:T(8,128)(2,1)}), bf16[8,8,256]{2,1,0:T(8,128)(2,1)S(1)}, u32[]{:S(2)}, u32[]{:S(2)}) async-start(bf16[8,8,256]{2,1,0:T(8,128)(2,1)} %bitcast.10), calls=%async_computation.3 | async-start | bytes 65536 | tf_op jit(solution)/shard_map/all_to_all | solution.py:274
  95.8 27.1 %copy-start.8 = (s32[1,4]{1,0:T(1,128)S(1)}, s32[1,4]{1,0:T(1,128)}, u32[]{:S(2)}) copy-start(s32[1,4]{1,0:T(1,128)} %hub.3) | copy-start | bytes 52
